TPU v7x, 256 devices: a whole 4x4x8 slice. The times are simulated.
256 devices in a mesh: cls: 4 (over z_hi), grp: 4 (over x), dom: 16 (over y, z_lo, core).
Axes of the slice: x: 4, y: 4, z: 8 (z_hi: 4, z_lo: 2; z = z_hi * 2 + z_lo), core: 2. Of those that a mesh axis runs over, the one named last changes fastest.
Arguments:
- particle_images: bfloat16 [2560, 8192], P(('grp', 'dom')), may hold values from -110 to 110, as said below
- particle_groups: int32 [2560], P(('grp', 'dom')), may hold values from 0 to 7
- live_counts: int32 [64], P(('grp', 'dom')), may hold values from 1 to 40, as said below
- ctf_table: float32 [8, 4096], replicated, may hold values from -1 to 1
- projections: bfloat16 [8192, 8, 200], P(('grp', 'dom'), 'cls'), may hold values from -0.25 to 0.25
Outputs:
- insertions: float32 [8, 200, 8192], P('cls', None, ('grp', 'dom'))
- class_weights: float32 [8, 8, 200], P('cls')
- log_evidence: float32 [2560], P(('grp', 'dom'))
Inputs may be any that keep to these rules, and one draw needn't show every extreme that they name: `particle_images`: particle image coefficients. `live_counts`: live particles of one shard; in every draw some shard has all 40 slots live.
All inputs are finite; a program needn't handle non-finite values.
Results may differ from a plain program's by a relative error of at most 0.012.
The roundings to bfloat16 on the way count: a program that leaves them out, or rounds other values in their place, can miss the bound.
Values may be sent and summed in bfloat16 or wider, within the bound.
No kernel may reach another device: no remote copies, remote signals or barrier semaphores. Data moves between devices by JAX's collectives and lax.ppermute only.
A program may use at most 128 MiB of HBM per device.

v0:
```python
import math

import jax
import jax.numpy as jnp
import numpy as np
from jax import lax
from jax.experimental import pallas as pl
from jax.experimental.pallas import tpu as pltpu
from jax.sharding import Mesh, PartitionSpec as P

IMG = 64
SIDE = 5
SHIFTS = SIDE * SIDE
HALF = SHIFTS // 2
GROUPS = 8
FREQS = IMG * IMG
LANE = 128
SLOTS = 40
ROWS = 1024
WIDTH = 200
WIDE = 256
TALL = WIDTH + 8
COUNTED = SLOTS * SHIFTS
BLOCKS = 32
DEPTH = BLOCKS * LANE
HIGHEST = lax.Precision.HIGHEST
F32 = jnp.float32
BF16 = jnp.bfloat16
MIB = 2**20
VMEM = pl.BlockSpec(memory_space=pltpu.VMEM)
SMEM = pl.BlockSpec(memory_space=pltpu.SMEM)
SWAP = [(0, 1), (1, 0)]


def shift_tables():
    index = np.arange(FREQS)
    shift = np.arange(HALF)
    offx = shift // SIDE - SIDE // 2
    offy = shift % SIDE - SIDE // 2
    phase = (offx[:, None] * (index // IMG)[None, :] + offy[:, None] * (index % IMG)[None, :]) % IMG
    theta = (phase.astype(np.float32) * np.float32(2.0 * math.pi / IMG)).astype(np.float64)
    return np.cos(theta).astype(np.float32), np.sin(theta).astype(np.float32)


def call(kernel, name, out, args, limit, flops=0, moved=0):
    return pl.pallas_call(
        kernel,
        name=name,
        in_specs=[SMEM] + [VMEM] * (len(args) - 1),
        out_specs=jax.tree.map(lambda _: VMEM, out),
        out_shape=out,
        cost_estimate=pl.CostEstimate(flops=flops, bytes_accessed=moved, transcendentals=0),
        compiler_params=pltpu.CompilerParams(vmem_limit_bytes=limit * MIB),
    )(*args)


def shape(*dims, dtype=F32):
    return jax.ShapeDtypeStruct(dims, dtype)


def lanes(block):
    return pl.ds(pl.multiple_of(block * LANE, LANE), LANE)


def cut(value):
    first = value.astype(BF16)
    rest = value - first.astype(F32)
    second = rest.astype(BF16)
    return first, second, (rest - second.astype(F32)).astype(BF16)


def split_kernel(place, images, meta, ctf, kept, given, parts):
    core = place[3]
    for i, part in enumerate(cut(ctf[...])):
        parts[16 * i : 16 * i + 16, :] = jnp.concatenate([part.astype(F32), jnp.zeros((8, FREQS), F32)], axis=0).astype(BF16)

    def turn(j, carry):
        kept[:, lanes(j)] = images[:, lanes(2 * j + core)]
        given[:, lanes(j)] = images[:, lanes(2 * j + 1 - core)]
        return carry

    lax.fori_loop(0, BLOCKS, turn, 0)
    kept[:, DEPTH:] = meta[...]
    given[:, DEPTH:] = meta[...]


def owner_block(place, p):
    return ((place[0] + p // 8) % 4) * 8 + ((place[1] + p % 8 // 2) % 4) * 2 + p % 2


def build_kernel(place, images, parts, cosv, sinv, out, token, rows):
    core = place[3]
    group = images[:, DEPTH : DEPTH + 1].astype(F32)
    lane = lax.broadcasted_iota(jnp.int32, (SLOTS, 48), 1)
    hot = jnp.where((group == (lane % 16).astype(F32)) & (lane % 16 < GROUPS), 1.0, 0.0).astype(BF16)
    rows[...] = jnp.dot(hot, parts[...], preferred_element_type=F32)

    def turn(p, carry):
        j = owner_block(place, p)
        at = lanes(2 * (j % 16) + core)
        sign = jnp.where(j < 16, 1.0, -1.0).astype(F32)
        row = rows[:, at]
        first = images[:, lanes(j)].astype(F32) * row
        second = images[:, lanes((j + 16) % 32)].astype(F32) * (row * sign)
        here = lanes(p)
        for s in range(HALF):
            a = first * cosv[s : s + 1, at]
            b = second * sinv[s : s + 1, at]
            out[2 * SLOTS * s : 2 * SLOTS * (s + 1), here] = jnp.concatenate([a + b, a - b], axis=0).astype(BF16)
        tail = jnp.concatenate([first, jnp.zeros((ROWS - SLOTS * SHIFTS, LANE), F32)], axis=0)
        out[2 * SLOTS * HALF : ROWS, here] = tail.astype(BF16)
        return carry

    lax.fori_loop(0, BLOCKS, turn, 0, unroll=2)
    token[...] = jnp.zeros_like(token)


def build_call(place, images, parts, cosv, sinv, name):
    return pl.pallas_call(
        build_kernel,
        name=name,
        in_specs=[SMEM] + [VMEM] * 4,
        out_specs=[VMEM, VMEM],
        out_shape=[shape(ROWS, DEPTH, dtype=BF16), shape(8, LANE)],
        scratch_shapes=[pltpu.VMEM((SLOTS, FREQS), F32)],
        cost_estimate=pl.CostEstimate(flops=6 * 10**9, bytes_accessed=2 * ROWS * DEPTH, transcendentals=0),
        compiler_params=pltpu.CompilerParams(vmem_limit_bytes=10 * MIB),
    )(place, images, parts, cosv, sinv)


def hot_rows(meta):
    group = meta[:, 0:1].astype(F32)
    lane = lax.broadcasted_iota(jnp.int32, (SLOTS, GROUPS), 1).astype(F32)
    return jnp.where(group == lane, 1.0, 0.0).astype(F32)


def pair_kernel(place, stacks, came, out):
    parity = place[2]
    out[parity] = stacks[parity]
    out[1 - parity] = came[...]


def weigh_kernel(place, ctf, t0, t1, t2, t3, p0, p1, p2, p3, out, power):
    core = place[3]
    total = jnp.zeros((3 * GROUPS, WIDE), F32)
    for q, piece in enumerate((p0, p1, p2, p3)):
        for r in range(8):
            p = 8 * q + r
            out[:WIDTH, p * LANE : (p + 1) * LANE] = piece[r]
    out[WIDTH - 8 :, :] = jnp.concatenate([out[WIDTH - 8 : WIDTH, :], jnp.zeros((WIDE - WIDTH, DEPTH), BF16)], axis=0)
    for q in range(8):
        left = []
        for r in range(4):
            j = owner_block(place, jnp.int32(4 * q + r))
            left.append(ctf[:, lanes(2 * (j % 16) + core)])
        left = jnp.concatenate(left, axis=1)
        left = left * left
        parts = jnp.concatenate([part.astype(F32) for part in cut(left)], axis=0).astype(BF16)
        square = out[:, 512 * q : 512 * (q + 1)].astype(F32)
        square = square * square
        high = square.astype(BF16)
        low = (square - high.astype(F32)).astype(BF16)
        dims = (((1,), (1,)), ((), ()))
        total = total + lax.dot_general(parts, high, dims, preferred_element_type=F32)
        total = total + lax.dot_general(parts, low, dims, preferred_element_type=F32)
    power[...] = total[:GROUPS] + total[GROUPS : 2 * GROUPS] + total[2 * GROUPS :]


def score_kernel(place, weights, power, shifted_a, shifted_b, meta_a, meta_b, out):
    for k, (shifted, meta) in enumerate(((shifted_a, meta_a), (shifted_b, meta_b))):
        half = 0.5 * jnp.dot(hot_rows(meta[...]), power[...], precision=HIGHEST, preferred_element_type=F32)
        out[k] = lax.dot_general(shifted[...], weights[...], (((1,), (1,)), ((), ())), preferred_element_type=F32)
        for s in range(SHIFTS):
            out[k, SLOTS * s : SLOTS * (s + 1), :] -= half


def settle_kernel(place, mine, theirs, log, stats):
    columns = []
    for k in range(2):
        best = None
        for s in range(SHIFTS):
            at = slice(SLOTS * s, SLOTS * (s + 1))
            value = mine[k, at, :WIDTH] + theirs[k, at, :WIDTH]
            log[k, at, :] = value
            best = value if best is None else jnp.maximum(best, value)
        top = jnp.max(best, axis=1, keepdims=True)
        total = jnp.zeros_like(best)
        for s in range(SHIFTS):
            total = total + jnp.exp(log[k, SLOTS * s : SLOTS * (s + 1), :] - top)
        columns += [top, jnp.sum(total, axis=1, keepdims=True)]
    lane = lax.broadcasted_iota(jnp.int32, (SLOTS, LANE), 1)
    spread = jnp.where(lane == 0, columns[0], jnp.where(lane == 1, columns[1], jnp.where(lane == 2, columns[2], columns[3])))
    spread = jnp.concatenate([spread, jnp.zeros((LANE - SLOTS, LANE), F32)], axis=0).T[:8, :]
    for d in range(8):
        stats[d] = spread


def posterior_kernel(place, log, stats, meta_a, meta_b, low, evidence, spare):
    parity = place[2]
    counted = jnp.zeros((GROUPS, WIDTH), F32)
    for k, meta in ((1, meta_b), (0, meta_a)):
        tops, totals = [], []
        for d in range(8):
            same = (parity == d % 2) == (k == 0)
            here = stats[d, :, :SLOTS]
            tops.append(jnp.where(same, here[0:1], here[2:3]))
            totals.append(jnp.where(same, here[1:2], here[3:4]))
        tops = jnp.concatenate(tops, axis=0)
        totals = jnp.concatenate(totals, axis=0)
        top = jnp.max(tops, axis=0, keepdims=True)
        total = jnp.sum(totals * jnp.exp(tops - top), axis=0, keepdims=True)
        row = lax.broadcasted_iota(jnp.int32, (8, SLOTS), 0)
        columns = jnp.where(row == 0, top, jnp.where(row == 1, total, top + jnp.log(total))).T
        live = meta[:, 1:2].astype(F32)
        scale = live / columns[:, 1:2]
        if k == 0:
            known = jnp.where(live > 0.0, columns[:, 2:3], 0.0)
            evidence[...] = jnp.broadcast_to(known, (SLOTS, LANE)).T[:8, :]
        gathered = None
        for s in range(SHIFTS):
            at = slice(SLOTS * s, SLOTS * (s + 1))
            value = jnp.exp(log[k, at, :] - columns[:, 0:1]) * scale
            spare[at, :] = value
            gathered = value if gathered is None else gathered + value
        hot = hot_rows(meta[...])
        counted = counted + lax.dot_general(
            hot, gathered, (((0,), (0,)), ((), ())), precision=HIGHEST, preferred_element_type=F32
        )
        spare[SLOTS * SHIFTS :, :] = jnp.zeros((ROWS - SLOTS * SHIFTS, WIDTH), F32)
        if k == 0:
            first = counted.astype(BF16).astype(F32)
            spare[COUNTED : COUNTED + GROUPS, :] = first
            spare[COUNTED + GROUPS : COUNTED + 2 * GROUPS, :] = counted - first
        low[k] = spare[...].T.astype(BF16)


def posterior_call(*args):
    out = [shape(2, WIDTH, ROWS, dtype=BF16), shape(8, SLOTS)]
    return pl.pallas_call(
        posterior_kernel,
        name="posterior",
        in_specs=[SMEM] + [VMEM] * (len(args) - 1),
        out_specs=[VMEM] * 2,
        out_shape=out,
        scratch_shapes=[pltpu.VMEM((ROWS, WIDTH), F32)],
        compiler_params=pltpu.CompilerParams(vmem_limit_bytes=10 * MIB),
    )(*args)


def insert_kernel(q):
    def kernel(place, mine, theirs, s0, s1, s2, s3, out):
        low = jnp.concatenate([mine[0], theirs[0], mine[1], theirs[1]], axis=1)
        for n in range(0, 8, 2):
            at = slice(q * 1024 + LANE * n, q * 1024 + LANE * (n + 2))
            shifted = jnp.concatenate([s0[:, at], s1[:, at], s2[:, at], s3[:, at]], axis=0)
            sums = jnp.dot(low, shifted, preferred_element_type=F32)
            for r in range(2):
                out[n + r, :WIDTH, :] = sums[:, r * LANE : (r + 1) * LANE].astype(BF16)
        tail = slice(ROWS - LANE, ROWS)
        start = COUNTED - ROWS + LANE
        both = (mine[0, :, tail].astype(F32) + theirs[0, :, tail].astype(F32)).T
        both = both[start : start + GROUPS] + both[start + GROUPS : start + 2 * GROUPS]
        both = jnp.concatenate([both, jnp.zeros((GROUPS, WIDE - WIDTH), F32)], axis=1).astype(BF16)
        for n in range(8):
            out[n, WIDTH:, :] = both[:, LANE * (n % 2) : LANE * (n % 2 + 1)]

    return kernel


def take(value, axis, d, n=4):
    return lax.ppermute(value, axis, [(i, (i - d) % n) for i in range(n)])


def push(value, axis, d, n=4):
    return lax.ppermute(value, axis, [(i, (i + d) % n) for i in range(n)])


def body(particle_images, particle_groups, live_counts, ctf_table, projections):
    x, y, zl, core = (lax.axis_index(a) for a in ("grp", "y", "zl", "core"))
    place = jnp.stack([x, y, zl, core]).astype(jnp.int32)
    ring = ("cls", "zl")

    slot = jnp.arange(SLOTS, dtype=jnp.int32)
    live = slot < live_counts[0]
    lane = jnp.arange(LANE, dtype=jnp.int32)[None, :]
    meta = jnp.where(lane == 0, particle_groups[:, None], jnp.where(lane == 1, live.astype(jnp.int32)[:, None], 0)).astype(BF16)

    stacks = jnp.transpose(projections, (1, 2, 0))
    theirs = lax.dynamic_index_in_dim(stacks, 1 - zl, axis=0, keepdims=False)
    came = lax.ppermute(theirs, "zl", SWAP)
    unit = call(pair_kernel, "pair", shape(2, WIDTH, LANE, dtype=BF16), (place, stacks, came), 4)

    half = shape(SLOTS, DEPTH + LANE, dtype=BF16)
    kept, other, parts = call(
        split_kernel, "split", [half, half, shape(48, FREQS, dtype=BF16)], (place, particle_images, meta, ctf_table), 8
    )
    halves = [kept, lax.ppermute(other, "core", SWAP)]

    column = jnp.concatenate([unit] + [take(unit, "y", d) for d in (1, 2, 3)])
    next_kept = push(kept, ring, 1, 8)
    next_other = push(other, ring, 7, 8)
    halves += [next_kept, lax.ppermute(next_other, "core", SWAP)]
    pieces = [column] + [take(column, "grp", d) for d in (1, 2, 3)]

    cosv, sinv = shift_tables()
    metas = [h[:, DEPTH:] for h in halves]
    built = [build_call(place, h, parts, cosv, sinv, f"build_{i}") for i, h in enumerate(halves)]
    shifted = [b[0] for b in built]
    tokens = [b[1] for b in built]
    weights, power = call(
        weigh_kernel,
        "weigh",
        [shape(WIDE, DEPTH, dtype=BF16), shape(GROUPS, WIDE)],
        (place, ctf_table, *tokens, *pieces),
        8,
    )
    score = shape(2, ROWS, WIDE)
    flops = 4 * ROWS * WIDE * DEPTH
    given = call(score_kernel, "score_given", score, (place, weights, power, shifted[1], shifted[3], metas[1], metas[3]), 8, flops)
    taken = lax.ppermute(given, "core", SWAP)
    own = call(score_kernel, "score_own", score, (place, weights, power, shifted[0], shifted[2], metas[0], metas[2]), 8, flops)
    log, stats = call(settle_kernel, "settle", [shape(2, ROWS, WIDTH), shape(8, 8, LANE)], (place, own, taken), 8)
    stats = lax.all_to_all(stats, ring, 0, 0, tiled=True)
    low, evidence = posterior_call(place, log, stats, metas[0], metas[2])
    other_low = lax.ppermute(low, "core", SWAP)

    flops = 2 * 4 * ROWS * WIDE * 1024
    chunk = shape(8, TALL, LANE, dtype=BF16)
    parts = {q: call(insert_kernel(q), f"insert_{q}", chunk, (place, low, other_low, *shifted), 8, flops) for q in (2, 1, 3, 0)}

    def total(own, axis, sent):
        got = [push(v, axis, q) for q, v in sent]
        return sum((g.astype(F32) for g in got), own.astype(F32))

    row = total(parts[0], "grp", [(q, parts[q]) for q in (2, 1, 3)])
    cell = total(row[:2], "y", [(q, row[2 * q : 2 * q + 2].astype(BF16)) for q in (2, 1, 3)])
    tally = jnp.concatenate([cell[0, WIDTH:], cell[1, WIDTH:]])
    out_a, out_b = cell[0, :WIDTH], cell[1, :WIDTH]
    stay = jnp.where(zl == 0, out_a, out_b)
    leave = jnp.where(zl == 0, out_b, out_a)
    came = lax.ppermute(jnp.concatenate([leave, tally]), "zl", SWAP)
    came, tally_came = came[:WIDTH], came[WIDTH:]
    insertions = jnp.stack([jnp.where(zl == 0, stay, came), jnp.where(zl == 0, came, stay)])

    def table(rows):
        return jnp.concatenate([rows[:GROUPS], rows[GROUPS:]], axis=1)[:, :WIDTH]

    here, there = table(tally), table(tally_came)
    class_weights = jnp.stack([jnp.where(zl == 0, here, there), jnp.where(zl == 0, there, here)])
    return insertions, class_weights, evidence[0]


def solution(mesh):
    fine = Mesh(mesh.devices.reshape(4, 4, 4, 2, 2), ("cls", "grp", "y", "zl", "core"))
    shards = ("grp", "y", "zl", "core")
    return jax.shard_map(
        body,
        mesh=fine,
        in_specs=(P(shards, None), P(shards), P(shards), P(), P(shards, "cls", None)),
        out_specs=(P("cls", None, shards), P("cls", None, None), P(shards)),
        check_vma=False,
    )
```

profile of v0, /device:TPU:32, one launch (start us, length us, event | category | flops | bytes accessed | tf_op | source)
XLA Modules:
  0.0 125.5 jit_solution(675254515557764860)
XLA Ops:
  1.4 1.8 %collective-permute-start.4 = (bf16[200,128]{1,0:T(8,128)(2,1)S(1)}, bf16[200,128]{1,0:T(8,128)(2,1)S(1)}, u32[]{:S(2)}, u32[]{:S(2)}) collective-permute-start(bf16[200,128]{1,0:T(8,128)(2,1)S(1)} %dynamic-slice_bitcast_fusion), channel_id=1, source_target_pairs={{0,2},{2,0},{1,3},{3,1},{4,6},{6,4},{5,7},{7,5},{8,10},{10,8},{9,1... | collective-permute-start | bytes 153608 | tf_op jit(solution)/shard_map/ppermute | solution.py:290
  9.4 1.7 %collective-permute-start.7 = (bf16[2,200,128]{2,1,0:T(8,128)(2,1)S(1)}, bf16[2,200,128]{2,1,0:T(8,128)(2,1)S(1)}, u32[]{:S(2)}, u32[]{:S(2)}) collective-permute-start(bf16[2,200,128]{2,1,0:T(8,128)(2,1)S(1)} %pair.1), channel_id=1, source_target_pairs={{0,4},{4,8},{8,12},{12,0},{1,5},{5,9},{9,13},{13,1},{2,6},{6,10},{... | collective-permute-start | bytes 307208 | tf_op jit(solution)/shard_map/ppermute | solution.py:271
  11.0 2.9 %collective-permute-start.6 = (bf16[2,200,128]{2,1,0:T(8,128)(2,1)S(1)}, bf16[2,200,128]{2,1,0:T(8,128)(2,1)S(1)}, u32[]{:S(2)}, u32[]{:S(2)}) collective-permute-start(bf16[2,200,128]{2,1,0:T(8,128)(2,1)S(1)} %pair.1), channel_id=1, source_target_pairs={{0,8},{4,12},{8,0},{12,4},{1,9},{5,13},{9,1},{13,5},{2,10},{6,14},... | collective-permute-start | bytes 307208 | tf_op jit(solution)/shard_map/ppermute | solution.py:271
  17.2 4.3 %build_0.1 = (bf16[1024,4096]{1,0:T(8,128)(2,1)S(1)}, f32[8,128]{1,0:T(8,128)S(1)}) custom-call(s32[4]{0:T(128)S(1)} %pad_add_fusion.place, bf16[40,4224]{1,0:T(8,128)(2,1)S(1)} %get-tuple-element.20.images, bf16[48,4096]{1,0:T(8,128)(2,1)S(1)} %get-tuple-element.21.parts, f32[12,4096]{1,0:T(8,128)S(1)} %copy-done.10, f32[12,4096]{1,0:T(8,128)S(1)} %copy-done.8), custom_call_target="tpu_custom_call" | custom-call | flops 6000000000 | bytes 8388608 | tf_op jit(solution)/shard_map/build_0/pallas_call | solution.py:119
  21.5 2.0 %collective-permute-start.1 = (bf16[40,4224]{1,0:T(8,128)(2,1)S(1)}, bf16[40,4224]{1,0:T(8,128)(2,1)S(1)}, u32[]{:S(2)}, u32[]{:S(2)}) collective-permute-start(bf16[40,4224]{1,0:T(8,128)(2,1)S(1)} %get-tuple-element.20.images), channel_id=1, source_target_pairs={{0,2},{2,64},{64,66},{66,128},{128,130},{130,192},{192,194},{194,0... | collective-permute-start | bytes 1013768 | tf_op jit(solution)/shard_map/ppermute | solution.py:275
  23.5 1.6 %collective-permute-start.10 = (bf16[8,200,128]{2,1,0:T(8,128)(2,1)S(1)}, bf16[8,200,128]{2,1,0:T(8,128)(2,1)S(1)}, u32[]{:S(2)}, u32[]{:S(2)}) collective-permute-start(bf16[8,200,128]{2,1,0:T(8,128)(2,1)S(1)} %pad_maximum_fusion.p0), channel_id=1, source_target_pairs={{0,16},{16,32},{32,48},{48,0},{1,17},{17,33},{33,49},{49,1},{2,18}... | collective-permute-start | bytes 1228808 | tf_op jit(solution)/shard_map/ppermute | solution.py:271
  25.1 2.7 %collective-permute-start.9 = (bf16[8,200,128]{2,1,0:T(8,128)(2,1)S(1)}, bf16[8,200,128]{2,1,0:T(8,128)(2,1)S(1)}, u32[]{:S(2)}, u32[]{:S(2)}) collective-permute-start(bf16[8,200,128]{2,1,0:T(8,128)(2,1)S(1)} %pad_maximum_fusion.p0), channel_id=1, source_target_pairs={{0,32},{16,48},{32,0},{48,16},{1,33},{17,49},{33,1},{49,17},{2,34}... | collective-permute-start | bytes 1228808 | tf_op jit(solution)/shard_map/ppermute | solution.py:271
  27.8 1.4 %collective-permute-start.8 = (bf16[8,200,128]{2,1,0:T(8,128)(2,1)S(1)}, bf16[8,200,128]{2,1,0:T(8,128)(2,1)S(1)}, u32[]{:S(2)}, u32[]{:S(2)}) collective-permute-start(bf16[8,200,128]{2,1,0:T(8,128)(2,1)S(1)} %pad_maximum_fusion.p0), channel_id=1, source_target_pairs={{0,48},{16,0},{32,16},{48,32},{1,49},{17,1},{33,17},{49,33},{2,50}... | collective-permute-start | bytes 1228808 | tf_op jit(solution)/shard_map/ppermute | solution.py:271
  29.3 4.3 %build_1.1 = (bf16[1024,4096]{1,0:T(8,128)(2,1)S(1)}, f32[8,128]{1,0:T(8,128)S(1)}) custom-call(s32[4]{0:T(128)S(1)} %pad_add_fusion.place, bf16[40,4224]{1,0:T(8,128)(2,1)S(1)} %collective-permute-done.images, bf16[48,4096]{1,0:T(8,128)(2,1)S(1)} %get-tuple-element.21.parts, f32[12,4096]{1,0:T(8,128)S(1)} %copy-done.10, f32[12,4096]{1,0:T(8,128)S(1)} %copy-done.9), custom_call_target="tpu_custom_call" | custom-call | flops 6000000000 | bytes 8388608 | tf_op jit(solution)/shard_map/build_1/pallas_call | solution.py:119
  34.2 4.3 %build_2.1 = (bf16[1024,4096]{1,0:T(8,128)(2,1)S(1)}, f32[8,128]{1,0:T(8,128)S(1)}) custom-call(s32[4]{0:T(128)S(1)} %pad_add_fusion.place, bf16[40,4224]{1,0:T(8,128)(2,1)S(1)} %collective-permute-done.1.images, bf16[48,4096]{1,0:T(8,128)(2,1)S(1)} %get-tuple-element.21.parts, f32[12,4096]{1,0:T(8,128)S(1)} %copy-done.10, f32[12,4096]{1,0:T(8,128)S(1)} %copy-done.9), custom_call_target="tpu_custom_call" | custom-call | flops 6000000000 | bytes 8388608 | tf_op jit(solution)/shard_map/build_2/pallas_call | solution.py:119
  38.5 4.3 %build_3.1 = (bf16[1024,4096]{1,0:T(8,128)(2,1)S(1)}, f32[8,128]{1,0:T(8,128)S(1)}) custom-call(s32[4]{0:T(128)S(1)} %pad_add_fusion.place, bf16[40,4224]{1,0:T(8,128)(2,1)S(1)} %collective-permute-done.3.images, bf16[48,4096]{1,0:T(8,128)(2,1)S(1)} %get-tuple-element.21.parts, f32[12,4096]{1,0:T(8,128)S(1)} %copy-done.10, f32[12,4096]{1,0:T(8,128)S(1)} %copy-done.9), custom_call_target="tpu_custom_call" | custom-call | flops 6000000000 | bytes 8388608 | tf_op jit(solution)/shard_map/build_3/pallas_call | solution.py:119
  42.8 3.2 %copy-done.2 = bf16[1024,4096]{1,0:T(8,128)(2,1)} copy-done((bf16[1024,4096]{1,0:T(8,128)(2,1)}, bf16[1024,4096]{1,0:T(8,128)(2,1)S(1)}, u32[]{:S(2)}) %copy-start.2) | copy-done | bytes 8388632
  46.1 2.0 %weigh.1 = (bf16[256,4096]{1,0:T(8,128)(2,1)S(1)}, f32[8,256]{1,0:T(8,128)S(1)}) custom-call(s32[4]{0:T(128)S(1)} %pad_add_fusion.place, f32[8,4096]{1,0:T(8,128)S(1)} %copy-done.6, f32[8,128]{1,0:T(8,128)S(1)} %get-tuple-element.22.t0, f32[8,128]{1,0:T(8,128)S(1)} %get-tuple-element.24.t1, f32[8,128]{1,0:T(8,128)S(1)} %get-tuple-element.25.t2, ...), custom_call_target="tpu_custom_call" | custom-call | tf_op jit(solution)/shard_map/weigh/pallas_call | solution.py:46
  48.1 3.4 %copy-done.3 = bf16[1024,4096]{1,0:T(8,128)(2,1)S(1)} copy-done((bf16[1024,4096]{1,0:T(8,128)(2,1)S(1)}, bf16[1024,4096]{1,0:T(8,128)(2,1)}, u32[]{:S(2)}) %copy-start.3) | copy-done | bytes 8388632
  51.4 5.2 %score_given.1 = f32[2,1024,256]{2,1,0:T(8,128)S(1)} custom-call(s32[4]{0:T(128)S(1)} %pad_add_fusion.place, bf16[256,4096]{1,0:T(8,128)(2,1)S(1)} %get-tuple-element.27.weights, f32[8,256]{1,0:T(8,128)S(1)} %get-tuple-element.28.power, bf16[1024,4096]{1,0:T(8,128)(2,1)S(1)} %get-tuple-element.31.shifted_a.s1, bf16[1024,4096]{1,0:T(8,128)(2,1)S(1)} %copy-done.3, ...), custom_call_target="tpu_custom_call" | custom-call | flops 4294967296 | tf_op jit(solution)/shard_map/score_given/pallas_call | solution.py:46
  56.8 5.2 %score_own.1.mine = f32[2,1024,256]{2,1,0:T(8,128)S(1)} custom-call(s32[4]{0:T(128)S(1)} %pad_add_fusion.place, bf16[256,4096]{1,0:T(8,128)(2,1)S(1)} %get-tuple-element.27.weights, f32[8,256]{1,0:T(8,128)S(1)} %get-tuple-element.28.power, bf16[1024,4096]{1,0:T(8,128)(2,1)S(1)} %get-tuple-element.29.shifted_a.s0, ...), custom_call_target="tpu_custom_call" | custom-call | flops 4294967296 | tf_op jit(solution)/shard_map/score_own/pallas_call | solution.py:46
  63.1 13.8 %all_to_all.5.stats = f32[8,8,128]{2,1,0:T(8,128)S(1)} all-to-all(f32[8,8,128]{2,1,0:T(8,128)S(1)} %get-tuple-element.34), channel_id=1, replica_groups=mesh['cls'=4,'grp'=4,'y'=4,'zl'=2,'core'=2] {'cls','zl'}, dimensions={0} | all-to-all | bytes 65536 | tf_op jit(solution)/shard_map/all_to_all | solution.py:323
  76.9 1.6 %posterior.1 = (bf16[2,200,1024]{2,1,0:T(8,128)(2,1)S(1)}, f32[8,40]{1,0:T(8,128)S(1)}) custom-call(s32[4]{0:T(128)S(1)} %pad_add_fusion.place, f32[2,1024,200]{2,1,0:T(8,128)S(1)} %get-tuple-element.33.log, f32[8,8,128]{2,1,0:T(8,128)S(1)} %all_to_all.5.stats, bf16[40,128]{1,0:T(8,128)(2,1)S(1)} %slice.60.meta_a, bf16[40,128]{1,0:T(8,128)(2,1)S(1)} %slice.78.meta_b), custom_call_target="tpu_custom_call" | custom-call | tf_op jit(solution)/shard_map/posterior/pallas_call | solution.py:239
  78.8 2.3 %collective-permute-done.12.theirs = bf16[2,200,1024]{2,1,0:T(8,128)(2,1)S(1)} collective-permute-done((bf16[2,200,1024]{2,1,0:T(8,128)(2,1)S(1)}, bf16[2,200,1024]{2,1,0:T(8,128)(2,1)S(1)}, u32[]{:S(2)}, u32[]{:S(2)}) %collective-permute-start.12) | collective-permute-done | bytes 819232 | tf_op jit(solution)/shard_map/ppermute | solution.py:325
  81.2 3.4 %copy-done.1 = bf16[1024,4096]{1,0:T(8,128)(2,1)S(1)} copy-done((bf16[1024,4096]{1,0:T(8,128)(2,1)S(1)}, bf16[1024,4096]{1,0:T(8,128)(2,1)}, u32[]{:S(2)}) %copy-start.1) | copy-done | bytes 8388632
  84.5 2.5 %insert_2.1 = bf16[8,208,128]{2,1,0:T(8,128)(2,1)S(1)} custom-call(s32[4]{0:T(128)S(1)} %pad_add_fusion.place, bf16[2,200,1024]{2,1,0:T(8,128)(2,1)S(1)} %get-tuple-element.35.mine, bf16[2,200,1024]{2,1,0:T(8,128)(2,1)S(1)} %collective-permute-done.12.theirs, bf16[1024,4096]{1,0:T(8,128)(2,1)S(1)} %get-tuple-element.29.shifted_a.s0, ...), custom_call_target="tpu_custom_call" | custom-call | flops 2147483648 | tf_op jit(solution)/shard_map/insert_2/pallas_call | solution.py:46
  87.0 2.2 %collective-permute-start.13 = (bf16[8,208,128]{2,1,0:T(8,128)(2,1)S(1)}, bf16[8,208,128]{2,1,0:T(8,128)(2,1)S(1)}, u32[]{:S(2)}, u32[]{:S(2)}) collective-permute-start(bf16[8,208,128]{2,1,0:T(8,128)(2,1)S(1)} %insert_2.1), channel_id=1, source_target_pairs={{0,32},{16,48},{32,0},{48,16},{1,33},{17,49},{33,1},{49,17},{2,34}... | collective-permute-start | bytes 1277960 | tf_op jit(solution)/shard_map/ppermute | solution.py:275
  89.2 2.5 %insert_1.1 = bf16[8,208,128]{2,1,0:T(8,128)(2,1)S(1)} custom-call(s32[4]{0:T(128)S(1)} %pad_add_fusion.place, bf16[2,200,1024]{2,1,0:T(8,128)(2,1)S(1)} %get-tuple-element.35.mine, bf16[2,200,1024]{2,1,0:T(8,128)(2,1)S(1)} %collective-permute-done.12.theirs, bf16[1024,4096]{1,0:T(8,128)(2,1)S(1)} %get-tuple-element.29.shifted_a.s0, ...), custom_call_target="tpu_custom_call" | custom-call | flops 2147483648 | tf_op jit(solution)/shard_map/insert_1/pallas_call | solution.py:46
  92.3 2.5 %insert_3.1 = bf16[8,208,128]{2,1,0:T(8,128)(2,1)S(1)} custom-call(s32[4]{0:T(128)S(1)} %pad_add_fusion.place, bf16[2,200,1024]{2,1,0:T(8,128)(2,1)S(1)} %get-tuple-element.35.mine, bf16[2,200,1024]{2,1,0:T(8,128)(2,1)S(1)} %collective-permute-done.12.theirs, bf16[1024,4096]{1,0:T(8,128)(2,1)S(1)} %get-tuple-element.29.shifted_a.s0, ...), custom_call_target="tpu_custom_call" | custom-call | flops 2147483648 | tf_op jit(solution)/shard_map/insert_3/pallas_call | solution.py:46
  94.8 2.9 %collective-permute-start.15 = (bf16[8,208,128]{2,1,0:T(8,128)(2,1)S(1)}, bf16[8,208,128]{2,1,0:T(8,128)(2,1)S(1)}, u32[]{:S(2)}, u32[]{:S(2)}) collective-permute-start(bf16[8,208,128]{2,1,0:T(8,128)(2,1)S(1)} %insert_3.1), channel_id=1, source_target_pairs={{0,48},{16,0},{32,16},{48,32},{1,49},{17,1},{33,17},{49,33},{2,50}... | collective-permute-start | bytes 1277960 | tf_op jit(solution)/shard_map/ppermute | solution.py:275
  97.6 2.5 %insert_0.1 = bf16[8,208,128]{2,1,0:T(8,128)(2,1)S(1)} custom-call(s32[4]{0:T(128)S(1)} %pad_add_fusion.place, bf16[2,200,1024]{2,1,0:T(8,128)(2,1)S(1)} %get-tuple-element.35.mine, bf16[2,200,1024]{2,1,0:T(8,128)(2,1)S(1)} %collective-permute-done.12.theirs, bf16[1024,4096]{1,0:T(8,128)(2,1)S(1)} %get-tuple-element.29.shifted_a.s0, ...), custom_call_target="tpu_custom_call" | custom-call | flops 2147483648 | tf_op jit(solution)/shard_map/insert_0/pallas_call | solution.py:46
  101.3 8.3 %collective-permute-done.14 = bf16[8,208,128]{2,1,0:T(8,128)(2,1)S(1)} collective-permute-done((bf16[8,208,128]{2,1,0:T(8,128)(2,1)S(1)}, bf16[8,208,128]{2,1,0:T(8,128)(2,1)S(1)}, u32[]{:S(2)}, u32[]{:S(2)}) %collective-permute-start.14) | collective-permute-done | bytes 426016 | tf_op jit(solution)/shard_map/ppermute | solution.py:275
  110.3 3.0 %collective-permute-start.18 = (bf16[2,208,128]{2,1,0:T(8,128)(2,1)S(1)}, bf16[2,208,128]{2,1,0:T(8,128)(2,1)S(1)}, u32[]{:S(2)}, u32[]{:S(2)}) collective-permute-start(bf16[2,208,128]{2,1,0:T(8,128)(2,1)S(1)} %get-tuple-element.40), channel_id=1, source_target_pairs={{0,12},{4,0},{8,4},{12,8},{1,13},{5,1},{9,5},{13,9},{2,14},{6,2},{... | collective-permute-start | bytes 319496 | tf_op jit(solution)/shard_map/ppermute | solution.py:275
  113.3 3.9 %collective-permute-done.16 = bf16[2,208,128]{2,1,0:T(8,128)(2,1)S(1)} collective-permute-done((bf16[2,208,128]{2,1,0:T(8,128)(2,1)S(1)}, bf16[2,208,128]{2,1,0:T(8,128)(2,1)S(1)}, u32[]{:S(2)}, u32[]{:S(2)}) %collective-permute-start.16) | collective-permute-done | bytes 106528 | tf_op jit(solution)/shard_map/ppermute | solution.py:275
  117.2 2.0 %collective-permute-done.17 = bf16[2,208,128]{2,1,0:T(8,128)(2,1)S(1)} collective-permute-done((bf16[2,208,128]{2,1,0:T(8,128)(2,1)S(1)}, bf16[2,208,128]{2,1,0:T(8,128)(2,1)S(1)}, u32[]{:S(2)}, u32[]{:S(2)}) %collective-permute-start.17) | collective-permute-done | bytes 106528 | tf_op jit(solution)/shard_map/ppermute | solution.py:275
  119.3 1.6 %collective-permute-start.19 = (f32[216,128]{1,0:T(8,128)S(1)}, f32[216,128]{1,0:T(8,128)S(1)}, u32[]{:S(2)}, u32[]{:S(2)}) collective-permute-start(f32[216,128]{1,0:T(8,128)S(1)} %pad_maximum_fusion.2), channel_id=1, source_target_pairs={{0,2},{2,0},{1,3},{3,1},{4,6},{6,4},{5,7},{7,5},{8,10},{10,8},{9,1... | collective-permute-start | bytes 331784 | tf_op jit(solution)/shard_map/ppermute | solution.py:341
  121.4 2.8 %collective-permute-done.19 = f32[216,128]{1,0:T(8,128)S(1)} collective-permute-done((f32[216,128]{1,0:T(8,128)S(1)}, f32[216,128]{1,0:T(8,128)S(1)}, u32[]{:S(2)}, u32[]{:S(2)}) %collective-permute-start.19) | collective-permute-done | bytes 110624 | tf_op jit(solution)/shard_map/ppermute | solution.py:341
  (73 shorter events, 16.2 us)
Async XLA Ops:
  1.4 6.5 %collective-permute-start.4 = (bf16[200,128]{1,0:T(8,128)(2,1)S(1)}, bf16[200,128]{1,0:T(8,128)(2,1)S(1)}, u32[]{:S(2)}, u32[]{:S(2)}) collective-permute-start(bf16[200,128]{1,0:T(8,128)(2,1)S(1)} %dynamic-slice_bitcast_fusion), channel_id=1, source_target_pairs={{0,2},{2,0},{1,3},{3,1},{4,6},{6,4},{5,7},{7,5},{8,10},{10,8},{9,1... | collective-permute-start | bytes 153608 | tf_op jit(solution)/shard_map/ppermute | solution.py:290
  4.8 1.1 copy-start.4
  5.9 0.9 copy-start.5
  7.7 20.2 %collective-permute-start.2 = (bf16[40,4224]{1,0:T(8,128)(2,1)S(1)}, bf16[40,4224]{1,0:T(8,128)(2,1)S(1)}, u32[]{:S(2)}, u32[]{:S(2)}) collective-permute-start(bf16[40,4224]{1,0:T(8,128)(2,1)S(1)} %get-tuple-element.23), channel_id=1, source_target_pairs={{0,194},{2,0},{64,2},{66,64},{128,66},{130,128},{192,130},{194,192... | collective-permute-start | bytes 1013768 | tf_op jit(solution)/shard_map/ppermute | solution.py:275
  7.9 21.4 %collective-permute-start = (bf16[40,4224]{1,0:T(8,128)(2,1)S(1)}, bf16[40,4224]{1,0:T(8,128)(2,1)S(1)}, u32[]{:S(2)}, u32[]{:S(2)}) collective-permute-start(bf16[40,4224]{1,0:T(8,128)(2,1)S(1)} %get-tuple-element.23), channel_id=1, source_target_pairs={{0,1},{1,0},{2,3},{3,2},{4,5},{5,4},{6,7},{7,6},{8,9},{9,8},{10,11... | collective-permute-start | bytes 1013768 | tf_op jit(solution)/shard_map/ppermute | solution.py:297
  9.4 12.1 %collective-permute-start.7 = (bf16[2,200,128]{2,1,0:T(8,128)(2,1)S(1)}, bf16[2,200,128]{2,1,0:T(8,128)(2,1)S(1)}, u32[]{:S(2)}, u32[]{:S(2)}) collective-permute-start(bf16[2,200,128]{2,1,0:T(8,128)(2,1)S(1)} %pair.1), channel_id=1, source_target_pairs={{0,4},{4,8},{8,12},{12,0},{1,5},{5,9},{9,13},{13,1},{2,6},{6,10},{... | collective-permute-start | bytes 307208 | tf_op jit(solution)/shard_map/ppermute | solution.py:271
  11.0 12.5 %collective-permute-start.6 = (bf16[2,200,128]{2,1,0:T(8,128)(2,1)S(1)}, bf16[2,200,128]{2,1,0:T(8,128)(2,1)S(1)}, u32[]{:S(2)}, u32[]{:S(2)}) collective-permute-start(bf16[2,200,128]{2,1,0:T(8,128)(2,1)S(1)} %pair.1), channel_id=1, source_target_pairs={{0,8},{4,12},{8,0},{12,4},{1,9},{5,13},{9,1},{13,5},{2,10},{6,14},... | collective-permute-start | bytes 307208 | tf_op jit(solution)/shard_map/ppermute | solution.py:271
  13.9 9.6 %collective-permute-start.5 = (bf16[2,200,128]{2,1,0:T(8,128)(2,1)S(1)}, bf16[2,200,128]{2,1,0:T(8,128)(2,1)S(1)}, u32[]{:S(2)}, u32[]{:S(2)}) collective-permute-start(bf16[2,200,128]{2,1,0:T(8,128)(2,1)S(1)} %pair.1), channel_id=1, source_target_pairs={{0,12},{4,0},{8,4},{12,8},{1,13},{5,1},{9,5},{13,9},{2,14},{6,2},{... | collective-permute-start | bytes 307208 | tf_op jit(solution)/shard_map/ppermute | solution.py:271
  15.3 0.9 copy-start.8
  16.2 0.9 copy-start.10
  17.2 12.1 %copy-start.9 = (f32[12,4096]{1,0:T(8,128)S(1)}, f32[12,4096]{1,0:T(8,128)}, u32[]{:S(2)}) copy-start(f32[12,4096]{1,0:T(8,128)} %constant.32.clone.sinv) | copy-start | bytes 589828
  21.5 12.8 %collective-permute-start.1 = (bf16[40,4224]{1,0:T(8,128)(2,1)S(1)}, bf16[40,4224]{1,0:T(8,128)(2,1)S(1)}, u32[]{:S(2)}, u32[]{:S(2)}) collective-permute-start(bf16[40,4224]{1,0:T(8,128)(2,1)S(1)} %get-tuple-element.20.images), channel_id=1, source_target_pairs={{0,2},{2,64},{64,66},{66,128},{128,130},{130,192},{192,194},{194,0... | collective-permute-start | bytes 1013768 | tf_op jit(solution)/shard_map/ppermute | solution.py:275
  23.5 22.5 %collective-permute-start.10 = (bf16[8,200,128]{2,1,0:T(8,128)(2,1)S(1)}, bf16[8,200,128]{2,1,0:T(8,128)(2,1)S(1)}, u32[]{:S(2)}, u32[]{:S(2)}) collective-permute-start(bf16[8,200,128]{2,1,0:T(8,128)(2,1)S(1)} %pad_maximum_fusion.p0), channel_id=1, source_target_pairs={{0,16},{16,32},{32,48},{48,0},{1,17},{17,33},{33,49},{49,1},{2,18}... | collective-permute-start | bytes 1228808 | tf_op jit(solution)/shard_map/ppermute | solution.py:271
  25.1 21.0 %collective-permute-start.9 = (bf16[8,200,128]{2,1,0:T(8,128)(2,1)S(1)}, bf16[8,200,128]{2,1,0:T(8,128)(2,1)S(1)}, u32[]{:S(2)}, u32[]{:S(2)}) collective-permute-start(bf16[8,200,128]{2,1,0:T(8,128)(2,1)S(1)} %pad_maximum_fusion.p0), channel_id=1, source_target_pairs={{0,32},{16,48},{32,0},{48,16},{1,33},{17,49},{33,1},{49,17},{2,34}... | collective-permute-start | bytes 1228808 | tf_op jit(solution)/shard_map/ppermute | solution.py:271
  27.8 18.2 %collective-permute-start.8 = (bf16[8,200,128]{2,1,0:T(8,128)(2,1)S(1)}, bf16[8,200,128]{2,1,0:T(8,128)(2,1)S(1)}, u32[]{:S(2)}, u32[]{:S(2)}) collective-permute-start(bf16[8,200,128]{2,1,0:T(8,128)(2,1)S(1)} %pad_maximum_fusion.p0), channel_id=1, source_target_pairs={{0,48},{16,0},{32,16},{48,32},{1,49},{17,1},{33,17},{49,33},{2,50}... | collective-permute-start | bytes 1228808 | tf_op jit(solution)/shard_map/ppermute | solution.py:271
  29.3 9.2 %collective-permute-start.3 = (bf16[40,4224]{1,0:T(8,128)(2,1)S(1)}, bf16[40,4224]{1,0:T(8,128)(2,1)S(1)}, u32[]{:S(2)}, u32[]{:S(2)}) collective-permute-start(bf16[40,4224]{1,0:T(8,128)(2,1)S(1)} %collective-permute-done.2), channel_id=1, source_target_pairs={{0,1},{1,0},{2,3},{3,2},{4,5},{5,4},{6,7},{7,6},{8,9},{9,8},{10,11... | collective-permute-start | bytes 1013768 | tf_op jit(solution)/shard_map/ppermute | solution.py:302
  38.5 18.3 %copy-start = (bf16[1024,4096]{1,0:T(8,128)(2,1)}, bf16[1024,4096]{1,0:T(8,128)(2,1)S(1)}, u32[]{:S(2)}) copy-start(bf16[1024,4096]{1,0:T(8,128)(2,1)S(1)} %get-tuple-element.30.shifted_b.s2) | copy-start | bytes 25165828
  38.5 7.5 %copy-start.6 = (f32[8,4096]{1,0:T(8,128)S(1)}, f32[8,4096]{1,0:T(8,128)}, u32[]{:S(2)}) copy-start(f32[8,4096]{1,0:T(8,128)} %ctf.3) | copy-start | bytes 393220
  42.8 3.3 %copy-start.2 = (bf16[1024,4096]{1,0:T(8,128)(2,1)}, bf16[1024,4096]{1,0:T(8,128)(2,1)S(1)}, u32[]{:S(2)}) copy-start(bf16[1024,4096]{1,0:T(8,128)(2,1)S(1)} %get-tuple-element.32.shifted_b.s3) | copy-start | bytes 25165828
  48.1 3.4 %copy-start.3 = (bf16[1024,4096]{1,0:T(8,128)(2,1)S(1)}, bf16[1024,4096]{1,0:T(8,128)(2,1)}, u32[]{:S(2)}) copy-start(bf16[1024,4096]{1,0:T(8,128)(2,1)} %copy-done.2) | copy-start | bytes 25165828
  56.6 5.3 %collective-permute-start.11 = (f32[2,1024,256]{2,1,0:T(8,128)S(1)}, f32[2,1024,256]{2,1,0:T(8,128)S(1)}, u32[]{:S(2)}, u32[]{:S(2)}) collective-permute-start(f32[2,1024,256]{2,1,0:T(8,128)S(1)} %score_given.1), channel_id=1, source_target_pairs={{0,1},{1,0},{2,3},{3,2},{4,5},{5,4},{6,7},{7,6},{8,9},{9,8},{10,11... | collective-permute-start | bytes 6291464 | tf_op jit(solution)/shard_map/ppermute | solution.py:320
  56.8 24.4 %slice-start = ((s8[8388608]{0:T(1024)(128)(4,1)}), s8[4194304]{0:T(1024)(128)(4,1)S(1)}, s32[]{:S(2)}) async-start(s8[8388608]{0:T(1024)(128)(4,1)} %bitcast.34), calls=%async_computation.1 | async-start | bytes 8388608
  56.8 24.4 %slice-start.1 = ((s8[8388608]{0:T(1024)(128)(4,1)}), s8[4194304]{0:T(1024)(128)(4,1)S(1)}, s32[]{:S(2)}) async-start(s8[8388608]{0:T(1024)(128)(4,1)} %bitcast.34), calls=%async_computation.2 | async-start | bytes 8388608
  78.5 2.6 %collective-permute-start.12 = (bf16[2,200,1024]{2,1,0:T(8,128)(2,1)S(1)}, bf16[2,200,1024]{2,1,0:T(8,128)(2,1)S(1)}, u32[]{:S(2)}, u32[]{:S(2)}) collective-permute-start(bf16[2,200,1024]{2,1,0:T(8,128)(2,1)S(1)} %get-tuple-element.35.mine), channel_id=1, source_target_pairs={{0,1},{1,0},{2,3},{3,2},{4,5},{5,4},{6,7},{7,6},{8,9},{9,8},{10,11... | collective-permute-start | bytes 2457608 | tf_op jit(solution)/shard_map/ppermute | solution.py:325
  81.2 3.4 %copy-start.1 = (bf16[1024,4096]{1,0:T(8,128)(2,1)S(1)}, bf16[1024,4096]{1,0:T(8,128)(2,1)}, u32[]{:S(2)}) copy-start(bf16[1024,4096]{1,0:T(8,128)(2,1)} %copy-done) | copy-start | bytes 25165828
  87.0 14.3 %collective-permute-start.13 = (bf16[8,208,128]{2,1,0:T(8,128)(2,1)S(1)}, bf16[8,208,128]{2,1,0:T(8,128)(2,1)S(1)}, u32[]{:S(2)}, u32[]{:S(2)}) collective-permute-start(bf16[8,208,128]{2,1,0:T(8,128)(2,1)S(1)} %insert_2.1), channel_id=1, source_target_pairs={{0,32},{16,48},{32,0},{48,16},{1,33},{17,49},{33,1},{49,17},{2,34}... | collective-permute-start | bytes 1277960 | tf_op jit(solution)/shard_map/ppermute | solution.py:275
  91.7 17.9 %collective-permute-start.14 = (bf16[8,208,128]{2,1,0:T(8,128)(2,1)S(1)}, bf16[8,208,128]{2,1,0:T(8,128)(2,1)S(1)}, u32[]{:S(2)}, u32[]{:S(2)}) collective-permute-start(bf16[8,208,128]{2,1,0:T(8,128)(2,1)S(1)} %insert_1.1), channel_id=1, source_target_pairs={{0,16},{16,32},{32,48},{48,0},{1,17},{17,33},{33,49},{49,1},{2,18}... | collective-permute-start | bytes 1277960 | tf_op jit(solution)/shard_map/ppermute | solution.py:275
  94.8 14.9 %collective-permute-start.15 = (bf16[8,208,128]{2,1,0:T(8,128)(2,1)S(1)}, bf16[8,208,128]{2,1,0:T(8,128)(2,1)S(1)}, u32[]{:S(2)}, u32[]{:S(2)}) collective-permute-start(bf16[8,208,128]{2,1,0:T(8,128)(2,1)S(1)} %insert_3.1), channel_id=1, source_target_pairs={{0,48},{16,0},{32,16},{48,32},{1,49},{17,1},{33,17},{49,33},{2,50}... | collective-permute-start | bytes 1277960 | tf_op jit(solution)/shard_map/ppermute | solution.py:275
  109.9 7.3 %collective-permute-start.16 = (bf16[2,208,128]{2,1,0:T(8,128)(2,1)S(1)}, bf16[2,208,128]{2,1,0:T(8,128)(2,1)S(1)}, u32[]{:S(2)}, u32[]{:S(2)}) collective-permute-start(bf16[2,208,128]{2,1,0:T(8,128)(2,1)S(1)} %get-tuple-element.39), channel_id=1, source_target_pairs={{0,8},{4,12},{8,0},{12,4},{1,9},{5,13},{9,1},{13,5},{2,10},{6,14},... | collective-permute-start | bytes 319496 | tf_op jit(solution)/shard_map/ppermute | solution.py:275
  110.3 6.9 %collective-permute-start.18 = (bf16[2,208,128]{2,1,0:T(8,128)(2,1)S(1)}, bf16[2,208,128]{2,1,0:T(8,128)(2,1)S(1)}, u32[]{:S(2)}, u32[]{:S(2)}) collective-permute-start(bf16[2,208,128]{2,1,0:T(8,128)(2,1)S(1)} %get-tuple-element.40), channel_id=1, source_target_pairs={{0,12},{4,0},{8,4},{12,8},{1,13},{5,1},{9,5},{13,9},{2,14},{6,2},{... | collective-permute-start | bytes 319496 | tf_op jit(solution)/shard_map/ppermute | solution.py:275
  113.3 5.9 %collective-permute-start.17 = (bf16[2,208,128]{2,1,0:T(8,128)(2,1)S(1)}, bf16[2,208,128]{2,1,0:T(8,128)(2,1)S(1)}, u32[]{:S(2)}, u32[]{:S(2)}) collective-permute-start(bf16[2,208,128]{2,1,0:T(8,128)(2,1)S(1)} %get-tuple-element.41), channel_id=1, source_target_pairs={{0,4},{4,8},{8,12},{12,0},{1,5},{5,9},{9,13},{13,1},{2,6},{6,10},{... | collective-permute-start | bytes 319496 | tf_op jit(solution)/shard_map/ppermute | solution.py:275
  119.3 4.8 %collective-permute-start.19 = (f32[216,128]{1,0:T(8,128)S(1)}, f32[216,128]{1,0:T(8,128)S(1)}, u32[]{:S(2)}, u32[]{:S(2)}) collective-permute-start(f32[216,128]{1,0:T(8,128)S(1)} %pad_maximum_fusion.2), channel_id=1, source_target_pairs={{0,2},{2,0},{1,3},{3,1},{4,6},{6,4},{5,7},{7,5},{8,10},{10,8},{9,1... | collective-permute-start | bytes 331784 | tf_op jit(solution)/shard_map/ppermute | solution.py:341
  (1 other events, 0.9 us)
where the time goes:
time: 127 us; the launch traced here: 126 us
  Pallas kernels  43.5 us (34%)
  starting transfers between devices  26.7 us (21%)
  waiting for transfers between devices  21.2 us (17%)
  local copies, waits for them, and re-layouts  16.2 us (13%)
  blocking collectives  13.8 us (11%)
  other arithmetic  2.52 us (2%)
  between operations  1.62 us (1%)
    pallas_call x10, Pallas kernels, call(): pl.pallas_call(kernel, name=name, in_specs=[SMEM] + [VMEM] * (len(args) -...  24.8 us
    pallas_call x4, Pallas kernels, build_call(): pl.pallas_call(build_kernel, name=name, in_specs=[SMEM] + [VMEM] * 4, out...  17 us
    ppermute x8, waiting for transfers between devices, push(): return lax.ppermute(value, axis, [(i, (i + d) % n) for i in range(n)])  16.1 us
    unnamed x26, local copies, waits for them, and re-layouts  14.8 us
    all_to_all x1, blocking collectives, body(): stats = lax.all_to_all(stats, ring, 0, 0, tiled=True)  13.8 us
    ppermute x6, starting transfers between devices, take(): return lax.ppermute(value, axis, [(i, (i - d) % n) for i in range(n)])  11.6 us
    ppermute x8, starting transfers between devices, push(): return lax.ppermute(value, axis, [(i, (i + d) % n) for i in range(n)])  11.3 us
    ppermute x1, waiting for transfers between devices, body(): came = lax.ppermute(jnp.concatenate([leave, tally]), 'zl', SWAP)  2.77 us
  transfers between devices with their start and end apart: 20, of which 7 were waited for; matrix products, arithmetic and copies ran while one was open for 1% of the time, Pallas kernels for 25%

commit v1 on v0

v1 whole, which is shorter than its diff:
```python
import math

import jax
import jax.numpy as jnp
import numpy as np
from jax import lax
from jax.experimental import pallas as pl
from jax.experimental.pallas import tpu as pltpu
from jax.sharding import Mesh, PartitionSpec as P

IMG = 64
SIDE = 5
SHIFTS = SIDE * SIDE
HALF = SHIFTS // 2
GROUPS = 8
FREQS = IMG * IMG
LANE = 128
SLOTS = 40
ROWS = 1024
WIDTH = 200
WIDE = 256
TALL = WIDTH + 8
COUNTED = SLOTS * SHIFTS
BLOCKS = 32
DEPTH = BLOCKS * LANE
CHUNK = DEPTH // 4
HIGHEST = lax.Precision.HIGHEST
F32 = jnp.float32
BF16 = jnp.bfloat16
MIB = 2**20
LIMIT = 4
VMEM = pl.BlockSpec(memory_space=pltpu.VMEM)
SMEM = pl.BlockSpec(memory_space=pltpu.SMEM)
SWAP = [(0, 1), (1, 0)]


def shift_tables():
    index = np.arange(FREQS)
    shift = np.arange(HALF)
    offx = shift // SIDE - SIDE // 2
    offy = shift % SIDE - SIDE // 2
    phase = (offx[:, None] * (index // IMG)[None, :] + offy[:, None] * (index % IMG)[None, :]) % IMG
    theta = (phase.astype(np.float32) * np.float32(2.0 * math.pi / IMG)).astype(np.float64)
    return np.cos(theta).astype(np.float32), np.sin(theta).astype(np.float32)


def call(kernel, name, out, args, limit, flops=0, moved=0):
    return pl.pallas_call(
        kernel,
        name=name,
        in_specs=[SMEM] + [VMEM] * (len(args) - 1),
        out_specs=jax.tree.map(lambda _: VMEM, out),
        out_shape=out,
        cost_estimate=pl.CostEstimate(flops=flops, bytes_accessed=moved, transcendentals=0),
        compiler_params=pltpu.CompilerParams(vmem_limit_bytes=limit * MIB),
    )(*args)


def shape(*dims, dtype=F32):
    return jax.ShapeDtypeStruct(dims, dtype)


def lanes(block):
    return pl.ds(pl.multiple_of(block * LANE, LANE), LANE)


def cut(value):
    first = value.astype(BF16)
    rest = value - first.astype(F32)
    second = rest.astype(BF16)
    return first, second, (rest - second.astype(F32)).astype(BF16)


def split_kernel(place, meta, unit, images, ctf, tables, kept, given, parts, turns, held, images_in, ctf_in, sems):
    core = place[3]
    copies = [
        pltpu.make_async_copy(source, target, sems.at[i])
        for i, (source, target) in enumerate(((images, images_in), (ctf, ctf_in), (tables, turns)))
    ]
    for copy in copies:
        copy.start()
    copies[1].wait()
    held[...] = ctf_in[...]
    for i, part in enumerate(cut(ctf_in[...])):
        parts[16 * i : 16 * i + 16, :] = jnp.concatenate([part.astype(F32), jnp.zeros((8, FREQS), F32)], axis=0).astype(BF16)
    copies[0].wait()

    def turn(j, carry):
        kept[:, lanes(j)] = images_in[:, lanes(2 * j + core)]
        given[:, lanes(j)] = images_in[:, lanes(2 * j + 1 - core)]
        return carry

    lax.fori_loop(0, BLOCKS, turn, 0)
    kept[:, DEPTH:] = meta[...]
    given[:, DEPTH:] = meta[...]
    copies[2].wait()


def split_call(place, meta, unit, images, ctf, tables):
    half = shape(SLOTS, DEPTH + LANE, dtype=BF16)
    anywhere = pl.BlockSpec(memory_space=pltpu.HBM)
    return pl.pallas_call(
        split_kernel,
        name="split",
        in_specs=[SMEM, VMEM, VMEM, anywhere, anywhere, anywhere],
        out_specs=[VMEM] * 5,
        out_shape=[half, half, shape(48, FREQS, dtype=BF16), shape(2 * HALF, FREQS), shape(GROUPS, FREQS)],
        scratch_shapes=[
            pltpu.VMEM((SLOTS, 2 * DEPTH), BF16),
            pltpu.VMEM((GROUPS, FREQS), F32),
            pltpu.SemaphoreType.DMA((3,)),
        ],
        compiler_params=pltpu.CompilerParams(vmem_limit_bytes=LIMIT * MIB),
    )(place, meta, unit, images, ctf, tables)


def owner_block(place, p):
    return (place[0] ^ (p // 8)) * 8 + (place[1] ^ (p % 8 // 2)) * 2 + (place[2] ^ (p % 2))


def build_kernel(place, after, images, parts, turns, out0, out1, out2, out3, token, rows):
    core = place[3]
    group = images[:, DEPTH : DEPTH + 1].astype(F32)
    lane = lax.broadcasted_iota(jnp.int32, (SLOTS, 48), 1)
    hot = jnp.where((group == (lane % 16).astype(F32)) & (lane % 16 < GROUPS), 1.0, 0.0).astype(BF16)
    rows[...] = jnp.dot(hot, parts[...], preferred_element_type=F32)
    for dx, out in enumerate((out0, out1, out2, out3)):

        def turn(p, carry):
            j = owner_block(place, 8 * dx + p)
            at = lanes(2 * (j % 16) + core)
            sign = jnp.where(j < 16, 1.0, -1.0).astype(F32)
            row = rows[:, at]
            first = images[:, lanes(j)].astype(F32) * row
            second = images[:, lanes(j ^ 16)].astype(F32) * (row * sign)
            here = lanes(p)
            for s in range(HALF):
                a = first * turns[s : s + 1, at]
                b = second * turns[HALF + s : HALF + s + 1, at]
                out[2 * SLOTS * s : 2 * SLOTS * (s + 1), here] = jnp.concatenate([a + b, a - b], axis=0).astype(BF16)
            tail = jnp.concatenate([first, jnp.zeros((ROWS - SLOTS * SHIFTS, LANE), F32)], axis=0)
            out[2 * SLOTS * HALF : ROWS, here] = tail.astype(BF16)
            return carry

        lax.fori_loop(0, 8, turn, 0, unroll=2)
    token[...] = jnp.zeros_like(token)


def build_call(place, after, images, parts, turns, name):
    return pl.pallas_call(
        build_kernel,
        name=name,
        in_specs=[SMEM] + [VMEM] * 4,
        out_specs=[VMEM] * 5,
        out_shape=[shape(ROWS, CHUNK, dtype=BF16)] * 4 + [shape(8, LANE)],
        scratch_shapes=[pltpu.VMEM((SLOTS, FREQS), F32)],
        cost_estimate=pl.CostEstimate(flops=6 * 10**9, bytes_accessed=2 * ROWS * DEPTH, transcendentals=0),
        compiler_params=pltpu.CompilerParams(vmem_limit_bytes=LIMIT * MIB),
    )(place, after, images, parts, turns)


def hot_rows(meta):
    group = meta[:, 0:1].astype(F32)
    lane = lax.broadcasted_iota(jnp.int32, (SLOTS, GROUPS), 1).astype(F32)
    return jnp.where(group == lane, 1.0, 0.0).astype(F32)


def stack_of(piece):
    return jnp.concatenate([piece[r] for r in range(8)], axis=1)


def weigh_kernel(place, ctf, t0, t1, t2, t3, p0, p1, p2, p3, power):
    core = place[3]
    total = jnp.zeros((3 * GROUPS, WIDTH), F32)
    for q, piece in enumerate((p0, p1, p2, p3)):
        left = jnp.concatenate([ctf[:, lanes(2 * (owner_block(place, 8 * q + r) % 16) + core)] for r in range(8)], axis=1)
        parts = jnp.concatenate([part.astype(F32) for part in cut(left * left)], axis=0).astype(BF16)
        square = stack_of(piece).astype(F32)
        square = square * square
        high = square.astype(BF16)
        low = (square - high.astype(F32)).astype(BF16)
        dims = (((1,), (1,)), ((), ()))
        total = total + lax.dot_general(parts, high, dims, preferred_element_type=F32)
        total = total + lax.dot_general(parts, low, dims, preferred_element_type=F32)
    power[...] = total[:GROUPS] + total[GROUPS : 2 * GROUPS] + total[2 * GROUPS :]


def score_kernel(place, power, meta_a, meta_b, p0, p1, p2, p3, *refs):
    out = refs[8]
    for k, meta in enumerate((meta_a, meta_b)):
        half = 0.5 * jnp.dot(hot_rows(meta[...]), power[...], precision=HIGHEST, preferred_element_type=F32)
        sums = None
        for dx, piece in enumerate((p0, p1, p2, p3)):
            part = lax.dot_general(
                refs[4 * k + dx][...], stack_of(piece), (((1,), (1,)), ((), ())), preferred_element_type=F32
            )
            sums = part if sums is None else sums + part
        spare = jnp.zeros((ROWS - SLOTS * SHIFTS, WIDTH), F32)
        out[k, :, :WIDTH] = sums - jnp.concatenate([half] * SHIFTS + [spare], axis=0)


def settle_kernel(place, mine, theirs, stats):
    columns = []
    for k in range(2):

        def value(s):
            at = slice(SLOTS * s, SLOTS * (s + 1))
            return mine[k, at, :WIDTH] + theirs[k, at, :WIDTH]

        best = value(0)
        for s in range(1, SHIFTS):
            best = jnp.maximum(best, value(s))
        top = jnp.max(best, axis=1, keepdims=True)
        total = jnp.exp(value(0) - top)
        for s in range(1, SHIFTS):
            total = total + jnp.exp(value(s) - top)
        columns += [top, jnp.sum(total, axis=1, keepdims=True)]
    lane = lax.broadcasted_iota(jnp.int32, (SLOTS, LANE), 1)
    spread = jnp.where(lane == 0, columns[0], jnp.where(lane == 1, columns[1], jnp.where(lane == 2, columns[2], columns[3])))
    spread = jnp.concatenate([spread, jnp.zeros((LANE - SLOTS, LANE), F32)], axis=0).T[:8, :]
    for d in range(8):
        stats[d] = spread


def posterior_kernel(place, mine, theirs, stats, meta_a, meta_b, low, evidence, spare):
    parity = place[2]
    counted = jnp.zeros((GROUPS, WIDTH), F32)
    for k, meta in ((1, meta_b), (0, meta_a)):
        tops, totals = [], []
        for d in range(8):
            same = (parity == d % 2) == (k == 0)
            here = stats[d, :, :SLOTS]
            tops.append(jnp.where(same, here[0:1], here[2:3]))
            totals.append(jnp.where(same, here[1:2], here[3:4]))
        tops = jnp.concatenate(tops, axis=0)
        totals = jnp.concatenate(totals, axis=0)
        top = jnp.max(tops, axis=0, keepdims=True)
        total = jnp.sum(totals * jnp.exp(tops - top), axis=0, keepdims=True)
        row = lax.broadcasted_iota(jnp.int32, (8, SLOTS), 0)
        columns = jnp.where(row == 0, top, jnp.where(row == 1, total, top + jnp.log(total))).T
        live = meta[:, 1:2].astype(F32)
        scale = live / columns[:, 1:2]
        if k == 0:
            known = jnp.where(live > 0.0, columns[:, 2:3], 0.0)
            evidence[...] = jnp.broadcast_to(known, (SLOTS, LANE)).T[:8, :]
        gathered = None
        for s in range(SHIFTS):
            at = slice(SLOTS * s, SLOTS * (s + 1))
            value = jnp.exp(mine[k, at, :WIDTH] + theirs[k, at, :WIDTH] - columns[:, 0:1]) * scale
            spare[at, :] = value
            gathered = value if gathered is None else gathered + value
        hot = hot_rows(meta[...])
        counted = counted + lax.dot_general(
            hot, gathered, (((0,), (0,)), ((), ())), precision=HIGHEST, preferred_element_type=F32
        )
        spare[SLOTS * SHIFTS :, :] = jnp.zeros((ROWS - SLOTS * SHIFTS, WIDTH), F32)
        if k == 0:
            first = counted.astype(BF16).astype(F32)
            spare[COUNTED : COUNTED + GROUPS, :] = first
            spare[COUNTED + GROUPS : COUNTED + 2 * GROUPS, :] = counted - first
        low[k] = spare[...].T.astype(BF16)


def posterior_call(*args):
    out = [shape(2, WIDTH, ROWS, dtype=BF16), shape(8, SLOTS)]
    return pl.pallas_call(
        posterior_kernel,
        name="posterior",
        in_specs=[SMEM] + [VMEM] * (len(args) - 1),
        out_specs=[VMEM] * 2,
        out_shape=out,
        scratch_shapes=[pltpu.VMEM((ROWS, WIDTH), F32)],
        compiler_params=pltpu.CompilerParams(vmem_limit_bytes=LIMIT * MIB),
    )(*args)


def insert_kernel(chunks):
    def kernel(place, after, mine, theirs, *refs):
        shifted_refs, outs = refs[: 4 * chunks], refs[4 * chunks :]
        low = jnp.concatenate([mine[0], theirs[0], mine[1], theirs[1]], axis=1)
        tail = slice(ROWS - LANE, ROWS)
        start = COUNTED - ROWS + LANE
        both = (mine[0, :, tail].astype(F32) + theirs[0, :, tail].astype(F32)).T
        both = both[start : start + GROUPS] + both[start + GROUPS : start + 2 * GROUPS]
        both = jnp.concatenate([both, jnp.zeros((GROUPS, WIDE - WIDTH), F32)], axis=1)
        outs[-1][...] = jnp.zeros((8, LANE), F32)
        for i, out in enumerate(outs[:-1]):
            columns = shifted_refs[4 * i : 4 * i + 4]
            for n in range(0, 8, 2):
                at = slice(LANE * n, LANE * (n + 2))
                shifted = jnp.concatenate([s[:, at] for s in columns], axis=0)
                sums = jnp.dot(low, shifted, preferred_element_type=F32)
                for r in range(2):
                    out[n + r, :WIDTH, :] = sums[:, r * LANE : (r + 1) * LANE].astype(out.dtype)
            for n in range(8):
                out[n, WIDTH:, :] = both[:, LANE * (n % 2) : LANE * (n % 2 + 1)].astype(out.dtype)

    return kernel


def absorb_kernel(place, own, far, out):
    out[...] = own[...] + far[...].astype(F32)


def gather_kernel(place, own, one, three, out):
    def total(n, rows):
        return own[n, rows] + one[n, rows].astype(F32) + three[n, rows].astype(F32)

    tail = slice(WIDTH, TALL)
    both = jnp.concatenate([total(0, tail), total(1, tail)], axis=0).astype(BF16)
    for n in range(8):
        to = (place[1] ^ (n // 2)) * 2 + (place[2] ^ (n % 2))
        out[to, :WIDTH] = total(n, slice(0, WIDTH)).astype(BF16)
        out[to, WIDTH:] = both


def finish_kernel(place, blocks, insertions, weights):
    for k in range(2):
        parts = [blocks[2 * n + k].astype(F32) for n in range(4)]
        sums = (parts[0] + parts[1]) + (parts[2] + parts[3])
        insertions[k] = sums[:WIDTH]
        weights[k] = jnp.concatenate([sums[WIDTH:TALL], sums[TALL:]], axis=1)[:, :WIDTH]


def swap(value, axis, d, n=4):
    return lax.ppermute(value, axis, [(i, i ^ d) for i in range(n)])


def body(particle_images, particle_groups, live_counts, ctf_table, projections):
    x, y, zl, core = (lax.axis_index(a) for a in ("grp", "y", "zl", "core"))
    place = jnp.stack([x, y, zl, core]).astype(jnp.int32)
    ring = ("cls", "zl")

    slot = jnp.arange(SLOTS, dtype=jnp.int32)
    live = slot < live_counts[0]
    lane = jnp.arange(LANE, dtype=jnp.int32)[None, :]
    meta = jnp.where(lane == 0, particle_groups[:, None], jnp.where(lane == 1, live.astype(jnp.int32)[:, None], 0)).astype(BF16)

    stacks = jnp.transpose(projections, (1, 2, 0))
    mine = lax.dynamic_index_in_dim(stacks, zl, axis=0)
    theirs = lax.dynamic_index_in_dim(stacks, 1 - zl, axis=0)
    unit = jnp.concatenate([mine, lax.ppermute(theirs, "zl", SWAP)])

    tables = np.concatenate(shift_tables())
    kept, other, parts, turns, ctf = split_call(place, meta, unit, particle_images, ctf_table, tables)
    halves = [kept, lax.ppermute(other, "core", SWAP)]

    column = jnp.concatenate([unit] + [swap(unit, "y", d) for d in (1, 2, 3)])
    next_kept = lax.ppermute(kept, "zl", SWAP)
    next_other = lax.ppermute(other, ring, [(i, (i + 1) % 8 if i % 2 else (i + 7) % 8) for i in range(8)])
    halves += [next_kept, lax.ppermute(next_other, "core", SWAP)]
    pieces = [column] + [swap(column, "grp", d) for d in (1, 2, 3)]

    metas = [h[:, DEPTH:] for h in halves]
    built = [build_call(place, column, h, parts, turns, f"build_{i}") for i, h in enumerate(halves)]
    shifted = [b[:4] for b in built]
    tokens = [b[4] for b in built]
    power = call(
        weigh_kernel,
        "weigh",
        shape(GROUPS, WIDTH),
        (place, ctf, *tokens, *pieces),
        LIMIT,
    )
    score = shape(2, ROWS, WIDE)
    flops = 4 * ROWS * WIDE * DEPTH
    given = call(score_kernel, "score_given", score, (place, power, metas[1], metas[3], *pieces, *shifted[1], *shifted[3]), LIMIT, flops)
    taken = lax.ppermute(given, "core", SWAP)
    kept_score = call(score_kernel, "score_own", score, (place, power, metas[0], metas[2], *pieces, *shifted[0], *shifted[2]), LIMIT, flops)
    stats = call(settle_kernel, "settle", shape(8, 8, LANE), (place, kept_score, taken), LIMIT)
    stats = lax.all_to_all(stats, ring, 0, 0, tiled=True)
    low, evidence = posterior_call(place, kept_score, taken, stats, metas[0], metas[2])
    other_low = lax.ppermute(low, "core", SWAP)

    flops = 2 * 4 * ROWS * WIDE * 1024
    chunk = shape(8, TALL, LANE, dtype=BF16)
    token = shape(8, LANE)

    def columns(*chunks):
        return [group[q] for q in chunks for group in shifted]

    send, after = call(insert_kernel(1), "insert_far", [chunk, token], (place, evidence, low, other_low, *columns(2)), LIMIT, flops)
    far = swap(send, "grp", 2)
    one, three, after = call(
        insert_kernel(2), "insert_near", [chunk, chunk, token], (place, after, low, other_low, *columns(1, 3)), LIMIT, 2 * flops
    )
    near = [swap(one, "grp", 1), swap(three, "grp", 3)]
    own, _ = call(insert_kernel(1), "insert_own", [shape(8, TALL, LANE), token], (place, after, low, other_low, *columns(0)), LIMIT, flops)
    own = call(absorb_kernel, "absorb", shape(8, TALL, LANE), (place, own, far), LIMIT)
    mixed = call(gather_kernel, "gather", shape(8, TALL + GROUPS, LANE, dtype=BF16), (place, own, *near), LIMIT)
    blocks = lax.all_to_all(mixed, ("y", "zl"), 0, 0, tiled=True)
    insertions, tally = call(finish_kernel, "finish", [shape(2, WIDTH, LANE), shape(2, GROUPS, WIDTH)], (place, blocks), LIMIT)
    return insertions, tally, evidence[0]


def solution(mesh):
    fine = Mesh(mesh.devices.reshape(4, 4, 4, 2, 2), ("cls", "grp", "y", "zl", "core"))
    shards = ("grp", "y", "zl", "core")
    return jax.shard_map(
        body,
        mesh=fine,
        in_specs=(P(shards, None), P(shards), P(shards), P(), P(shards, "cls", None)),
        out_specs=(P("cls", None, shards), P("cls", None, None), P(shards)),
        check_vma=False,
    )
```

time: 127 us -> 115 us (0.906)
  local copies, waits for them, and re-layouts: 16.2 us -> 5.21 us
  blocking collectives: 13.8 us -> 11 us
  Pallas kernels: 43.5 us -> 45.6 us
  other arithmetic: 2.52 us -> 0.83 us
    unnamed x26 -> x10, local copies, waits for them, and re-layouts: 14.8 us -> 3.85 us
    all_to_all x0 -> x1, waiting for transfers between devices: none -> 7.55 us  [body(): blocks = lax.all_to_all(mixed, ('y', 'zl'), 0, 0, tiled=True)]
    ppermute x16 -> x12, waiting for transfers between devices: 18.9 us -> 12.1 us  [the longest x9 12 us: swap(): return lax.ppermute(value, axis, [(i, i ^ d) for i in range(n)])]
    all_to_all x0 -> x1, starting transfers between devices: none -> 5.93 us  [body(): blocks = lax.all_to_all(mixed, ('y', 'zl'), 0, 0, tiled=True)]
    ppermute x16 -> x12, starting transfers between devices: 26.3 us -> 20.8 us  [the longest x9 12.9 us: swap(): return lax.ppermute(value, axis, [(i, i ^ d) for i in range(n)])]
    all_to_all x1, blocking collectives: 13.8 us -> 11 us  [body(): stats = lax.all_to_all(stats, ring, 0, 0, tiled=True)]
    another operation x5 -> x0, other arithmetic: 1.57 us -> none  [the longest x2 0.73 us: body(): jnp.stack([jnp.where(zl == 0, stay, came), jnp.where(zl == 0, came, stay)])]
    pallas_call x0 -> x1, Pallas kernels: none -> 1.47 us  [split_call(): pl.pallas_call(split_kernel, name='split', in_specs=[SMEM, VMEM, VMEM, an...]
  transfers between devices with their start and end apart: 20 -> 17, of which waited for: 7 -> 6; matrix products, arithmetic and copies ran while one was open for 1% -> 2% of each run, Pallas kernels for 25% -> 27%
where the time goes in v1:
time: 115 us; the launch traced here: 113 us
  Pallas kernels  45.6 us (40%)
  starting transfers between devices  27.2 us (24%)
  waiting for transfers between devices  21.9 us (19%)
  blocking collectives  11 us (10%)
  local copies, waits for them, and re-layouts  5.21 us (5%)
  between operations  1.53 us (1%)
    pallas_call x10, Pallas kernels, call(): pl.pallas_call(kernel, name=name, in_specs=[SMEM] + [VMEM] * (len(args) -...  26.2 us
    pallas_call x4, Pallas kernels, build_call(): pl.pallas_call(build_kernel, name=name, in_specs=[SMEM] + [VMEM] * 4, out...  16.3 us
    ppermute x9, starting transfers between devices, swap(): return lax.ppermute(value, axis, [(i, i ^ d) for i in range(n)])  12.9 us
    ppermute x9, waiting for transfers between devices, swap(): return lax.ppermute(value, axis, [(i, i ^ d) for i in range(n)])  12 us
    all_to_all x1, blocking collectives, body(): stats = lax.all_to_all(stats, ring, 0, 0, tiled=True)  11 us
    all_to_all x1, waiting for transfers between devices, body(): blocks = lax.all_to_all(mixed, ('y', 'zl'), 0, 0, tiled=True)  7.55 us
    all_to_all x1, starting transfers between devices, body(): blocks = lax.all_to_all(mixed, ('y', 'zl'), 0, 0, tiled=True)  5.93 us
    ppermute x1, starting transfers between devices, body(): next_kept = lax.ppermute(kept, 'zl', SWAP)  4.01 us
  transfers between devices with their start and end apart: 17, of which 6 were waited for; matrix products, arithmetic and copies ran while one was open for 2% of the time, Pallas kernels for 27%

profile of v1, /device:TPU:32, one launch (start us, length us, event | category | flops | bytes accessed | tf_op | source)
XLA Modules:
  0.0 113.3 jit_solution(12938840020555644898)
XLA Ops:
  1.4 1.8 %collective-permute-start = (bf16[1,200,128]{2,1,0:T(8,128)(2,1)S(1)}, bf16[1,200,128]{2,1,0:T(8,128)(2,1)S(1)}, u32[]{:S(2)}, u32[]{:S(2)}) collective-permute-start(bf16[1,200,128]{2,1,0:T(8,128)(2,1)S(1)} %dynamic-slice_bitcast_fusion), channel_id=1, source_target_pairs={{0,2},{2,0},{1,3},{3,1},{4,6},{6,4},{5,7},{7,5},{8,10},{10,8},{9,1... | collective-permute-start | bytes 153608 | tf_op jit(solution)/shard_map/ppermute | solution.py:342
  4.0 0.8 constant_dynamic-update-slice_fusion.4
  5.6 3.1 %collective-permute-start.3 = (bf16[2,200,128]{2,1,0:T(8,128)(2,1)S(1)}, bf16[2,200,128]{2,1,0:T(8,128)(2,1)S(1)}, u32[]{:S(2)}, u32[]{:S(2)}) collective-permute-start(bf16[2,200,128]{2,1,0:T(8,128)(2,1)S(1)} %pad_maximum_fusion.unit), channel_id=1, source_target_pairs={{0,12},{4,8},{8,4},{12,0},{1,13},{5,9},{9,5},{13,1},{2,14},{6,10},... | collective-permute-start | bytes 307208 | tf_op jit(solution)/shard_map/ppermute | solution.py:326
  9.8 1.1 copy-done
  10.9 1.0 copy-done.1
  11.9 0.9 copy-done.2
  12.8 1.5 %split.1 = (bf16[40,4224]{1,0:T(8,128)(2,1)S(1)}, bf16[40,4224]{1,0:T(8,128)(2,1)S(1)}, bf16[48,4096]{1,0:T(8,128)(2,1)S(1)}, f32[24,4096]{1,0:T(8,128)S(1)}, f32[8,4096]{1,0:T(8,128)S(1)}) custom-call(s32[4]{0:T(128)S(1)} %pad_add_fusion.place, bf16[40,128]{1,0:T(8,128)(2,1)S(1)} %select_convert_fusion.meta, bf16[2,200,128]{2,1,0:T(8,128)(2,1)S(1)} %pad_maximum_fusion.unit, ...), custom_call_target="tpu_custom_call" | custom-call | tf_op jit(solution)/shard_map/split/pallas_call | solution.py:102
  14.3 2.1 %collective-permute-start.6 = (bf16[40,4224]{1,0:T(8,128)(2,1)S(1)}, bf16[40,4224]{1,0:T(8,128)(2,1)S(1)}, u32[]{:S(2)}, u32[]{:S(2)}) collective-permute-start(bf16[40,4224]{1,0:T(8,128)(2,1)S(1)} %get-tuple-element.43), channel_id=1, source_target_pairs={{0,194},{2,64},{64,2},{66,128},{128,66},{130,192},{192,130},{194,0... | collective-permute-start | bytes 1013768 | tf_op jit(solution)/shard_map/ppermute | solution.py:350
  16.4 4.0 %collective-permute-start.5 = (bf16[40,4224]{1,0:T(8,128)(2,1)S(1)}, bf16[40,4224]{1,0:T(8,128)(2,1)S(1)}, u32[]{:S(2)}, u32[]{:S(2)}) collective-permute-start(bf16[40,4224]{1,0:T(8,128)(2,1)S(1)} %get-tuple-element.39.images), channel_id=1, source_target_pairs={{0,2},{2,0},{1,3},{3,1},{4,6},{6,4},{5,7},{7,5},{8,10},{10,8},{9,1... | collective-permute-start | bytes 1013768 | tf_op jit(solution)/shard_map/ppermute | solution.py:349
  20.5 2.8 %collective-permute-start.10 = (bf16[8,200,128]{2,1,0:T(8,128)(2,1)S(1)}, bf16[8,200,128]{2,1,0:T(8,128)(2,1)S(1)}, u32[]{:S(2)}, u32[]{:S(2)}) collective-permute-start(bf16[8,200,128]{2,1,0:T(8,128)(2,1)S(1)} %constant_dynamic-update-slice_fusion.after.p0), channel_id=1, source_target_pairs={{0,48},{16,32},{32,16},{48,0},{1,49},{17,33},{33,17},{49,1},{2,50}... | collective-permute-start | bytes 1228808 | tf_op jit(solution)/shard_map/ppermute | solution.py:326
  24.1 4.1 %build_0.1 = (bf16[1024,1024]{1,0:T(8,128)(2,1)S(1)}, bf16[1024,1024]{1,0:T(8,128)(2,1)S(1)}, bf16[1024,1024]{1,0:T(8,128)(2,1)S(1)}, bf16[1024,1024]{1,0:T(8,128)(2,1)S(1)}, f32[8,128]{1,0:T(8,128)S(1)}) custom-call(s32[4]{0:T(128)S(1)} %pad_add_fusion.place, bf16[8,200,128]{2,1,0:T(8,128)(2,1)S(1)} %constant_dynamic-update-slice_fusion.after.p0, ...), custom_call_target="tpu_custom_call" | custom-call | flops 6000000000 | bytes 8388608 | tf_op jit(solution)/shard_map/build_0/pallas_call | solution.py:150
  28.8 4.1 %build_1.1 = (bf16[1024,1024]{1,0:T(8,128)(2,1)S(1)}, bf16[1024,1024]{1,0:T(8,128)(2,1)S(1)}, bf16[1024,1024]{1,0:T(8,128)(2,1)S(1)}, bf16[1024,1024]{1,0:T(8,128)(2,1)S(1)}, f32[8,128]{1,0:T(8,128)S(1)}) custom-call(s32[4]{0:T(128)S(1)} %pad_add_fusion.place, bf16[8,200,128]{2,1,0:T(8,128)(2,1)S(1)} %constant_dynamic-update-slice_fusion.after.p0, ...), custom_call_target="tpu_custom_call" | custom-call | flops 6000000000 | bytes 8388608 | tf_op jit(solution)/shard_map/build_1/pallas_call | solution.py:150
  32.9 4.1 %build_2.1 = (bf16[1024,1024]{1,0:T(8,128)(2,1)S(1)}, bf16[1024,1024]{1,0:T(8,128)(2,1)S(1)}, bf16[1024,1024]{1,0:T(8,128)(2,1)S(1)}, bf16[1024,1024]{1,0:T(8,128)(2,1)S(1)}, f32[8,128]{1,0:T(8,128)S(1)}) custom-call(s32[4]{0:T(128)S(1)} %pad_add_fusion.place, bf16[8,200,128]{2,1,0:T(8,128)(2,1)S(1)} %constant_dynamic-update-slice_fusion.after.p0, ...), custom_call_target="tpu_custom_call" | custom-call | flops 6000000000 | bytes 8388608 | tf_op jit(solution)/shard_map/build_2/pallas_call | solution.py:150
  37.0 4.1 %build_3.1 = (bf16[1024,1024]{1,0:T(8,128)(2,1)S(1)}, bf16[1024,1024]{1,0:T(8,128)(2,1)S(1)}, bf16[1024,1024]{1,0:T(8,128)(2,1)S(1)}, bf16[1024,1024]{1,0:T(8,128)(2,1)S(1)}, f32[8,128]{1,0:T(8,128)S(1)}) custom-call(s32[4]{0:T(128)S(1)} %pad_add_fusion.place, bf16[8,200,128]{2,1,0:T(8,128)(2,1)S(1)} %constant_dynamic-update-slice_fusion.after.p0, ...), custom_call_target="tpu_custom_call" | custom-call | flops 6000000000 | bytes 8388608 | tf_op jit(solution)/shard_map/build_3/pallas_call | solution.py:150
  41.1 1.0 collective-permute-done.10.p3
  42.8 1.6 %weigh.1.power = f32[8,200]{1,0:T(8,128)S(1)} custom-call(s32[4]{0:T(128)S(1)} %pad_add_fusion.place, f32[8,4096]{1,0:T(8,128)S(1)} %get-tuple-element.38.ctf, f32[8,128]{1,0:T(8,128)S(1)} %get-tuple-element.42.t0, f32[8,128]{1,0:T(8,128)S(1)} %get-tuple-element.44.t1, f32[8,128]{1,0:T(8,128)S(1)} %get-tuple-element.45.t2, ...), custom_call_target="tpu_custom_call" | custom-call | tf_op jit(solution)/shard_map/weigh/pallas_call | solution.py:48
  44.4 5.2 %score_given.1 = f32[2,1024,256]{2,1,0:T(8,128)S(1)} custom-call(s32[4]{0:T(128)S(1)} %pad_add_fusion.place, f32[8,200]{1,0:T(8,128)S(1)} %weigh.1.power, bf16[40,128]{1,0:T(8,128)(2,1)S(1)} %slice.21.meta_a, bf16[40,128]{1,0:T(8,128)(2,1)S(1)} %slice.22.meta_b, bf16[8,200,128]{2,1,0:T(8,128)(2,1)S(1)} %constant_dynamic-update-slice_fusion.after.p0, ...), custom_call_target="tpu_custom_call" | custom-call | flops 4294967296 | tf_op jit(solution)/shard_map/score_given/pallas_call | solution.py:48
  49.7 5.2 %score_own.1.mine = f32[2,1024,256]{2,1,0:T(8,128)S(1)} custom-call(s32[4]{0:T(128)S(1)} %pad_add_fusion.place, f32[8,200]{1,0:T(8,128)S(1)} %weigh.1.power, bf16[40,128]{1,0:T(8,128)(2,1)S(1)} %slice.15.meta_a, bf16[40,128]{1,0:T(8,128)(2,1)S(1)} %slice.20.meta_b, bf16[8,200,128]{2,1,0:T(8,128)(2,1)S(1)} %constant_dynamic-update-slice_fusion.after.p0, ...), custom_call_target="tpu_custom_call" | custom-call | flops 4294967296 | tf_op jit(solution)/shard_map/score_own/pallas_call | solution.py:48
  54.9 1.2 %settle.1 = f32[8,8,128]{2,1,0:T(8,128)S(1)} custom-call(s32[4]{0:T(128)S(1)} %pad_add_fusion.place, f32[2,1024,256]{2,1,0:T(8,128)S(1)} %score_own.1.mine, f32[2,1024,256]{2,1,0:T(8,128)S(1)} %collective-permute-done.11.theirs), custom_call_target="tpu_custom_call" | custom-call | tf_op jit(solution)/shard_map/settle/pallas_call | solution.py:48
  56.1 11.0 %all_to_all.10.stats = f32[8,8,128]{2,1,0:T(8,128)S(1)} all-to-all(f32[8,8,128]{2,1,0:T(8,128)S(1)} %settle.1), channel_id=1, replica_groups=mesh['cls'=4,'grp'=4,'y'=4,'zl'=2,'core'=2] {'cls','zl'}, dimensions={0} | all-to-all | bytes 65536 | tf_op jit(solution)/shard_map/all_to_all | solution.py:371
  67.1 1.6 %posterior.1 = (bf16[2,200,1024]{2,1,0:T(8,128)(2,1)S(1)}, f32[8,40]{1,0:T(8,128)S(1)}) custom-call(s32[4]{0:T(128)S(1)} %pad_add_fusion.place, f32[2,1024,256]{2,1,0:T(8,128)S(1)} %score_own.1.mine, f32[2,1024,256]{2,1,0:T(8,128)S(1)} %collective-permute-done.11.theirs, f32[8,8,128]{2,1,0:T(8,128)S(1)} %all_to_all.10.stats, ...), custom_call_target="tpu_custom_call" | custom-call | tf_op jit(solution)/shard_map/posterior/pallas_call | solution.py:266
  69.0 2.3 %collective-permute-done.12.theirs = bf16[2,200,1024]{2,1,0:T(8,128)(2,1)S(1)} collective-permute-done((bf16[2,200,1024]{2,1,0:T(8,128)(2,1)S(1)}, bf16[2,200,1024]{2,1,0:T(8,128)(2,1)S(1)}, u32[]{:S(2)}, u32[]{:S(2)}) %collective-permute-start.12) | collective-permute-done | bytes 819232 | tf_op jit(solution)/shard_map/ppermute | solution.py:373
  71.3 2.5 %insert_far.1 = (bf16[8,208,128]{2,1,0:T(8,128)(2,1)S(1)}, f32[8,128]{1,0:T(8,128)S(1)}) custom-call(s32[4]{0:T(128)S(1)} %pad_add_fusion.place, f32[8,40]{1,0:T(8,128)S(1)} %get-tuple-element.63.after, bf16[2,200,1024]{2,1,0:T(8,128)(2,1)S(1)} %get-tuple-element.64.mine, bf16[2,200,1024]{2,1,0:T(8,128)(2,1)S(1)} %collective-permute-done.12.theirs, ...), custom_call_target="tpu_custom_call" | custom-call | flops 2147483648 | tf_op jit(solution)/shard_map/insert_far/pallas_call | solution.py:48
  73.9 3.1 %collective-permute-start.13 = (bf16[8,208,128]{2,1,0:T(8,128)(2,1)S(1)}, bf16[8,208,128]{2,1,0:T(8,128)(2,1)S(1)}, u32[]{:S(2)}, u32[]{:S(2)}) collective-permute-start(bf16[8,208,128]{2,1,0:T(8,128)(2,1)S(1)} %get-tuple-element.68), channel_id=1, source_target_pairs={{0,32},{16,48},{32,0},{48,16},{1,33},{17,49},{33,1},{49,17},{2,34}... | collective-permute-start | bytes 1277960 | tf_op jit(solution)/shard_map/ppermute | solution.py:326
  77.0 4.3 %insert_near.1 = (bf16[8,208,128]{2,1,0:T(8,128)(2,1)S(1)}, bf16[8,208,128]{2,1,0:T(8,128)(2,1)S(1)}, f32[8,128]{1,0:T(8,128)S(1)}) custom-call(s32[4]{0:T(128)S(1)} %pad_add_fusion.place, f32[8,128]{1,0:T(8,128)S(1)} %get-tuple-element.65.after, bf16[2,200,1024]{2,1,0:T(8,128)(2,1)S(1)} %get-tuple-element.64.mine, ...), custom_call_target="tpu_custom_call" | custom-call | flops 4294967296 | tf_op jit(solution)/shard_map/insert_near/pallas_call | solution.py:48
  82.6 2.9 %insert_own.1 = (f32[8,208,128]{2,1,0:T(8,128)S(1)}, f32[8,128]{1,0:T(8,128)}) custom-call(s32[4]{0:T(128)S(1)} %pad_add_fusion.place, f32[8,128]{1,0:T(8,128)S(1)} %get-tuple-element.66.after, bf16[2,200,1024]{2,1,0:T(8,128)(2,1)S(1)} %get-tuple-element.64.mine, bf16[2,200,1024]{2,1,0:T(8,128)(2,1)S(1)} %collective-permute-done.12.theirs, ...), custom_call_target="tpu_custom_call" | custom-call | flops 2147483648 | tf_op jit(solution)/shard_map/insert_own/pallas_call | solution.py:48
  85.6 2.6 %collective-permute-done.13.far = bf16[8,208,128]{2,1,0:T(8,128)(2,1)S(1)} collective-permute-done((bf16[8,208,128]{2,1,0:T(8,128)(2,1)S(1)}, bf16[8,208,128]{2,1,0:T(8,128)(2,1)S(1)}, u32[]{:S(2)}, u32[]{:S(2)}) %collective-permute-start.13) | collective-permute-done | bytes 426016 | tf_op jit(solution)/shard_map/ppermute | solution.py:326
  88.7 7.8 %collective-permute-done.14.one = bf16[8,208,128]{2,1,0:T(8,128)(2,1)S(1)} collective-permute-done((bf16[8,208,128]{2,1,0:T(8,128)(2,1)S(1)}, bf16[8,208,128]{2,1,0:T(8,128)(2,1)S(1)}, u32[]{:S(2)}, u32[]{:S(2)}) %collective-permute-start.14) | collective-permute-done | bytes 426016 | tf_op jit(solution)/shard_map/ppermute | solution.py:326
  96.6 1.4 %gather.1 = bf16[8,216,128]{2,1,0:T(8,128)(2,1)} custom-call(s32[4]{0:T(128)S(1)} %pad_add_fusion.place, f32[8,208,128]{2,1,0:T(8,128)S(1)} %absorb.1.own, bf16[8,208,128]{2,1,0:T(8,128)(2,1)S(1)} %collective-permute-done.14.one, bf16[8,208,128]{2,1,0:T(8,128)(2,1)S(1)} %collective-permute-done.15.three), custom_call_target="tpu_custom_call" | custom-call | tf_op jit(solution)/shard_map/gather/pallas_call | solution.py:48
  98.0 5.9 %all-to-all-start.1 = ((bf16[8,216,128]{2,1,0:T(8,128)(2,1)}), bf16[8,216,128]{2,1,0:T(8,128)(2,1)S(1)}, u32[]{:S(2)}, u32[]{:S(2)}) async-start(bf16[8,216,128]{2,1,0:T(8,128)(2,1)} %gather.1), calls=%async_computation.1 | async-start | bytes 884736 | tf_op jit(solution)/shard_map/all_to_all | solution.py:391
  104.5 7.6 %all-to-all-done.1.blocks = bf16[8,216,128]{2,1,0:T(8,128)(2,1)S(1)} async-done(((bf16[8,216,128]{2,1,0:T(8,128)(2,1)}), bf16[8,216,128]{2,1,0:T(8,128)(2,1)S(1)}, u32[]{:S(2)}, u32[]{:S(2)}) %all-to-all-start.1) | async-done | bytes 442400 | tf_op jit(solution)/shard_map/all_to_all | solution.py:391
  112.0 1.3 %finish.1 = (f32[2,200,128]{2,1,0:T(8,128)}, f32[2,8,200]{2,1,0:T(8,128)}) custom-call(s32[4]{0:T(128)S(1)} %pad_add_fusion.place, bf16[8,216,128]{2,1,0:T(8,128)(2,1)S(1)} %all-to-all-done.1.blocks), custom_call_target="tpu_custom_call" | custom-call | tf_op jit(solution)/shard_map/finish/pallas_call | solution.py:48
  (41 shorter events, 7.8 us)
Async XLA Ops:
  1.4 4.2 %collective-permute-start = (bf16[1,200,128]{2,1,0:T(8,128)(2,1)S(1)}, bf16[1,200,128]{2,1,0:T(8,128)(2,1)S(1)}, u32[]{:S(2)}, u32[]{:S(2)}) collective-permute-start(bf16[1,200,128]{2,1,0:T(8,128)(2,1)S(1)} %dynamic-slice_bitcast_fusion), channel_id=1, source_target_pairs={{0,2},{2,0},{1,3},{3,1},{4,6},{6,4},{5,7},{7,5},{8,10},{10,8},{9,1... | collective-permute-start | bytes 153608 | tf_op jit(solution)/shard_map/ppermute | solution.py:342
  5.6 14.8 %collective-permute-start.3 = (bf16[2,200,128]{2,1,0:T(8,128)(2,1)S(1)}, bf16[2,200,128]{2,1,0:T(8,128)(2,1)S(1)}, u32[]{:S(2)}, u32[]{:S(2)}) collective-permute-start(bf16[2,200,128]{2,1,0:T(8,128)(2,1)S(1)} %pad_maximum_fusion.unit), channel_id=1, source_target_pairs={{0,12},{4,8},{8,4},{12,0},{1,13},{5,9},{9,5},{13,1},{2,14},{6,10},... | collective-permute-start | bytes 307208 | tf_op jit(solution)/shard_map/ppermute | solution.py:326
  8.7 11.7 %collective-permute-start.2 = (bf16[2,200,128]{2,1,0:T(8,128)(2,1)S(1)}, bf16[2,200,128]{2,1,0:T(8,128)(2,1)S(1)}, u32[]{:S(2)}, u32[]{:S(2)}) collective-permute-start(bf16[2,200,128]{2,1,0:T(8,128)(2,1)S(1)} %pad_maximum_fusion.unit), channel_id=1, source_target_pairs={{0,8},{4,12},{8,0},{12,4},{1,9},{5,13},{9,1},{13,5},{2,10},{6,14},... | collective-permute-start | bytes 307208 | tf_op jit(solution)/shard_map/ppermute | solution.py:326
  9.3 7.1 %collective-permute-start.1 = (bf16[2,200,128]{2,1,0:T(8,128)(2,1)S(1)}, bf16[2,200,128]{2,1,0:T(8,128)(2,1)S(1)}, u32[]{:S(2)}, u32[]{:S(2)}) collective-permute-start(bf16[2,200,128]{2,1,0:T(8,128)(2,1)S(1)} %pad_maximum_fusion.unit), channel_id=1, source_target_pairs={{0,4},{4,0},{8,12},{12,8},{1,5},{5,1},{9,13},{13,9},{2,6},{6,2},{1... | collective-permute-start | bytes 307208 | tf_op jit(solution)/shard_map/ppermute | solution.py:326
  9.8 1.1 copy-start
  10.9 1.0 copy-start.1
  11.9 0.9 copy-start.2
  14.3 13.9 %collective-permute-start.6 = (bf16[40,4224]{1,0:T(8,128)(2,1)S(1)}, bf16[40,4224]{1,0:T(8,128)(2,1)S(1)}, u32[]{:S(2)}, u32[]{:S(2)}) collective-permute-start(bf16[40,4224]{1,0:T(8,128)(2,1)S(1)} %get-tuple-element.43), channel_id=1, source_target_pairs={{0,194},{2,64},{64,2},{66,128},{128,66},{130,192},{192,130},{194,0... | collective-permute-start | bytes 1013768 | tf_op jit(solution)/shard_map/ppermute | solution.py:350
  16.4 12.5 %collective-permute-start.4 = (bf16[40,4224]{1,0:T(8,128)(2,1)S(1)}, bf16[40,4224]{1,0:T(8,128)(2,1)S(1)}, u32[]{:S(2)}, u32[]{:S(2)}) collective-permute-start(bf16[40,4224]{1,0:T(8,128)(2,1)S(1)} %get-tuple-element.43), channel_id=1, source_target_pairs={{0,1},{1,0},{2,3},{3,2},{4,5},{5,4},{6,7},{7,6},{8,9},{9,8},{10,11... | collective-permute-start | bytes 1013768 | tf_op jit(solution)/shard_map/ppermute | solution.py:346
  16.4 16.6 %collective-permute-start.5 = (bf16[40,4224]{1,0:T(8,128)(2,1)S(1)}, bf16[40,4224]{1,0:T(8,128)(2,1)S(1)}, u32[]{:S(2)}, u32[]{:S(2)}) collective-permute-start(bf16[40,4224]{1,0:T(8,128)(2,1)S(1)} %get-tuple-element.39.images), channel_id=1, source_target_pairs={{0,2},{2,0},{1,3},{3,1},{4,6},{6,4},{5,7},{7,5},{8,10},{10,8},{9,1... | collective-permute-start | bytes 1013768 | tf_op jit(solution)/shard_map/ppermute | solution.py:349
  20.5 21.7 %collective-permute-start.10 = (bf16[8,200,128]{2,1,0:T(8,128)(2,1)S(1)}, bf16[8,200,128]{2,1,0:T(8,128)(2,1)S(1)}, u32[]{:S(2)}, u32[]{:S(2)}) collective-permute-start(bf16[8,200,128]{2,1,0:T(8,128)(2,1)S(1)} %constant_dynamic-update-slice_fusion.after.p0), channel_id=1, source_target_pairs={{0,48},{16,32},{32,16},{48,0},{1,49},{17,33},{33,17},{49,1},{2,50}... | collective-permute-start | bytes 1228808 | tf_op jit(solution)/shard_map/ppermute | solution.py:326
  23.3 18.8 %collective-permute-start.9 = (bf16[8,200,128]{2,1,0:T(8,128)(2,1)S(1)}, bf16[8,200,128]{2,1,0:T(8,128)(2,1)S(1)}, u32[]{:S(2)}, u32[]{:S(2)}) collective-permute-start(bf16[8,200,128]{2,1,0:T(8,128)(2,1)S(1)} %constant_dynamic-update-slice_fusion.after.p0), channel_id=1, source_target_pairs={{0,32},{16,48},{32,0},{48,16},{1,33},{17,49},{33,1},{49,17},{2,34}... | collective-permute-start | bytes 1228808 | tf_op jit(solution)/shard_map/ppermute | solution.py:326
  28.2 14.6 %collective-permute-start.8 = (bf16[8,200,128]{2,1,0:T(8,128)(2,1)S(1)}, bf16[8,200,128]{2,1,0:T(8,128)(2,1)S(1)}, u32[]{:S(2)}, u32[]{:S(2)}) collective-permute-start(bf16[8,200,128]{2,1,0:T(8,128)(2,1)S(1)} %constant_dynamic-update-slice_fusion.after.p0), channel_id=1, source_target_pairs={{0,16},{16,0},{32,48},{48,32},{1,17},{17,1},{33,49},{49,33},{2,18}... | collective-permute-start | bytes 1228808 | tf_op jit(solution)/shard_map/ppermute | solution.py:326
  28.8 8.2 %collective-permute-start.7 = (bf16[40,4224]{1,0:T(8,128)(2,1)S(1)}, bf16[40,4224]{1,0:T(8,128)(2,1)S(1)}, u32[]{:S(2)}, u32[]{:S(2)}) collective-permute-start(bf16[40,4224]{1,0:T(8,128)(2,1)S(1)} %collective-permute-done.6), channel_id=1, source_target_pairs={{0,1},{1,0},{2,3},{3,2},{4,5},{5,4},{6,7},{7,6},{8,9},{9,8},{10,11... | collective-permute-start | bytes 1013768 | tf_op jit(solution)/shard_map/ppermute | solution.py:351
  49.6 5.3 %collective-permute-start.11 = (f32[2,1024,256]{2,1,0:T(8,128)S(1)}, f32[2,1024,256]{2,1,0:T(8,128)S(1)}, u32[]{:S(2)}, u32[]{:S(2)}) collective-permute-start(f32[2,1024,256]{2,1,0:T(8,128)S(1)} %score_given.1), channel_id=1, source_target_pairs={{0,1},{1,0},{2,3},{3,2},{4,5},{5,4},{6,7},{7,6},{8,9},{9,8},{10,11... | collective-permute-start | bytes 6291464 | tf_op jit(solution)/shard_map/ppermute | solution.py:368
  68.7 2.6 %collective-permute-start.12 = (bf16[2,200,1024]{2,1,0:T(8,128)(2,1)S(1)}, bf16[2,200,1024]{2,1,0:T(8,128)(2,1)S(1)}, u32[]{:S(2)}, u32[]{:S(2)}) collective-permute-start(bf16[2,200,1024]{2,1,0:T(8,128)(2,1)S(1)} %get-tuple-element.64.mine), channel_id=1, source_target_pairs={{0,1},{1,0},{2,3},{3,2},{4,5},{5,4},{6,7},{7,6},{8,9},{9,8},{10,11... | collective-permute-start | bytes 2457608 | tf_op jit(solution)/shard_map/ppermute | solution.py:373
  73.9 14.3 %collective-permute-start.13 = (bf16[8,208,128]{2,1,0:T(8,128)(2,1)S(1)}, bf16[8,208,128]{2,1,0:T(8,128)(2,1)S(1)}, u32[]{:S(2)}, u32[]{:S(2)}) collective-permute-start(bf16[8,208,128]{2,1,0:T(8,128)(2,1)S(1)} %get-tuple-element.68), channel_id=1, source_target_pairs={{0,32},{16,48},{32,0},{48,16},{1,33},{17,49},{33,1},{49,17},{2,34}... | collective-permute-start | bytes 1277960 | tf_op jit(solution)/shard_map/ppermute | solution.py:326
  81.3 15.3 %collective-permute-start.14 = (bf16[8,208,128]{2,1,0:T(8,128)(2,1)S(1)}, bf16[8,208,128]{2,1,0:T(8,128)(2,1)S(1)}, u32[]{:S(2)}, u32[]{:S(2)}) collective-permute-start(bf16[8,208,128]{2,1,0:T(8,128)(2,1)S(1)} %get-tuple-element.69), channel_id=1, source_target_pairs={{0,16},{16,0},{32,48},{48,32},{1,17},{17,1},{33,49},{49,33},{2,18}... | collective-permute-start | bytes 1277960 | tf_op jit(solution)/shard_map/ppermute | solution.py:326
  82.0 14.6 %collective-permute-start.15 = (bf16[8,208,128]{2,1,0:T(8,128)(2,1)S(1)}, bf16[8,208,128]{2,1,0:T(8,128)(2,1)S(1)}, u32[]{:S(2)}, u32[]{:S(2)}) collective-permute-start(bf16[8,208,128]{2,1,0:T(8,128)(2,1)S(1)} %get-tuple-element.70), channel_id=1, source_target_pairs={{0,48},{16,32},{32,16},{48,0},{1,49},{17,33},{33,17},{49,1},{2,50}... | collective-permute-start | bytes 1277960 | tf_op jit(solution)/shard_map/ppermute | solution.py:326
  98.0 14.0 %all-to-all-start.1 = ((bf16[8,216,128]{2,1,0:T(8,128)(2,1)}), bf16[8,216,128]{2,1,0:T(8,128)(2,1)S(1)}, u32[]{:S(2)}, u32[]{:S(2)}) async-start(bf16[8,216,128]{2,1,0:T(8,128)(2,1)} %gather.1), calls=%async_computation.1 | async-start | bytes 884736 | tf_op jit(solution)/shard_map/all_to_all | solution.py:391

commit v2 on v1

v2 whole, which is shorter than its diff:
```python
import math

import jax
import jax.numpy as jnp
import numpy as np
from jax import lax
from jax.experimental import pallas as pl
from jax.experimental.pallas import tpu as pltpu
from jax.sharding import Mesh, PartitionSpec as P

IMG = 64
SIDE = 5
SHIFTS = SIDE * SIDE
HALF = SHIFTS // 2
GROUPS = 8
FREQS = IMG * IMG
LANE = 128
SLOTS = 40
ROWS = 1024
WIDTH = 200
WIDE = 256
TALL = WIDTH + 16
COUNTED = SLOTS * SHIFTS
BLOCKS = 32
DEPTH = BLOCKS * LANE
CHUNK = DEPTH // 8
HIGHEST = lax.Precision.HIGHEST
F32 = jnp.float32
BF16 = jnp.bfloat16
MIB = 2**20
LIMIT = 4
VMEM = pl.BlockSpec(memory_space=pltpu.VMEM)
SMEM = pl.BlockSpec(memory_space=pltpu.SMEM)
SWAP = [(0, 1), (1, 0)]


def shift_tables():
    index = np.arange(FREQS)
    shift = np.arange(HALF)
    offx = shift // SIDE - SIDE // 2
    offy = shift % SIDE - SIDE // 2
    phase = (offx[:, None] * (index // IMG)[None, :] + offy[:, None] * (index % IMG)[None, :]) % IMG
    theta = (phase.astype(np.float32) * np.float32(2.0 * math.pi / IMG)).astype(np.float64)
    return np.cos(theta).astype(np.float32), np.sin(theta).astype(np.float32)


def call(kernel, name, out, args, limit, flops=0, moved=0):
    return pl.pallas_call(
        kernel,
        name=name,
        in_specs=[SMEM] + [VMEM] * (len(args) - 1),
        out_specs=jax.tree.map(lambda _: VMEM, out),
        out_shape=out,
        cost_estimate=pl.CostEstimate(flops=flops, bytes_accessed=moved, transcendentals=0),
        compiler_params=pltpu.CompilerParams(vmem_limit_bytes=limit * MIB),
    )(*args)


def shape(*dims, dtype=F32):
    return jax.ShapeDtypeStruct(dims, dtype)


def lanes(block):
    return pl.ds(pl.multiple_of(block * LANE, LANE), LANE)


def cut(value):
    first = value.astype(BF16)
    rest = value - first.astype(F32)
    second = rest.astype(BF16)
    return first, second, (rest - second.astype(F32)).astype(BF16)


def spread_kernel(stacks, out, held, sem):
    copy = pltpu.make_async_copy(stacks, held, sem)
    copy.start()
    copy.wait()
    for n in range(8):
        out[n] = held[n % 2]


def spread_call(stacks):
    return pl.pallas_call(
        spread_kernel,
        name="spread",
        in_specs=[pl.BlockSpec(memory_space=pltpu.HBM)],
        out_specs=VMEM,
        out_shape=shape(8, WIDTH, LANE, dtype=BF16),
        scratch_shapes=[pltpu.VMEM((2, WIDTH, LANE), BF16), pltpu.SemaphoreType.DMA],
        compiler_params=pltpu.CompilerParams(vmem_limit_bytes=LIMIT * MIB),
    )(pltpu.with_memory_space_constraint(stacks, pltpu.HBM))


def split_kernel(place, groups, count, images, ctf, tables, kept, given, parts, turns, held, images_in, ctf_in, sems):
    core = place[3]
    copies = [
        pltpu.make_async_copy(source, target, sems.at[i])
        for i, (source, target) in enumerate(((images, images_in), (ctf, ctf_in), (tables, turns)))
    ]
    for copy in copies:
        copy.start()
    copies[1].wait()
    held[...] = ctf_in[...]
    for i, part in enumerate(cut(ctf_in[...])):
        parts[16 * i : 16 * i + 16, :] = jnp.concatenate([part.astype(F32), jnp.zeros((8, FREQS), F32)], axis=0).astype(BF16)
    copies[0].wait()

    def turn(j, carry):
        kept[:, lanes(j)] = images_in[:, lanes(2 * j + core)]
        given[:, lanes(j)] = images_in[:, lanes(2 * j + 1 - core)]
        return carry

    lax.fori_loop(0, BLOCKS, turn, 0)
    row = lax.broadcasted_iota(jnp.int32, (SLOTS, LANE), 0)
    lane = lax.broadcasted_iota(jnp.int32, (SLOTS, LANE), 1)
    group = jnp.zeros((SLOTS, LANE), jnp.int32)
    for i in range(SLOTS):
        group = jnp.where(row == i, groups[i], group)
    live = jnp.where(row < count[0], 1, 0)
    meta = jnp.where(lane == 0, group, jnp.where(lane == 1, live, 0)).astype(F32).astype(BF16)
    kept[:, DEPTH:] = meta
    given[:, DEPTH:] = meta
    copies[2].wait()


def split_call(place, groups, count, images, ctf, tables):
    half = shape(SLOTS, DEPTH + LANE, dtype=BF16)
    anywhere = pl.BlockSpec(memory_space=pltpu.HBM)
    return pl.pallas_call(
        split_kernel,
        name="split",
        in_specs=[SMEM, SMEM, SMEM, anywhere, anywhere, anywhere],
        out_specs=[VMEM] * 5,
        out_shape=[half, half, shape(48, FREQS, dtype=BF16), shape(2 * HALF, FREQS), shape(GROUPS, FREQS)],
        scratch_shapes=[
            pltpu.VMEM((SLOTS, 2 * DEPTH), BF16),
            pltpu.VMEM((GROUPS, FREQS), F32),
            pltpu.SemaphoreType.DMA((3,)),
        ],
        compiler_params=pltpu.CompilerParams(vmem_limit_bytes=LIMIT * MIB),
    )(place, groups, count, *(pltpu.with_memory_space_constraint(v, pltpu.HBM) for v in (images, ctf, tables)))


def owner_block(place, p):
    later, first, second = p // 16, p % 16 // 4, p % 4
    across = jnp.where(later == 0, first, second)
    along = jnp.where(later == 0, second, place[1] ^ first)
    return (place[0] ^ across) * 8 + along * 2 + later


def build_kernel(place, after, images_a, images_b, parts, turns, *refs):
    outs, (token, rows) = refs[:8], refs[8:]
    core = place[3]
    lane = lax.broadcasted_iota(jnp.int32, (SLOTS, 48), 1)

    def member(k, carry):
        def read(at):
            return jnp.where(k == 0, images_a[:, at].astype(F32), images_b[:, at].astype(F32))

        group = read(slice(DEPTH, DEPTH + LANE))[:, :1]
        hot = jnp.where((group == (lane % 16).astype(F32)) & (lane % 16 < GROUPS), 1.0, 0.0).astype(BF16)
        rows[...] = jnp.dot(hot, parts[...], preferred_element_type=F32)
        for t, out in enumerate(outs):

            def turn(p, carry):
                j = owner_block(place, 4 * t + p)
                at = lanes(2 * (j % 16) + core)
                sign = jnp.where(j < 16, 1.0, -1.0).astype(F32)
                row = rows[:, at]
                first = read(lanes(j)) * row
                second = read(lanes(j ^ 16)) * (row * sign)
                here = lanes(p)
                for s in range(HALF):
                    a = first * turns[s : s + 1, at]
                    b = second * turns[HALF + s : HALF + s + 1, at]
                    pair = jnp.concatenate([a + b, a - b], axis=0).astype(BF16)
                    out[k, 2 * SLOTS * s : 2 * SLOTS * (s + 1), here] = pair
                tail = jnp.concatenate([first, jnp.zeros((ROWS - SLOTS * SHIFTS, LANE), F32)], axis=0)
                out[k, 2 * SLOTS * HALF : ROWS, here] = tail.astype(BF16)
                return carry

            lax.fori_loop(0, 4, turn, 0, unroll=4)
        return carry

    lax.fori_loop(0, 2, member, 0)
    token[...] = jnp.zeros_like(token)


def build_call(place, after, images_a, images_b, parts, turns, name, flops):
    return pl.pallas_call(
        build_kernel,
        name=name,
        in_specs=[SMEM] + [VMEM] * 5,
        out_specs=[VMEM] * 9,
        out_shape=[shape(2, ROWS, CHUNK, dtype=BF16)] * 8 + [shape(8, WIDE)],
        scratch_shapes=[pltpu.VMEM((SLOTS, FREQS), F32)],
        cost_estimate=pl.CostEstimate(flops=flops, bytes_accessed=10**5, transcendentals=0),
        compiler_params=pltpu.CompilerParams(vmem_limit_bytes=LIMIT * MIB),
    )(place, after, images_a, images_b, parts, turns)


def hot_rows(meta):
    group = meta[:, DEPTH : DEPTH + 1].astype(F32)
    lane = lax.broadcasted_iota(jnp.int32, (SLOTS, GROUPS), 1).astype(F32)
    return jnp.where(group == lane, 1.0, 0.0).astype(F32)


def stack_of(piece):
    return jnp.concatenate([piece[r] for r in range(8)], axis=1)


def weigh_kernel(chunks):
    def kernel(place, ctf, after, *refs):
        pieces, power = refs[:-1], refs[-1]
        core = place[3]
        total = jnp.zeros((3 * GROUPS, WIDTH), F32)
        for q, piece in zip(chunks, pieces):
            left = jnp.concatenate([ctf[:, lanes(2 * (((place[0] ^ q) * 8 + r) % 16) + core)] for r in range(8)], axis=1)
            parts = jnp.concatenate([part.astype(F32) for part in cut(left * left)], axis=0).astype(BF16)
            square = stack_of(piece).astype(F32)
            square = square * square
            high = square.astype(BF16)
            low = (square - high.astype(F32)).astype(BF16)
            dims = (((1,), (1,)), ((), ()))
            total = total + lax.dot_general(parts, high, dims, preferred_element_type=F32)
            total = total + lax.dot_general(parts, low, dims, preferred_element_type=F32)
        power[...] = after[:, :WIDTH] + total[:GROUPS] + total[GROUPS : 2 * GROUPS] + total[2 * GROUPS :]

    return kernel


def score_kernel(member):
    def kernel(place, power, meta_a, meta_b, *refs):
        pieces, out = refs[:4], refs[20]
        for k, meta in enumerate((meta_a, meta_b)):
            half = 0.5 * jnp.dot(hot_rows(meta), power[...], precision=HIGHEST, preferred_element_type=F32)
            sums = None
            for t in range(4):
                weights = [pieces[t][2 * n] for n in range(4)] + [pieces[n][2 * (place[1] ^ t) + 1] for n in range(4)]
                shifted = jnp.concatenate([refs[4 + 8 * k + t][member], refs[8 + 8 * k + t][member]], axis=1)
                part = lax.dot_general(
                    shifted, jnp.concatenate(weights, axis=1), (((1,), (1,)), ((), ())), preferred_element_type=F32
                )
                sums = part if sums is None else sums + part
            spare = jnp.zeros((ROWS - SLOTS * SHIFTS, WIDTH), F32)
            out[k, :, :WIDTH] = sums - jnp.concatenate([half] * SHIFTS + [spare], axis=0)

    return kernel


def settle_kernel(place, mine, theirs, stats):
    columns = []
    for k in range(2):

        def value(s):
            at = slice(SLOTS * s, SLOTS * (s + 1))
            return mine[k, at, :WIDTH] + theirs[k, at, :WIDTH]

        best = value(0)
        for s in range(1, SHIFTS):
            best = jnp.maximum(best, value(s))
        top = jnp.max(best, axis=1, keepdims=True)
        total = jnp.exp(value(0) - top)
        for s in range(1, SHIFTS):
            total = total + jnp.exp(value(s) - top)
        columns += [top, jnp.sum(total, axis=1, keepdims=True)]
    lane = lax.broadcasted_iota(jnp.int32, (SLOTS, LANE), 1)
    spread = jnp.where(lane == 0, columns[0], jnp.where(lane == 1, columns[1], jnp.where(lane == 2, columns[2], columns[3])))
    spread = jnp.concatenate([spread, jnp.zeros((LANE - SLOTS, LANE), F32)], axis=0).T[:8, :]
    for d in range(8):
        stats[d] = spread


def posterior_kernel(place, mine, theirs, stats, meta_a, meta_b, low, evidence, spare):
    parity = place[2]
    counted = jnp.zeros((GROUPS, WIDTH), F32)
    for k, meta in ((1, meta_b), (0, meta_a)):
        tops, totals = [], []
        for d in range(8):
            same = (parity == d % 2) == (k == 0)
            here = stats[d, :, :SLOTS]
            tops.append(jnp.where(same, here[0:1], here[2:3]))
            totals.append(jnp.where(same, here[1:2], here[3:4]))
        tops = jnp.concatenate(tops, axis=0)
        totals = jnp.concatenate(totals, axis=0)
        top = jnp.max(tops, axis=0, keepdims=True)
        total = jnp.sum(totals * jnp.exp(tops - top), axis=0, keepdims=True)
        row = lax.broadcasted_iota(jnp.int32, (8, SLOTS), 0)
        columns = jnp.where(row == 0, top, jnp.where(row == 1, total, top + jnp.log(total))).T
        live = meta[:, DEPTH + 1 : DEPTH + 2].astype(F32)
        scale = live / columns[:, 1:2]
        if k == 0:
            known = jnp.where(live > 0.0, columns[:, 2:3], 0.0)
            evidence[...] = jnp.broadcast_to(known, (SLOTS, LANE)).T[:8, :]
        gathered = None
        for s in range(SHIFTS):
            at = slice(SLOTS * s, SLOTS * (s + 1))
            value = jnp.exp(mine[k, at, :WIDTH] + theirs[k, at, :WIDTH] - columns[:, 0:1]) * scale
            spare[at, :] = value
            gathered = value if gathered is None else gathered + value
        hot = hot_rows(meta)
        counted = counted + lax.dot_general(
            hot, gathered, (((0,), (0,)), ((), ())), precision=HIGHEST, preferred_element_type=F32
        )
        spare[SLOTS * SHIFTS :, :] = jnp.zeros((ROWS - SLOTS * SHIFTS, WIDTH), F32)
        if k == 0:
            first = counted.astype(BF16).astype(F32)
            spare[COUNTED : COUNTED + GROUPS, :] = first
            spare[COUNTED + GROUPS : COUNTED + 2 * GROUPS, :] = counted - first
        low[k] = spare[...].T.astype(BF16)


def posterior_call(*args):
    out = [shape(2, WIDTH, ROWS, dtype=BF16), shape(8, SLOTS)]
    return pl.pallas_call(
        posterior_kernel,
        name="posterior",
        in_specs=[SMEM] + [VMEM] * (len(args) - 1),
        out_specs=[VMEM] * 2,
        out_shape=out,
        scratch_shapes=[pltpu.VMEM((ROWS, WIDTH), F32)],
        compiler_params=pltpu.CompilerParams(vmem_limit_bytes=LIMIT * MIB),
    )(*args)


def block_sums(low, groups, put):
    for n in (0, 2):
        at = slice(LANE * n, LANE * (n + 2))
        sums = jnp.dot(low, jnp.concatenate([g[:, at] for g in groups], axis=0), preferred_element_type=F32)
        for r in range(2):
            put(n + r, sums[:, r * LANE : (r + 1) * LANE])


def own_kernel(place, mine, a0, a1, b0, b1, out_a, out_b):
    low = jnp.concatenate([mine[0], mine[1]], axis=1)
    for groups, out in (((a0.at[0], a1.at[0]), out_a), ((b0.at[0], b1.at[0]), out_b)):

        def put(n, value):
            out[n] = value

        block_sums(low, groups, put)


def insert_kernel(chunks, begun=False):
    def kernel(place, after, mine, theirs, *refs):
        starts, refs = (refs[:2], refs[2:]) if begun else ((None, None), refs)
        members = (1,) if begun else (0, 1)
        shifted, outs = refs[: 4 * chunks], refs[4 * chunks :]
        lows = [theirs[0], theirs[1]] if begun else [mine[0], theirs[0], mine[1], theirs[1]]
        low = jnp.concatenate(lows, axis=1)
        tail = slice(ROWS - LANE, ROWS)
        first = COUNTED - ROWS + LANE
        both = (mine[0, :, tail].astype(F32) + theirs[0, :, tail].astype(F32)).T
        both = both[first : first + GROUPS] + both[first + GROUPS : first + 2 * GROUPS]
        both = jnp.concatenate([both, jnp.zeros((GROUPS, WIDE - WIDTH), F32)], axis=1)
        both = jnp.concatenate([both[:, :LANE], both[:, LANE:]], axis=0)
        outs[-1][...] = jnp.zeros((8, LANE), F32)
        for i, out in enumerate(outs[:-1]):
            start = starts[i % 2]

            def put(n, value):
                if start is not None:
                    value = value + start[n]
                out[n, :WIDTH, :] = value.astype(out.dtype)

            block_sums(low, [pair.at[k] for pair in shifted[2 * i : 2 * i + 2] for k in members], put)
            if i % 2 == 0:
                for n in range(4):
                    out[n, WIDTH:, :] = both.astype(out.dtype)

    return kernel


def absorb_kernel(place, own_a, own_b, far_a, far_b, out_a, out_b):
    out_a[...] = own_a[...] + far_a[...].astype(F32)
    out_b[...] = own_b[...] + far_b[...].astype(F32)


def gather_kernel(place, own_a, own_b, one_a, one_b, three_a, three_b, kept_a, kept_b, sent_a, sent_b):
    y = place[1]
    for out, planes in ((kept_a, (y, y ^ 3)), (sent_a, (y ^ 1, y ^ 2))):
        for i, n in enumerate(planes):
            out[i] = (own_a[n] + one_a[n].astype(F32) + three_a[n].astype(F32)).astype(out.dtype)
    for out, planes in ((kept_b, (0, 3)), (sent_b, (1, 2))):
        for i, n in enumerate(planes):
            out[i] = (own_b[n] + one_b[n].astype(F32) + three_b[n].astype(F32)).astype(out.dtype)


def middle_kernel(place, kept_a, kept_b, got_a, got_b, out_a, out_b, sent_a, sent_b):
    for kept, got, out, sent in ((kept_a, got_a, out_a, sent_a), (kept_b, got_b, out_b, sent_b)):
        out[...] = kept[0] + got[0].astype(F32)
        sent[...] = (kept[1] + got[1].astype(F32)).astype(BF16)


def part_kernel(place, kept_a, kept_b, got_a, got_b, stay, leave):
    even = kept_a[...] + got_a[...].astype(F32)
    odd = kept_b[...] + got_b[...].astype(F32)
    stay[WIDTH:] = even[WIDTH:]
    leave[WIDTH:] = even[WIDTH:].astype(BF16)
    stay[:WIDTH] = jnp.where(place[2] == 0, even[:WIDTH], odd)
    leave[:WIDTH] = jnp.where(place[2] == 0, odd, even[:WIDTH]).astype(BF16)


def finish_kernel(place, stay, came, insertions, weights):
    for k, sums in ((place[2], stay[...]), (1 - place[2], came[...].astype(F32))):
        insertions[k] = sums[:WIDTH]
        weights[k] = jnp.concatenate([sums[WIDTH : WIDTH + GROUPS], sums[WIDTH + GROUPS :]], axis=1)[:, :WIDTH]


def swap(value, axis, d, n=4):
    return lax.ppermute(value, axis, [(i, i ^ d) for i in range(n)])


def body(particle_images, particle_groups, live_counts, ctf_table, projections):
    x, y, zl, core = (lax.axis_index(a) for a in ("grp", "y", "zl", "core"))
    place = jnp.stack([x, y, zl, core]).astype(jnp.int32)
    ring = ("cls", "zl")

    stacks = jnp.transpose(projections, (1, 2, 0))
    column = lax.all_to_all(spread_call(stacks), ("y", "zl"), 0, 0, tiled=True)

    tables = np.concatenate(shift_tables())
    kept, other, parts, turns, ctf = split_call(place, particle_groups, live_counts, particle_images, ctf_table, jnp.asarray(tables))
    halves = [kept, lax.ppermute(other, "core", SWAP)]

    column, to_pair, to_next = lax.optimization_barrier((column, kept, other))
    next_kept = lax.ppermute(to_pair, "zl", SWAP)
    next_other = lax.ppermute(to_next, ring, [(i, (i + 1) % 8 if i % 2 else (i + 7) % 8) for i in range(8)])
    pieces = [column] + [swap(column, "grp", d) for d in (1, 2, 3)]

    built = [build_call(place, column, halves[0], halves[1], parts, turns, "build_here", 6 * 10**9)]
    next_kept, next_other, _ = lax.optimization_barrier((next_kept, next_other, built[0][8]))
    halves += [next_kept, lax.ppermute(next_other, "core", SWAP)]
    built += [build_call(place, column, halves[2], halves[3], parts, turns, "build_next", 10**8)]
    shifted = [b[:8] for b in built]
    tokens = [b[8] for b in built]
    power = call(weigh_kernel((0,)), "weigh_own", shape(GROUPS, WIDTH), (place, ctf, tokens[0], column), LIMIT, 10**8)
    power = call(weigh_kernel((1, 2, 3)), "weigh", shape(GROUPS, WIDTH), (place, ctf, power, *pieces[1:], *tokens[1:]), LIMIT)
    score = shape(2, ROWS, WIDE)
    flops = 4 * ROWS * WIDE * DEPTH
    given = call(score_kernel(1), "score_given", score, (place, power, halves[1], halves[3], *pieces, *shifted[0], *shifted[1]), LIMIT, flops)
    taken = lax.ppermute(given, "core", SWAP)
    kept_score = call(score_kernel(0), "score_own", score, (place, power, halves[0], halves[2], *pieces, *shifted[0], *shifted[1]), LIMIT, flops)
    stats = call(settle_kernel, "settle", shape(8, 8, LANE), (place, kept_score, taken), LIMIT)
    stats = lax.all_to_all(stats, ring, 0, 0, tiled=True)
    low, evidence = posterior_call(place, kept_score, taken, stats, halves[0], halves[2])
    other_low = lax.ppermute(low, "core", SWAP)

    flops = 2 * 4 * ROWS * WIDE * 1024
    token = shape(8, LANE)

    def block(kind):
        return [shape(4, TALL, LANE, dtype=kind), shape(4, WIDTH, LANE, dtype=kind)]

    def columns(chunk):
        return [pair[part + chunk] for part in (0, 4) for pair in shifted]

    begun = call(own_kernel, "insert_begin", [shape(4, WIDTH, LANE)] * 2, (place, low, *columns(2)), LIMIT, flops // 2)
    *send, after = call(
        insert_kernel(1, True), "insert_far", [*block(BF16), token], (place, evidence, low, other_low, *begun, *columns(2)), LIMIT, flops // 2
    )
    far = [swap(send[0], "grp", 2), swap(send[1], "y", 2)]
    *send, after = call(
        insert_kernel(2),
        "insert_near",
        [*block(BF16), *block(BF16), token],
        (place, after, low, other_low, *columns(1), *columns(3)),
        LIMIT,
        2 * flops,
    )
    near = [swap(send[0], "grp", 1), swap(send[1], "y", 1), swap(send[2], "grp", 3), swap(send[3], "y", 3)]
    *own, _ = call(insert_kernel(1), "insert_own", [*block(F32), token], (place, after, low, other_low, *columns(0)), LIMIT, flops)
    own = call(absorb_kernel, "absorb", block(F32), (place, *own, *far), LIMIT)
    tall, wide = (TALL, LANE), (WIDTH, LANE)
    out = [shape(2, *tall), shape(2, *wide), shape(2, *tall, dtype=BF16), shape(2, *wide, dtype=BF16)]
    *kept, send_a, send_b = call(gather_kernel, "gather", out, (place, *own, *near), LIMIT)
    out = [shape(*tall), shape(*wide), shape(*tall, dtype=BF16), shape(*wide, dtype=BF16)]
    *kept, send_a, send_b = call(middle_kernel, "middle", out, (place, *kept, swap(send_a, "y", 1), swap(send_b, "grp", 1)), LIMIT)
    out = [shape(*tall), shape(*tall, dtype=BF16)]
    stay, leave = call(part_kernel, "part", out, (place, *kept, swap(send_a, "y", 3), swap(send_b, "grp", 3)), LIMIT)
    came = lax.ppermute(leave, "zl", SWAP)
    insertions, tally = call(finish_kernel, "finish", [shape(2, WIDTH, LANE), shape(2, GROUPS, WIDTH)], (place, stay, came), LIMIT)
    return insertions, tally, evidence[0]


def solution(mesh):
    fine = Mesh(mesh.devices.reshape(4, 4, 4, 2, 2), ("cls", "grp", "y", "zl", "core"))
    shards = ("grp", "y", "zl", "core")
    return jax.shard_map(
        body,
        mesh=fine,
        in_specs=(P(shards, None), P(shards), P(shards), P(), P(shards, "cls", None)),
        out_specs=(P("cls", None, shards), P("cls", None, None), P(shards)),
        check_vma=False,
    )
```

time: 115 us -> 112 us (0.974)
  blocking collectives: 11 us -> 15.4 us
  local copies, waits for them, and re-layouts: 5.21 us -> 1.17 us
  Pallas kernels: 45.6 us -> 43.6 us
    all_to_all x1, blocking collectives: 11 us -> 15.4 us  [body(): stats = lax.all_to_all(stats, ring, 0, 0, tiled=True)]
    pallas_call x5 -> x4, Pallas kernels: 17.8 us -> 13.8 us  [the longest x2 10.1 us: build_call(): pl.pallas_call(build_kernel, name=name, in_specs=[SMEM] + [VMEM] * 5, out...]
    ppermute x9 -> x13, starting transfers between devices: 12.9 us -> 16.5 us  [swap(): return lax.ppermute(value, axis, [(i, i ^ d) for i in range(n)])]
    all_to_all x1, waiting for transfers between devices: 7.55 us -> 4.15 us  [body(): column = lax.all_to_all(spread_call(stacks), ('y', 'zl'), 0, 0, tiled=True)]
    unnamed x10 -> x2, local copies, waits for them, and re-layouts: 3.85 us -> 0.66 us
    ppermute x3, starting transfers between devices: 7.93 us -> 5.38 us  [the longest x1 2.67 us: body(): lax.ppermute(to_next, ring, [(i, (i + 1) % 8 if i % 2 else (i + 7) % 8) f...]
    ppermute x3, waiting for transfers between devices: 0.01 us -> 2.43 us  [the longest x1 2.18 us: body(): came = lax.ppermute(leave, 'zl', SWAP)]
    pallas_call x10 -> x14, Pallas kernels: 26.2 us -> 28.1 us  [call(): pl.pallas_call(kernel, name=name, in_specs=[SMEM] + [VMEM] * (len(args) -...]
  transfers between devices with their start and end apart: 17 -> 21, of which waited for: 6 -> 10; matrix products, arithmetic and copies ran while one was open for 2% -> 1% of each run, Pallas kernels for 27% -> 25%
where the time goes in v2:
time: 112 us; the launch traced here: 111 us
  Pallas kernels  43.6 us (39%)
  starting transfers between devices  28.3 us (25%)
  waiting for transfers between devices  21 us (19%)
  blocking collectives  15.4 us (14%)
  between operations  1.49 us (1%)
  local copies, waits for them, and re-layouts  1.17 us (1%)
    pallas_call x14, Pallas kernels, call(): pl.pallas_call(kernel, name=name, in_specs=[SMEM] + [VMEM] * (len(args) -...  28.1 us
    ppermute x13, starting transfers between devices, swap(): return lax.ppermute(value, axis, [(i, i ^ d) for i in range(n)])  16.5 us
    all_to_all x1, blocking collectives, body(): stats = lax.all_to_all(stats, ring, 0, 0, tiled=True)  15.4 us
    ppermute x13, waiting for transfers between devices, swap(): return lax.ppermute(value, axis, [(i, i ^ d) for i in range(n)])  13 us
    pallas_call x2, Pallas kernels, build_call(): pl.pallas_call(build_kernel, name=name, in_specs=[SMEM] + [VMEM] * 5, out...  10.1 us
    all_to_all x1, starting transfers between devices, body(): column = lax.all_to_all(spread_call(stacks), ('y', 'zl'), 0, 0, tiled=True)  5.94 us
    all_to_all x1, waiting for transfers between devices, body(): column = lax.all_to_all(spread_call(stacks), ('y', 'zl'), 0, 0, tiled=True)  4.15 us
    ppermute x1, starting transfers between devices, body(): lax.ppermute(to_next, ring, [(i, (i + 1) % 8 if i % 2 else (i + 7) % 8) f...  2.67 us
  transfers between devices with their start and end apart: 21, of which 10 were waited for; matrix products, arithmetic and copies ran while one was open for 1% of the time, Pallas kernels for 25%

profile of v2, /device:TPU:32, one launch (start us, length us, event | category | flops | bytes accessed | tf_op | source)
XLA Modules:
  0.0 111.0 jit_solution(14965721148640626594)
XLA Ops:
  0.6 1.7 %spread.1 = bf16[8,200,128]{2,1,0:T(8,128)(2,1)} custom-call(bf16[2,200,128]{2,1,0:T(8,128)(2,1)} %bitcast.7), custom_call_target="tpu_custom_call" | custom-call | tf_op jit(solution)/shard_map/spread/pallas_call | solution.py:83
  2.3 5.9 %all-to-all-start = ((bf16[8,200,128]{2,1,0:T(8,128)(2,1)}), bf16[8,200,128]{2,1,0:T(8,128)(2,1)S(1)}, u32[]{:S(2)}, u32[]{:S(2)}) async-start(bf16[8,200,128]{2,1,0:T(8,128)(2,1)} %spread.1), calls=%async_computation | async-start | bytes 819200 | tf_op jit(solution)/shard_map/all_to_all | solution.py:420
  9.7 2.0 %split.1 = (bf16[40,4224]{1,0:T(8,128)(2,1)S(1)}, bf16[40,4224]{1,0:T(8,128)(2,1)S(1)}, bf16[48,4096]{1,0:T(8,128)(2,1)S(1)}, f32[24,4096]{1,0:T(8,128)S(1)}, f32[8,4096]{1,0:T(8,128)S(1)}) custom-call(s32[4]{0:T(128)S(1)} %pad_add_fusion.place, s32[40]{0:T(128)S(1)} %copy-done, s32[1]{0:T(128)S(6)} %copy.9.count, bf16[40,8192]{1,0:T(8,128)(2,1)} %images.1, ...), custom_call_target="tpu_custom_call" | custom-call | tf_op jit(solution)/shard_map/split/pallas_call | solution.py:129
  11.8 4.1 %all-to-all-done.after.refs_0_ = bf16[8,200,128]{2,1,0:T(8,128)(2,1)S(1)} async-done(((bf16[8,200,128]{2,1,0:T(8,128)(2,1)}), bf16[8,200,128]{2,1,0:T(8,128)(2,1)S(1)}, u32[]{:S(2)}, u32[]{:S(2)}) %all-to-all-start) | async-done | bytes 409632 | tf_op jit(solution)/shard_map/all_to_all | solution.py:420
  16.0 1.5 %collective-permute-start.1 = (bf16[8,200,128]{2,1,0:T(8,128)(2,1)S(1)}, bf16[8,200,128]{2,1,0:T(8,128)(2,1)S(1)}, u32[]{:S(2)}, u32[]{:S(2)}) collective-permute-start(bf16[8,200,128]{2,1,0:T(8,128)(2,1)S(1)} %all-to-all-done.after.refs_0_), channel_id=1, source_target_pairs={{0,16},{16,0},{32,48},{48,32},{1,17},{17,1},{33,49},{49,33},{2,18}... | collective-permute-start | bytes 1228808 | tf_op jit(solution)/shard_map/ppermute | solution.py:411
  17.5 2.7 %collective-permute-start.2 = (bf16[8,200,128]{2,1,0:T(8,128)(2,1)S(1)}, bf16[8,200,128]{2,1,0:T(8,128)(2,1)S(1)}, u32[]{:S(2)}, u32[]{:S(2)}) collective-permute-start(bf16[8,200,128]{2,1,0:T(8,128)(2,1)S(1)} %all-to-all-done.after.refs_0_), channel_id=1, source_target_pairs={{0,32},{16,48},{32,0},{48,16},{1,33},{17,49},{33,1},{49,17},{2,34}... | collective-permute-start | bytes 1228808 | tf_op jit(solution)/shard_map/ppermute | solution.py:411
  20.7 1.2 %collective-permute-start.4 = (bf16[40,4224]{1,0:T(8,128)(2,1)S(1)}, bf16[40,4224]{1,0:T(8,128)(2,1)S(1)}, u32[]{:S(2)}, u32[]{:S(2)}) collective-permute-start(bf16[40,4224]{1,0:T(8,128)(2,1)S(1)} %get-tuple-element.66.images_a.meta_a), channel_id=1, source_target_pairs={{0,2},{2,0},{1,3},{3,1},{4,6},{6,4},{5,7},{7,5},{8,10},{10,8},{9,1... | collective-permute-start | bytes 1013768 | tf_op jit(solution)/shard_map/ppermute | solution.py:427
  21.8 2.7 %collective-permute-start.5 = (bf16[40,4224]{1,0:T(8,128)(2,1)S(1)}, bf16[40,4224]{1,0:T(8,128)(2,1)S(1)}, u32[]{:S(2)}, u32[]{:S(2)}) collective-permute-start(bf16[40,4224]{1,0:T(8,128)(2,1)S(1)} %get-tuple-element.67), channel_id=1, source_target_pairs={{0,194},{2,64},{64,2},{66,128},{128,66},{130,192},{192,130},{194,0... | collective-permute-start | bytes 1013768 | tf_op jit(solution)/shard_map/ppermute | solution.py:428
  24.5 5.1 %build_here.1 = (bf16[2,1024,512]{2,1,0:T(8,128)(2,1)S(1)}, bf16[2,1024,512]{2,1,0:T(8,128)(2,1)S(1)}, bf16[2,1024,512]{2,1,0:T(8,128)(2,1)S(1)}, bf16[2,1024,51...) custom-call(s32[4]{0:T(128)S(1)} %pad_add_fusion.place, ...), custom_call_target="tpu_custom_call" | custom-call | flops 6000000000 | bytes 100000 | tf_op jit(solution)/shard_map/build_here/pallas_call | solution.py:190
  31.5 5.0 %build_next.1 = (bf16[2,1024,512]{2,1,0:T(8,128)(2,1)S(1)}, bf16[2,1024,512]{2,1,0:T(8,128)(2,1)S(1)}, bf16[2,1024,512]{2,1,0:T(8,128)(2,1)S(1)}, bf16[2,1024,51...) custom-call(s32[4]{0:T(128)S(1)} %pad_add_fusion.place, ...), custom_call_target="tpu_custom_call" | custom-call | flops 100000000 | bytes 100000 | tf_op jit(solution)/shard_map/build_next/pallas_call | solution.py:190
  36.8 2.6 %collective-permute-done.3.refs_2_.refs_3_ = bf16[8,200,128]{2,1,0:T(8,128)(2,1)S(1)} collective-permute-done((bf16[8,200,128]{2,1,0:T(8,128)(2,1)S(1)}, bf16[8,200,128]{2,1,0:T(8,128)(2,1)S(1)}, u32[]{:S(2)}, u32[]{:S(2)}) %collective-permute-start.3) | collective-permute-done | bytes 409632 | tf_op jit(solution)/shard_map/ppermute | solution.py:411
  39.3 1.5 %weigh.1.power = f32[8,200]{1,0:T(8,128)S(1)} custom-call(s32[4]{0:T(128)S(1)} %pad_add_fusion.place, f32[8,4096]{1,0:T(8,128)S(1)} %get-tuple-element.59.ctf, f32[8,200]{1,0:T(8,128)S(1)} %weigh_own.1.after, bf16[8,200,128]{2,1,0:T(8,128)(2,1)S(1)} %collective-permute-done.1.refs_0_.refs_1_, ...), custom_call_target="tpu_custom_call" | custom-call | tf_op jit(solution)/shard_map/weigh/pallas_call | solution.py:48
  40.8 5.2 %score_given.1 = f32[2,1024,256]{2,1,0:T(8,128)S(1)} custom-call(s32[4]{0:T(128)S(1)} %pad_add_fusion.place, f32[8,200]{1,0:T(8,128)S(1)} %weigh.1.power, bf16[40,4224]{1,0:T(8,128)(2,1)S(1)} %collective-permute-done.images_b.meta_a, bf16[40,4224]{1,0:T(8,128)(2,1)S(1)} %collective-permute-done.6.images_b.meta_b, ...), custom_call_target="tpu_custom_call" | custom-call | flops 4294967296 | tf_op jit(solution)/shard_map/score_given/pallas_call | solution.py:48
  46.1 5.2 %score_own.1.mine = f32[2,1024,256]{2,1,0:T(8,128)S(1)} custom-call(s32[4]{0:T(128)S(1)} %pad_add_fusion.place, f32[8,200]{1,0:T(8,128)S(1)} %weigh.1.power, bf16[40,4224]{1,0:T(8,128)(2,1)S(1)} %get-tuple-element.66.images_a.meta_a, bf16[40,4224]{1,0:T(8,128)(2,1)S(1)} %collective-permute-done.4.images_a.meta_b, ...), custom_call_target="tpu_custom_call" | custom-call | flops 4294967296 | tf_op jit(solution)/shard_map/score_own/pallas_call | solution.py:48
  51.3 1.2 %settle.1 = f32[8,8,128]{2,1,0:T(8,128)S(1)} custom-call(s32[4]{0:T(128)S(1)} %pad_add_fusion.place, f32[2,1024,256]{2,1,0:T(8,128)S(1)} %score_own.1.mine, f32[2,1024,256]{2,1,0:T(8,128)S(1)} %collective-permute-done.7.theirs), custom_call_target="tpu_custom_call" | custom-call | tf_op jit(solution)/shard_map/settle/pallas_call | solution.py:48
  52.5 15.4 %all_to_all.10.stats = f32[8,8,128]{2,1,0:T(8,128)S(1)} all-to-all(f32[8,8,128]{2,1,0:T(8,128)S(1)} %settle.1), channel_id=1, replica_groups=mesh['cls'=4,'grp'=4,'y'=4,'zl'=2,'core'=2] {'cls','zl'}, dimensions={0} | all-to-all | bytes 65536 | tf_op jit(solution)/shard_map/all_to_all | solution.py:445
  67.9 1.6 %posterior.1 = (bf16[2,200,1024]{2,1,0:T(8,128)(2,1)S(1)}, f32[8,40]{1,0:T(8,128)S(1)}) custom-call(s32[4]{0:T(128)S(1)} %pad_add_fusion.place, f32[2,1024,256]{2,1,0:T(8,128)S(1)} %score_own.1.mine, f32[2,1024,256]{2,1,0:T(8,128)S(1)} %collective-permute-done.7.theirs, f32[8,8,128]{2,1,0:T(8,128)S(1)} %all_to_all.10.stats, ...), custom_call_target="tpu_custom_call" | custom-call | tf_op jit(solution)/shard_map/posterior/pallas_call | solution.py:315
  69.8 1.6 %insert_begin.1 = (f32[4,200,128]{2,1,0:T(8,128)S(1)}, f32[4,200,128]{2,1,0:T(8,128)S(1)}) custom-call(s32[4]{0:T(128)S(1)} %pad_add_fusion.place, bf16[2,200,1024]{2,1,0:T(8,128)(2,1)S(1)} %get-tuple-element.88.mine, bf16[2,1024,512]{2,1,0:T(8,128)(2,1)S(1)} %get-tuple-element.73.refs_6_.a0.refs_2_, ...), custom_call_target="tpu_custom_call" | custom-call | flops 1073741824 | tf_op jit(solution)/shard_map/insert_begin/pallas_call | solution.py:48
  72.1 1.6 %insert_far.1 = (bf16[4,216,128]{2,1,0:T(8,128)(2,1)S(1)}, bf16[4,200,128]{2,1,0:T(8,128)(2,1)S(1)}, f32[8,128]{1,0:T(8,128)S(1)}) custom-call(s32[4]{0:T(128)S(1)} %pad_add_fusion.place, f32[8,40]{1,0:T(8,128)S(1)} %get-tuple-element.87.after, bf16[2,200,1024]{2,1,0:T(8,128)(2,1)S(1)} %get-tuple-element.88.mine, ...), custom_call_target="tpu_custom_call" | custom-call | flops 1073741824 | tf_op jit(solution)/shard_map/insert_far/pallas_call | solution.py:48
  73.9 0.9 collective-permute-start.10
  74.8 4.3 %insert_near.1 = (bf16[4,216,128]{2,1,0:T(8,128)(2,1)S(1)}, bf16[4,200,128]{2,1,0:T(8,128)(2,1)S(1)}, bf16[4,216,128]{2,1,0:T(8,128)(2,1)S(1)}, bf16[4,200,128]{2,1,0:T(8,128)(2,1)S(1)}, f32[8,128]{1,0:T(8,128)S(1)}) custom-call(s32[4]{0:T(128)S(1)} %pad_add_fusion.place, f32[8,128]{1,0:T(8,128)S(1)} %get-tuple-element.91.after, ...), custom_call_target="tpu_custom_call" | custom-call | flops 4294967296 | tf_op jit(solution)/shard_map/insert_near/pallas_call | solution.py:48
  79.1 1.4 %collective-permute-start.11 = (bf16[4,216,128]{2,1,0:T(8,128)(2,1)S(1)}, bf16[4,216,128]{2,1,0:T(8,128)(2,1)S(1)}, u32[]{:S(2)}, u32[]{:S(2)}) collective-permute-start(bf16[4,216,128]{2,1,0:T(8,128)(2,1)S(1)} %get-tuple-element.99), channel_id=1, source_target_pairs={{0,16},{16,0},{32,48},{48,32},{1,17},{17,1},{33,49},{49,33},{2,18}... | collective-permute-start | bytes 663560 | tf_op jit(solution)/shard_map/ppermute | solution.py:411
  80.5 2.7 %collective-permute-start.13 = (bf16[4,216,128]{2,1,0:T(8,128)(2,1)S(1)}, bf16[4,216,128]{2,1,0:T(8,128)(2,1)S(1)}, u32[]{:S(2)}, u32[]{:S(2)}) collective-permute-start(bf16[4,216,128]{2,1,0:T(8,128)(2,1)S(1)} %get-tuple-element.101), channel_id=1, source_target_pairs={{0,48},{16,32},{32,16},{48,0},{1,49},{17,33},{33,17},{49,1},{2,50}... | collective-permute-start | bytes 663560 | tf_op jit(solution)/shard_map/ppermute | solution.py:411
  84.1 2.4 %collective-permute-start.14 = (bf16[4,200,128]{2,1,0:T(8,128)(2,1)S(1)}, bf16[4,200,128]{2,1,0:T(8,128)(2,1)S(1)}, u32[]{:S(2)}, u32[]{:S(2)}) collective-permute-start(bf16[4,200,128]{2,1,0:T(8,128)(2,1)S(1)} %get-tuple-element.102), channel_id=1, source_target_pairs={{0,12},{4,8},{8,4},{12,0},{1,13},{5,9},{9,5},{13,1},{2,14},{6,10},... | collective-permute-start | bytes 614408 | tf_op jit(solution)/shard_map/ppermute | solution.py:411
  86.5 2.9 %insert_own.1 = (f32[4,216,128]{2,1,0:T(8,128)S(1)}, f32[4,200,128]{2,1,0:T(8,128)S(1)}, f32[8,128]{1,0:T(8,128)}) custom-call(s32[4]{0:T(128)S(1)} %pad_add_fusion.place, f32[8,128]{1,0:T(8,128)S(1)} %get-tuple-element.92.after, bf16[2,200,1024]{2,1,0:T(8,128)(2,1)S(1)} %get-tuple-element.88.mine, bf16[2,200,1024]{2,1,0:T(8,128)(2,1)S(1)} %collective-permute-done.8.theirs, ...), custom_call_target="tpu_custom_call" | custom-call | flops 2147483648 | tf_op jit(solution)/shard_map/insert_own/pallas_call | solution.py:48
  90.0 1.0 collective-permute-done.14.three_b
  92.0 4.6 %collective-permute-done.16.got_b = bf16[2,200,128]{2,1,0:T(8,128)(2,1)S(1)} collective-permute-done((bf16[2,200,128]{2,1,0:T(8,128)(2,1)S(1)}, bf16[2,200,128]{2,1,0:T(8,128)(2,1)S(1)}, u32[]{:S(2)}, u32[]{:S(2)}) %collective-permute-start.16) | collective-permute-done | bytes 102432 | tf_op jit(solution)/shard_map/ppermute | solution.py:411
  97.2 2.5 %collective-permute-start.17 = (bf16[216,128]{1,0:T(8,128)(2,1)S(1)}, bf16[216,128]{1,0:T(8,128)(2,1)S(1)}, u32[]{:S(2)}, u32[]{:S(2)}) collective-permute-start(bf16[216,128]{1,0:T(8,128)(2,1)S(1)} %get-tuple-element.109), channel_id=1, source_target_pairs={{0,12},{4,8},{8,4},{12,0},{1,13},{5,9},{9,5},{13,1},{2,14},{6,10},... | collective-permute-start | bytes 165896 | tf_op jit(solution)/shard_map/ppermute | solution.py:411
  100.4 4.6 %collective-permute-done.18.got_b = bf16[200,128]{1,0:T(8,128)(2,1)S(1)} collective-permute-done((bf16[200,128]{1,0:T(8,128)(2,1)S(1)}, bf16[200,128]{1,0:T(8,128)(2,1)S(1)}, u32[]{:S(2)}, u32[]{:S(2)}) %collective-permute-start.18) | collective-permute-done | bytes 51232 | tf_op jit(solution)/shard_map/ppermute | solution.py:411
  105.6 1.5 %collective-permute-start.19 = (bf16[216,128]{1,0:T(8,128)(2,1)S(1)}, bf16[216,128]{1,0:T(8,128)(2,1)S(1)}, u32[]{:S(2)}, u32[]{:S(2)}) collective-permute-start(bf16[216,128]{1,0:T(8,128)(2,1)S(1)} %get-tuple-element.112), channel_id=1, source_target_pairs={{0,2},{2,0},{1,3},{3,1},{4,6},{6,4},{5,7},{7,5},{8,10},{10,8},{9,1... | collective-permute-start | bytes 165896 | tf_op jit(solution)/shard_map/ppermute | solution.py:481
  107.6 2.2 %collective-permute-done.19.came = bf16[216,128]{1,0:T(8,128)(2,1)S(1)} collective-permute-done((bf16[216,128]{1,0:T(8,128)(2,1)S(1)}, bf16[216,128]{1,0:T(8,128)(2,1)S(1)}, u32[]{:S(2)}, u32[]{:S(2)}) %collective-permute-start.19) | collective-permute-done | bytes 55328 | tf_op jit(solution)/shard_map/ppermute | solution.py:481
  109.8 1.2 %finish.1 = (f32[2,200,128]{2,1,0:T(8,128)}, f32[2,8,200]{2,1,0:T(8,128)}) custom-call(s32[4]{0:T(128)S(1)} %pad_add_fusion.place, f32[216,128]{1,0:T(8,128)S(1)} %get-tuple-element.111.stay, bf16[216,128]{1,0:T(8,128)(2,1)S(1)} %collective-permute-done.19.came), custom_call_target="tpu_custom_call" | custom-call | tf_op jit(solution)/shard_map/finish/pallas_call | solution.py:48
  (34 shorter events, 9.4 us)
Async XLA Ops:
  2.3 13.6 %all-to-all-start = ((bf16[8,200,128]{2,1,0:T(8,128)(2,1)}), bf16[8,200,128]{2,1,0:T(8,128)(2,1)S(1)}, u32[]{:S(2)}, u32[]{:S(2)}) async-start(bf16[8,200,128]{2,1,0:T(8,128)(2,1)} %spread.1), calls=%async_computation | async-start | bytes 819200 | tf_op jit(solution)/shard_map/all_to_all | solution.py:420
  9.0 0.7 copy-start
  11.7 10.1 %collective-permute-start = (bf16[40,4224]{1,0:T(8,128)(2,1)S(1)}, bf16[40,4224]{1,0:T(8,128)(2,1)S(1)}, u32[]{:S(2)}, u32[]{:S(2)}) collective-permute-start(bf16[40,4224]{1,0:T(8,128)(2,1)S(1)} %get-tuple-element.67), channel_id=1, source_target_pairs={{0,1},{1,0},{2,3},{3,2},{4,5},{5,4},{6,7},{7,6},{8,9},{9,8},{10,11... | collective-permute-start | bytes 1013768 | tf_op jit(solution)/shard_map/ppermute | solution.py:424
  16.0 20.6 %collective-permute-start.1 = (bf16[8,200,128]{2,1,0:T(8,128)(2,1)S(1)}, bf16[8,200,128]{2,1,0:T(8,128)(2,1)S(1)}, u32[]{:S(2)}, u32[]{:S(2)}) collective-permute-start(bf16[8,200,128]{2,1,0:T(8,128)(2,1)S(1)} %all-to-all-done.after.refs_0_), channel_id=1, source_target_pairs={{0,16},{16,0},{32,48},{48,32},{1,17},{17,1},{33,49},{49,33},{2,18}... | collective-permute-start | bytes 1228808 | tf_op jit(solution)/shard_map/ppermute | solution.py:411
  17.5 19.3 %collective-permute-start.2 = (bf16[8,200,128]{2,1,0:T(8,128)(2,1)S(1)}, bf16[8,200,128]{2,1,0:T(8,128)(2,1)S(1)}, u32[]{:S(2)}, u32[]{:S(2)}) collective-permute-start(bf16[8,200,128]{2,1,0:T(8,128)(2,1)S(1)} %all-to-all-done.after.refs_0_), channel_id=1, source_target_pairs={{0,32},{16,48},{32,0},{48,16},{1,33},{17,49},{33,1},{49,17},{2,34}... | collective-permute-start | bytes 1228808 | tf_op jit(solution)/shard_map/ppermute | solution.py:411
  20.2 19.1 %collective-permute-start.3 = (bf16[8,200,128]{2,1,0:T(8,128)(2,1)S(1)}, bf16[8,200,128]{2,1,0:T(8,128)(2,1)S(1)}, u32[]{:S(2)}, u32[]{:S(2)}) collective-permute-start(bf16[8,200,128]{2,1,0:T(8,128)(2,1)S(1)} %all-to-all-done.after.refs_0_), channel_id=1, source_target_pairs={{0,48},{16,32},{32,16},{48,0},{1,49},{17,33},{33,17},{49,1},{2,50}... | collective-permute-start | bytes 1228808 | tf_op jit(solution)/shard_map/ppermute | solution.py:411
  20.7 8.9 %collective-permute-start.4 = (bf16[40,4224]{1,0:T(8,128)(2,1)S(1)}, bf16[40,4224]{1,0:T(8,128)(2,1)S(1)}, u32[]{:S(2)}, u32[]{:S(2)}) collective-permute-start(bf16[40,4224]{1,0:T(8,128)(2,1)S(1)} %get-tuple-element.66.images_a.meta_a), channel_id=1, source_target_pairs={{0,2},{2,0},{1,3},{3,1},{4,6},{6,4},{5,7},{7,5},{8,10},{10,8},{9,1... | collective-permute-start | bytes 1013768 | tf_op jit(solution)/shard_map/ppermute | solution.py:427
  21.8 8.0 %collective-permute-start.5 = (bf16[40,4224]{1,0:T(8,128)(2,1)S(1)}, bf16[40,4224]{1,0:T(8,128)(2,1)S(1)}, u32[]{:S(2)}, u32[]{:S(2)}) collective-permute-start(bf16[40,4224]{1,0:T(8,128)(2,1)S(1)} %get-tuple-element.67), channel_id=1, source_target_pairs={{0,194},{2,64},{64,2},{66,128},{128,66},{130,192},{192,130},{194,0... | collective-permute-start | bytes 1013768 | tf_op jit(solution)/shard_map/ppermute | solution.py:428
  29.8 1.7 %collective-permute-start.6 = (bf16[40,4224]{1,0:T(8,128)(2,1)S(1)}, bf16[40,4224]{1,0:T(8,128)(2,1)S(1)}, u32[]{:S(2)}, u32[]{:S(2)}) collective-permute-start(bf16[40,4224]{1,0:T(8,128)(2,1)S(1)} %collective-permute-done.5), channel_id=1, source_target_pairs={{0,1},{1,0},{2,3},{3,2},{4,5},{5,4},{6,7},{7,6},{8,9},{9,8},{10,11... | collective-permute-start | bytes 1013768 | tf_op jit(solution)/shard_map/ppermute | solution.py:433
  46.0 5.3 %collective-permute-start.7 = (f32[2,1024,256]{2,1,0:T(8,128)S(1)}, f32[2,1024,256]{2,1,0:T(8,128)S(1)}, u32[]{:S(2)}, u32[]{:S(2)}) collective-permute-start(f32[2,1024,256]{2,1,0:T(8,128)S(1)} %score_given.1), channel_id=1, source_target_pairs={{0,1},{1,0},{2,3},{3,2},{4,5},{5,4},{6,7},{7,6},{8,9},{9,8},{10,11... | collective-permute-start | bytes 6291464 | tf_op jit(solution)/shard_map/ppermute | solution.py:442
  69.5 2.6 %collective-permute-start.8 = (bf16[2,200,1024]{2,1,0:T(8,128)(2,1)S(1)}, bf16[2,200,1024]{2,1,0:T(8,128)(2,1)S(1)}, u32[]{:S(2)}, u32[]{:S(2)}) collective-permute-start(bf16[2,200,1024]{2,1,0:T(8,128)(2,1)S(1)} %get-tuple-element.88.mine), channel_id=1, source_target_pairs={{0,1},{1,0},{2,3},{3,2},{4,5},{5,4},{6,7},{7,6},{8,9},{9,8},{10,11... | collective-permute-start | bytes 2457608 | tf_op jit(solution)/shard_map/ppermute | solution.py:447
  73.8 15.6 %collective-permute-start.9 = (bf16[4,216,128]{2,1,0:T(8,128)(2,1)S(1)}, bf16[4,216,128]{2,1,0:T(8,128)(2,1)S(1)}, u32[]{:S(2)}, u32[]{:S(2)}) collective-permute-start(bf16[4,216,128]{2,1,0:T(8,128)(2,1)S(1)} %get-tuple-element.95), channel_id=1, source_target_pairs={{0,32},{16,48},{32,0},{48,16},{1,33},{17,49},{33,1},{49,17},{2,34}... | collective-permute-start | bytes 663560 | tf_op jit(solution)/shard_map/ppermute | solution.py:411
  73.9 10.2 %collective-permute-start.10 = (bf16[4,200,128]{2,1,0:T(8,128)(2,1)S(1)}, bf16[4,200,128]{2,1,0:T(8,128)(2,1)S(1)}, u32[]{:S(2)}, u32[]{:S(2)}) collective-permute-start(bf16[4,200,128]{2,1,0:T(8,128)(2,1)S(1)} %get-tuple-element.96), channel_id=1, source_target_pairs={{0,8},{4,12},{8,0},{12,4},{1,9},{5,13},{9,1},{13,5},{2,10},{6,14},... | collective-permute-start | bytes 614408 | tf_op jit(solution)/shard_map/ppermute | solution.py:411
  79.1 11.9 %collective-permute-start.11 = (bf16[4,216,128]{2,1,0:T(8,128)(2,1)S(1)}, bf16[4,216,128]{2,1,0:T(8,128)(2,1)S(1)}, u32[]{:S(2)}, u32[]{:S(2)}) collective-permute-start(bf16[4,216,128]{2,1,0:T(8,128)(2,1)S(1)} %get-tuple-element.99), channel_id=1, source_target_pairs={{0,16},{16,0},{32,48},{48,32},{1,17},{17,1},{33,49},{49,33},{2,18}... | collective-permute-start | bytes 663560 | tf_op jit(solution)/shard_map/ppermute | solution.py:411
  80.5 10.6 %collective-permute-start.13 = (bf16[4,216,128]{2,1,0:T(8,128)(2,1)S(1)}, bf16[4,216,128]{2,1,0:T(8,128)(2,1)S(1)}, u32[]{:S(2)}, u32[]{:S(2)}) collective-permute-start(bf16[4,216,128]{2,1,0:T(8,128)(2,1)S(1)} %get-tuple-element.101), channel_id=1, source_target_pairs={{0,48},{16,32},{32,16},{48,0},{1,49},{17,33},{33,17},{49,1},{2,50}... | collective-permute-start | bytes 663560 | tf_op jit(solution)/shard_map/ppermute | solution.py:411
  83.2 6.8 %collective-permute-start.12 = (bf16[4,200,128]{2,1,0:T(8,128)(2,1)S(1)}, bf16[4,200,128]{2,1,0:T(8,128)(2,1)S(1)}, u32[]{:S(2)}, u32[]{:S(2)}) collective-permute-start(bf16[4,200,128]{2,1,0:T(8,128)(2,1)S(1)} %get-tuple-element.100), channel_id=1, source_target_pairs={{0,4},{4,0},{8,12},{12,8},{1,5},{5,1},{9,13},{13,9},{2,6},{6,2},{1... | collective-permute-start | bytes 614408 | tf_op jit(solution)/shard_map/ppermute | solution.py:411
  84.1 7.0 %collective-permute-start.14 = (bf16[4,200,128]{2,1,0:T(8,128)(2,1)S(1)}, bf16[4,200,128]{2,1,0:T(8,128)(2,1)S(1)}, u32[]{:S(2)}, u32[]{:S(2)}) collective-permute-start(bf16[4,200,128]{2,1,0:T(8,128)(2,1)S(1)} %get-tuple-element.102), channel_id=1, source_target_pairs={{0,12},{4,8},{8,4},{12,0},{1,13},{5,9},{9,5},{13,1},{2,14},{6,10},... | collective-permute-start | bytes 614408 | tf_op jit(solution)/shard_map/ppermute | solution.py:411
  91.7 4.9 %collective-permute-start.15 = (bf16[2,216,128]{2,1,0:T(8,128)(2,1)S(1)}, bf16[2,216,128]{2,1,0:T(8,128)(2,1)S(1)}, u32[]{:S(2)}, u32[]{:S(2)}) collective-permute-start(bf16[2,216,128]{2,1,0:T(8,128)(2,1)S(1)} %get-tuple-element.105), channel_id=1, source_target_pairs={{0,4},{4,0},{8,12},{12,8},{1,5},{5,1},{9,13},{13,9},{2,6},{6,2},{1... | collective-permute-start | bytes 331784 | tf_op jit(solution)/shard_map/ppermute | solution.py:411
  91.8 4.7 %collective-permute-start.16 = (bf16[2,200,128]{2,1,0:T(8,128)(2,1)S(1)}, bf16[2,200,128]{2,1,0:T(8,128)(2,1)S(1)}, u32[]{:S(2)}, u32[]{:S(2)}) collective-permute-start(bf16[2,200,128]{2,1,0:T(8,128)(2,1)S(1)} %get-tuple-element.106), channel_id=1, source_target_pairs={{0,16},{16,0},{32,48},{48,32},{1,17},{17,1},{33,49},{49,33},{2,18}... | collective-permute-start | bytes 307208 | tf_op jit(solution)/shard_map/ppermute | solution.py:411
  97.2 7.8 %collective-permute-start.17 = (bf16[216,128]{1,0:T(8,128)(2,1)S(1)}, bf16[216,128]{1,0:T(8,128)(2,1)S(1)}, u32[]{:S(2)}, u32[]{:S(2)}) collective-permute-start(bf16[216,128]{1,0:T(8,128)(2,1)S(1)} %get-tuple-element.109), channel_id=1, source_target_pairs={{0,12},{4,8},{8,4},{12,0},{1,13},{5,9},{9,5},{13,1},{2,14},{6,10},... | collective-permute-start | bytes 165896 | tf_op jit(solution)/shard_map/ppermute | solution.py:411
  99.7 5.3 %collective-permute-start.18 = (bf16[200,128]{1,0:T(8,128)(2,1)S(1)}, bf16[200,128]{1,0:T(8,128)(2,1)S(1)}, u32[]{:S(2)}, u32[]{:S(2)}) collective-permute-start(bf16[200,128]{1,0:T(8,128)(2,1)S(1)} %get-tuple-element.110), channel_id=1, source_target_pairs={{0,48},{16,32},{32,16},{48,0},{1,49},{17,33},{33,17},{49,1},{2,50}... | collective-permute-start | bytes 153608 | tf_op jit(solution)/shard_map/ppermute | solution.py:411
  105.6 4.2 %collective-permute-start.19 = (bf16[216,128]{1,0:T(8,128)(2,1)S(1)}, bf16[216,128]{1,0:T(8,128)(2,1)S(1)}, u32[]{:S(2)}, u32[]{:S(2)}) collective-permute-start(bf16[216,128]{1,0:T(8,128)(2,1)S(1)} %get-tuple-element.112), channel_id=1, source_target_pairs={{0,2},{2,0},{1,3},{3,1},{4,6},{6,4},{5,7},{7,5},{8,10},{10,8},{9,1... | collective-permute-start | bytes 165896 | tf_op jit(solution)/shard_map/ppermute | solution.py:481

commit v3 on v2

--- a/solution.py
+++ b/solution.py
@@ -341,9 +341,9 @@
         block_sums(low, groups, put)
 
 
-def insert_kernel(chunks, begun=False):
+def insert_kernel(chunks, begun=False, joined=False):
     def kernel(place, after, mine, theirs, *refs):
-        starts, refs = (refs[:2], refs[2:]) if begun else ((None, None), refs)
+        starts, refs = (refs[:2], refs[2:]) if begun or joined else ((None, None), refs)
         members = (1,) if begun else (0, 1)
         shifted, outs = refs[: 4 * chunks], refs[4 * chunks :]
         lows = [theirs[0], theirs[1]] if begun else [mine[0], theirs[0], mine[1], theirs[1]]
@@ -360,20 +360,14 @@
 
             def put(n, value):
                 if start is not None:
-                    value = value + start[n]
+                    value = value + start[n, :WIDTH].astype(F32)
                 out[n, :WIDTH, :] = value.astype(out.dtype)
 
             block_sums(low, [pair.at[k] for pair in shifted[2 * i : 2 * i + 2] for k in members], put)
-            if i % 2 == 0:
-                for n in range(4):
-                    out[n, WIDTH:, :] = both.astype(out.dtype)
+            for n in range(4):
+                out[n, WIDTH:, :] = (both + start[n, WIDTH:].astype(F32) if joined else both).astype(out.dtype)
 
     return kernel
-
-
-def absorb_kernel(place, own_a, own_b, far_a, far_b, out_a, out_b):
-    out_a[...] = own_a[...] + far_a[...].astype(F32)
-    out_b[...] = own_b[...] + far_b[...].astype(F32)
 
 
 def gather_kernel(place, own_a, own_b, one_a, one_b, three_a, three_b, kept_a, kept_b, sent_a, sent_b):
@@ -386,23 +380,18 @@
             out[i] = (own_b[n] + one_b[n].astype(F32) + three_b[n].astype(F32)).astype(out.dtype)
 
 
-def middle_kernel(place, kept_a, kept_b, got_a, got_b, out_a, out_b, sent_a, sent_b):
-    for kept, got, out, sent in ((kept_a, got_a, out_a, sent_a), (kept_b, got_b, out_b, sent_b)):
-        out[...] = kept[0] + got[0].astype(F32)
-        sent[...] = (kept[1] + got[1].astype(F32)).astype(BF16)
-
-
-def part_kernel(place, kept_a, kept_b, got_a, got_b, stay, leave):
-    even = kept_a[...] + got_a[...].astype(F32)
-    odd = kept_b[...] + got_b[...].astype(F32)
-    stay[WIDTH:] = even[WIDTH:]
-    leave[WIDTH:] = even[WIDTH:].astype(BF16)
-    stay[:WIDTH] = jnp.where(place[2] == 0, even[:WIDTH], odd)
-    leave[:WIDTH] = jnp.where(place[2] == 0, odd, even[:WIDTH]).astype(BF16)
-
-
-def finish_kernel(place, stay, came, insertions, weights):
-    for k, sums in ((place[2], stay[...]), (1 - place[2], came[...].astype(F32))):
+def middle_kernel(place, kept_a, kept_b, got_a, got_b, stay, same, other, across):
+    side = place[2] == 0
+    for out, (i, turned) in ((stay, (0, False)), (same, (1, False)), (other, (0, True)), (across, (1, True))):
+        even = kept_a[i] + got_a[i].astype(F32)
+        odd = kept_b[i] + got_b[i].astype(F32)
+        out[...] = (jnp.where(side, odd, even) if turned else jnp.where(side, even, odd)).astype(out.dtype)
+
+
+def finish_kernel(place, stay, same, other, across, insertions, weights):
+    mine = stay[...] + same[...].astype(F32)
+    theirs = other[...].astype(F32) + across[...].astype(F32)
+    for k, sums in ((place[2], mine), (1 - place[2], theirs)):
         insertions[k] = sums[:WIDTH]
         weights[k] = jnp.concatenate([sums[WIDTH : WIDTH + GROUPS], sums[WIDTH + GROUPS :]], axis=1)[:, :WIDTH]
 
@@ -450,7 +439,7 @@
     token = shape(8, LANE)
 
     def block(kind):
-        return [shape(4, TALL, LANE, dtype=kind), shape(4, WIDTH, LANE, dtype=kind)]
+        return [shape(4, TALL, LANE, dtype=kind)] * 2
 
     def columns(chunk):
         return [pair[part + chunk] for part in (0, 4) for pair in shifted]
@@ -469,17 +458,27 @@
         2 * flops,
     )
     near = [swap(send[0], "grp", 1), swap(send[1], "y", 1), swap(send[2], "grp", 3), swap(send[3], "y", 3)]
-    *own, _ = call(insert_kernel(1), "insert_own", [*block(F32), token], (place, after, low, other_low, *columns(0)), LIMIT, flops)
-    own = call(absorb_kernel, "absorb", block(F32), (place, *own, *far), LIMIT)
-    tall, wide = (TALL, LANE), (WIDTH, LANE)
-    out = [shape(2, *tall), shape(2, *wide), shape(2, *tall, dtype=BF16), shape(2, *wide, dtype=BF16)]
+    *own, _ = call(
+        insert_kernel(1, joined=True), "insert_own", [*block(F32), token], (place, after, low, other_low, *far, *columns(0)), LIMIT, flops
+    )
+    pair = (2, TALL, LANE)
+    out = [shape(*pair)] * 2 + [shape(*pair, dtype=BF16)] * 2
     *kept, send_a, send_b = call(gather_kernel, "gather", out, (place, *own, *near), LIMIT)
-    out = [shape(*tall), shape(*wide), shape(*tall, dtype=BF16), shape(*wide, dtype=BF16)]
-    *kept, send_a, send_b = call(middle_kernel, "middle", out, (place, *kept, swap(send_a, "y", 1), swap(send_b, "grp", 1)), LIMIT)
-    out = [shape(*tall), shape(*tall, dtype=BF16)]
-    stay, leave = call(part_kernel, "part", out, (place, *kept, swap(send_a, "y", 3), swap(send_b, "grp", 3)), LIMIT)
-    came = lax.ppermute(leave, "zl", SWAP)
-    insertions, tally = call(finish_kernel, "finish", [shape(2, WIDTH, LANE), shape(2, GROUPS, WIDTH)], (place, stay, came), LIMIT)
+    out = [shape(*pair[1:])] + [shape(*pair[1:], dtype=BF16)] * 3
+    stay, *sent = call(middle_kernel, "middle", out, (place, *kept, swap(send_a, "y", 1), swap(send_b, "grp", 1)), LIMIT)
+    plane = ("grp", "y", "zl")
+    spots = [(i, j, k) for i in range(4) for j in range(4) for k in range(2)]
+
+    def number(i, j, k):
+        return i * 8 + j * 2 + k
+
+    def turn(i, j, side):
+        return (i, j ^ 3) if side == 0 else (i ^ 3, j)
+
+    same = lax.ppermute(sent[0], plane, [(number(i, j, k), number(*turn(i, j, k), k)) for i, j, k in spots])
+    other = lax.ppermute(sent[1], plane, [(number(i, j, k), number(i, j, 1 - k)) for i, j, k in spots])
+    across = lax.ppermute(sent[2], plane, [(number(i, j, k), number(*turn(i, j, 1 - k), 1 - k)) for i, j, k in spots])
+    insertions, tally = call(finish_kernel, "finish", [shape(2, WIDTH, LANE), shape(2, GROUPS, WIDTH)], (place, stay, same, other, across), LIMIT)
     return insertions, tally, evidence[0]
 
 

time: 112 us -> 109 us (0.973); the launches traced: 111 us -> 109 us
    ppermute x13 -> x11, waiting for transfers between devices: 13 us -> 9.31 us  [swap(): return lax.ppermute(value, axis, [(i, i ^ d) for i in range(n)])]
    ppermute x13 -> x11, starting transfers between devices: 16.5 us -> 13.3 us  [swap(): return lax.ppermute(value, axis, [(i, i ^ d) for i in range(n)])]
    ppermute x1 -> x3, starting transfers between devices: 1.55 us -> 4.6 us  [the longest x1 2.49 us: body(): lax.ppermute(sent[1], plane, [(number(i, j, k), number(i, j, 1 - k)) for...]
    ppermute x1 -> x3, waiting for transfers between devices: 2.18 us -> 5.08 us  [the longest x1 4.13 us: body(): lax.ppermute(sent[2], plane, [(number(i, j, k), number(*turn(i, j, 1 - k)...]
    pallas_call x14 -> x12, Pallas kernels: 28.1 us -> 27.1 us  [call(): pl.pallas_call(kernel, name=name, in_specs=[SMEM] + [VMEM] * (len(args) -...]
  transfers between devices with their start and end apart: 21 -> 21, of which waited for: 10 -> 12; matrix products, arithmetic and copies ran while one was open for 1% -> 1% of each run, Pallas kernels for 25% -> 25%
where the time goes in v3:
time: 109 us
  Pallas kernels  42.7 us (39%)
  starting transfers between devices  28.2 us (26%)
  waiting for transfers between devices  20.2 us (19%)
  blocking collectives  15.4 us (14%)
  between operations  1.47 us (1%)
  local copies, waits for them, and re-layouts  1.17 us (1%)
    pallas_call x12, Pallas kernels, call(): pl.pallas_call(kernel, name=name, in_specs=[SMEM] + [VMEM] * (len(args) -...  27.1 us
    all_to_all x1, blocking collectives, body(): stats = lax.all_to_all(stats, ring, 0, 0, tiled=True)  15.4 us
    ppermute x11, starting transfers between devices, swap(): return lax.ppermute(value, axis, [(i, i ^ d) for i in range(n)])  13.3 us
    pallas_call x2, Pallas kernels, build_call(): pl.pallas_call(build_kernel, name=name, in_specs=[SMEM] + [VMEM] * 5, out...  10.1 us
    ppermute x11, waiting for transfers between devices, swap(): return lax.ppermute(value, axis, [(i, i ^ d) for i in range(n)])  9.31 us
    all_to_all x1, starting transfers between devices, body(): column = lax.all_to_all(spread_call(stacks), ('y', 'zl'), 0, 0, tiled=True)  5.94 us
    all_to_all x1, waiting for transfers between devices, body(): column = lax.all_to_all(spread_call(stacks), ('y', 'zl'), 0, 0, tiled=True)  4.15 us
    ppermute x1, waiting for transfers between devices, body(): lax.ppermute(sent[2], plane, [(number(i, j, k), number(*turn(i, j, 1 - k)...  4.13 us
  transfers between devices with their start and end apart: 21, of which 12 were waited for; matrix products, arithmetic and copies ran while one was open for 1% of the time, Pallas kernels for 25%

profile of v3, /device:TPU:32, one launch (start us, length us, event | category | flops | bytes accessed | tf_op | source)
XLA Modules:
  0.0 109.2 jit_solution(4628074358918799515)
XLA Ops:
  0.6 1.7 %spread.1 = bf16[8,200,128]{2,1,0:T(8,128)(2,1)} custom-call(bf16[2,200,128]{2,1,0:T(8,128)(2,1)} %bitcast.7), custom_call_target="tpu_custom_call" | custom-call | tf_op jit(solution)/shard_map/spread/pallas_call | solution.py:83
  2.3 5.9 %all-to-all-start = ((bf16[8,200,128]{2,1,0:T(8,128)(2,1)}), bf16[8,200,128]{2,1,0:T(8,128)(2,1)S(1)}, u32[]{:S(2)}, u32[]{:S(2)}) async-start(bf16[8,200,128]{2,1,0:T(8,128)(2,1)} %spread.1), calls=%async_computation | async-start | bytes 819200 | tf_op jit(solution)/shard_map/all_to_all | solution.py:409
  9.7 2.0 %split.1 = (bf16[40,4224]{1,0:T(8,128)(2,1)S(1)}, bf16[40,4224]{1,0:T(8,128)(2,1)S(1)}, bf16[48,4096]{1,0:T(8,128)(2,1)S(1)}, f32[24,4096]{1,0:T(8,128)S(1)}, f32[8,4096]{1,0:T(8,128)S(1)}) custom-call(s32[4]{0:T(128)S(1)} %pad_add_fusion.place, s32[40]{0:T(128)S(1)} %copy-done, s32[1]{0:T(128)S(6)} %copy.9.count, bf16[40,8192]{1,0:T(8,128)(2,1)} %images.1, ...), custom_call_target="tpu_custom_call" | custom-call | tf_op jit(solution)/shard_map/split/pallas_call | solution.py:129
  11.8 4.1 %all-to-all-done.after.refs_0_ = bf16[8,200,128]{2,1,0:T(8,128)(2,1)S(1)} async-done(((bf16[8,200,128]{2,1,0:T(8,128)(2,1)}), bf16[8,200,128]{2,1,0:T(8,128)(2,1)S(1)}, u32[]{:S(2)}, u32[]{:S(2)}) %all-to-all-start) | async-done | bytes 409632 | tf_op jit(solution)/shard_map/all_to_all | solution.py:409
  16.0 1.5 %collective-permute-start.1 = (bf16[8,200,128]{2,1,0:T(8,128)(2,1)S(1)}, bf16[8,200,128]{2,1,0:T(8,128)(2,1)S(1)}, u32[]{:S(2)}, u32[]{:S(2)}) collective-permute-start(bf16[8,200,128]{2,1,0:T(8,128)(2,1)S(1)} %all-to-all-done.after.refs_0_), channel_id=1, source_target_pairs={{0,16},{16,0},{32,48},{48,32},{1,17},{17,1},{33,49},{49,33},{2,18}... | collective-permute-start | bytes 1228808 | tf_op jit(solution)/shard_map/ppermute | solution.py:400
  17.5 2.7 %collective-permute-start.2 = (bf16[8,200,128]{2,1,0:T(8,128)(2,1)S(1)}, bf16[8,200,128]{2,1,0:T(8,128)(2,1)S(1)}, u32[]{:S(2)}, u32[]{:S(2)}) collective-permute-start(bf16[8,200,128]{2,1,0:T(8,128)(2,1)S(1)} %all-to-all-done.after.refs_0_), channel_id=1, source_target_pairs={{0,32},{16,48},{32,0},{48,16},{1,33},{17,49},{33,1},{49,17},{2,34}... | collective-permute-start | bytes 1228808 | tf_op jit(solution)/shard_map/ppermute | solution.py:400
  20.7 1.2 %collective-permute-start.4 = (bf16[40,4224]{1,0:T(8,128)(2,1)S(1)}, bf16[40,4224]{1,0:T(8,128)(2,1)S(1)}, u32[]{:S(2)}, u32[]{:S(2)}) collective-permute-start(bf16[40,4224]{1,0:T(8,128)(2,1)S(1)} %get-tuple-element.62.images_a.meta_a), channel_id=1, source_target_pairs={{0,2},{2,0},{1,3},{3,1},{4,6},{6,4},{5,7},{7,5},{8,10},{10,8},{9,1... | collective-permute-start | bytes 1013768 | tf_op jit(solution)/shard_map/ppermute | solution.py:416
  21.8 2.7 %collective-permute-start.5 = (bf16[40,4224]{1,0:T(8,128)(2,1)S(1)}, bf16[40,4224]{1,0:T(8,128)(2,1)S(1)}, u32[]{:S(2)}, u32[]{:S(2)}) collective-permute-start(bf16[40,4224]{1,0:T(8,128)(2,1)S(1)} %get-tuple-element.63), channel_id=1, source_target_pairs={{0,194},{2,64},{64,2},{66,128},{128,66},{130,192},{192,130},{194,0... | collective-permute-start | bytes 1013768 | tf_op jit(solution)/shard_map/ppermute | solution.py:417
  24.5 5.1 %build_here.1 = (bf16[2,1024,512]{2,1,0:T(8,128)(2,1)S(1)}, bf16[2,1024,512]{2,1,0:T(8,128)(2,1)S(1)}, bf16[2,1024,512]{2,1,0:T(8,128)(2,1)S(1)}, bf16[2,1024,51...) custom-call(s32[4]{0:T(128)S(1)} %pad_add_fusion.place, ...), custom_call_target="tpu_custom_call" | custom-call | flops 6000000000 | bytes 100000 | tf_op jit(solution)/shard_map/build_here/pallas_call | solution.py:190
  29.9 0.9 weigh_own.1.after
  31.5 5.1 %build_next.1 = (bf16[2,1024,512]{2,1,0:T(8,128)(2,1)S(1)}, bf16[2,1024,512]{2,1,0:T(8,128)(2,1)S(1)}, bf16[2,1024,512]{2,1,0:T(8,128)(2,1)S(1)}, bf16[2,1024,51...) custom-call(s32[4]{0:T(128)S(1)} %pad_add_fusion.place, ...), custom_call_target="tpu_custom_call" | custom-call | flops 100000000 | bytes 100000 | tf_op jit(solution)/shard_map/build_next/pallas_call | solution.py:190
  36.8 2.6 %collective-permute-done.3.refs_2_.refs_3_ = bf16[8,200,128]{2,1,0:T(8,128)(2,1)S(1)} collective-permute-done((bf16[8,200,128]{2,1,0:T(8,128)(2,1)S(1)}, bf16[8,200,128]{2,1,0:T(8,128)(2,1)S(1)}, u32[]{:S(2)}, u32[]{:S(2)}) %collective-permute-start.3) | collective-permute-done | bytes 409632 | tf_op jit(solution)/shard_map/ppermute | solution.py:400
  39.3 1.5 %weigh.1.power = f32[8,200]{1,0:T(8,128)S(1)} custom-call(s32[4]{0:T(128)S(1)} %pad_add_fusion.place, f32[8,4096]{1,0:T(8,128)S(1)} %get-tuple-element.55.ctf, f32[8,200]{1,0:T(8,128)S(1)} %weigh_own.1.after, bf16[8,200,128]{2,1,0:T(8,128)(2,1)S(1)} %collective-permute-done.1.refs_0_.refs_1_, ...), custom_call_target="tpu_custom_call" | custom-call | tf_op jit(solution)/shard_map/weigh/pallas_call | solution.py:48
  40.8 5.2 %score_given.1 = f32[2,1024,256]{2,1,0:T(8,128)S(1)} custom-call(s32[4]{0:T(128)S(1)} %pad_add_fusion.place, f32[8,200]{1,0:T(8,128)S(1)} %weigh.1.power, bf16[40,4224]{1,0:T(8,128)(2,1)S(1)} %collective-permute-done.images_b.meta_a, bf16[40,4224]{1,0:T(8,128)(2,1)S(1)} %collective-permute-done.6.images_b.meta_b, ...), custom_call_target="tpu_custom_call" | custom-call | flops 4294967296 | tf_op jit(solution)/shard_map/score_given/pallas_call | solution.py:48
  46.1 5.2 %score_own.1.mine = f32[2,1024,256]{2,1,0:T(8,128)S(1)} custom-call(s32[4]{0:T(128)S(1)} %pad_add_fusion.place, f32[8,200]{1,0:T(8,128)S(1)} %weigh.1.power, bf16[40,4224]{1,0:T(8,128)(2,1)S(1)} %get-tuple-element.62.images_a.meta_a, bf16[40,4224]{1,0:T(8,128)(2,1)S(1)} %collective-permute-done.4.images_a.meta_b, ...), custom_call_target="tpu_custom_call" | custom-call | flops 4294967296 | tf_op jit(solution)/shard_map/score_own/pallas_call | solution.py:48
  51.3 1.3 %settle.1 = f32[8,8,128]{2,1,0:T(8,128)S(1)} custom-call(s32[4]{0:T(128)S(1)} %pad_add_fusion.place, f32[2,1024,256]{2,1,0:T(8,128)S(1)} %score_own.1.mine, f32[2,1024,256]{2,1,0:T(8,128)S(1)} %collective-permute-done.7.theirs), custom_call_target="tpu_custom_call" | custom-call | tf_op jit(solution)/shard_map/settle/pallas_call | solution.py:48
  52.6 15.4 %all_to_all.10.stats = f32[8,8,128]{2,1,0:T(8,128)S(1)} all-to-all(f32[8,8,128]{2,1,0:T(8,128)S(1)} %settle.1), channel_id=1, replica_groups=mesh['cls'=4,'grp'=4,'y'=4,'zl'=2,'core'=2] {'cls','zl'}, dimensions={0} | all-to-all | bytes 65536 | tf_op jit(solution)/shard_map/all_to_all | solution.py:434
  68.0 1.7 %posterior.1 = (bf16[2,200,1024]{2,1,0:T(8,128)(2,1)S(1)}, f32[8,40]{1,0:T(8,128)S(1)}) custom-call(s32[4]{0:T(128)S(1)} %pad_add_fusion.place, f32[2,1024,256]{2,1,0:T(8,128)S(1)} %score_own.1.mine, f32[2,1024,256]{2,1,0:T(8,128)S(1)} %collective-permute-done.7.theirs, f32[8,8,128]{2,1,0:T(8,128)S(1)} %all_to_all.10.stats, ...), custom_call_target="tpu_custom_call" | custom-call | tf_op jit(solution)/shard_map/posterior/pallas_call | solution.py:315
  70.0 1.6 %insert_begin.1 = (f32[4,200,128]{2,1,0:T(8,128)S(1)}, f32[4,200,128]{2,1,0:T(8,128)S(1)}) custom-call(s32[4]{0:T(128)S(1)} %pad_add_fusion.place, bf16[2,200,1024]{2,1,0:T(8,128)(2,1)S(1)} %get-tuple-element.84.mine, bf16[2,1024,512]{2,1,0:T(8,128)(2,1)S(1)} %get-tuple-element.69.refs_6_.a0.refs_2_, ...), custom_call_target="tpu_custom_call" | custom-call | flops 1073741824 | tf_op jit(solution)/shard_map/insert_begin/pallas_call | solution.py:48
  72.3 1.6 %insert_far.1 = (bf16[4,216,128]{2,1,0:T(8,128)(2,1)S(1)}, bf16[4,216,128]{2,1,0:T(8,128)(2,1)S(1)}, f32[8,128]{1,0:T(8,128)S(1)}) custom-call(s32[4]{0:T(128)S(1)} %pad_add_fusion.place, f32[8,40]{1,0:T(8,128)S(1)} %get-tuple-element.83.after, bf16[2,200,1024]{2,1,0:T(8,128)(2,1)S(1)} %get-tuple-element.84.mine, ...), custom_call_target="tpu_custom_call" | custom-call | flops 1073741824 | tf_op jit(solution)/shard_map/insert_far/pallas_call | solution.py:48
  73.9 0.9 collective-permute-start.10
  74.9 4.3 %insert_near.1 = (bf16[4,216,128]{2,1,0:T(8,128)(2,1)S(1)}, bf16[4,216,128]{2,1,0:T(8,128)(2,1)S(1)}, bf16[4,216,128]{2,1,0:T(8,128)(2,1)S(1)}, bf16[4,216,128]{2,1,0:T(8,128)(2,1)S(1)}, f32[8,128]{1,0:T(8,128)S(1)}) custom-call(s32[4]{0:T(128)S(1)} %pad_add_fusion.place, f32[8,128]{1,0:T(8,128)S(1)} %get-tuple-element.87.after, ...), custom_call_target="tpu_custom_call" | custom-call | flops 4294967296 | tf_op jit(solution)/shard_map/insert_near/pallas_call | solution.py:48
  79.2 1.5 %collective-permute-start.11 = (bf16[4,216,128]{2,1,0:T(8,128)(2,1)S(1)}, bf16[4,216,128]{2,1,0:T(8,128)(2,1)S(1)}, u32[]{:S(2)}, u32[]{:S(2)}) collective-permute-start(bf16[4,216,128]{2,1,0:T(8,128)(2,1)S(1)} %get-tuple-element.93), channel_id=1, source_target_pairs={{0,16},{16,0},{32,48},{48,32},{1,17},{17,1},{33,49},{49,33},{2,18}... | collective-permute-start | bytes 663560 | tf_op jit(solution)/shard_map/ppermute | solution.py:400
  81.5 2.8 %collective-permute-start.13 = (bf16[4,216,128]{2,1,0:T(8,128)(2,1)S(1)}, bf16[4,216,128]{2,1,0:T(8,128)(2,1)S(1)}, u32[]{:S(2)}, u32[]{:S(2)}) collective-permute-start(bf16[4,216,128]{2,1,0:T(8,128)(2,1)S(1)} %get-tuple-element.95), channel_id=1, source_target_pairs={{0,48},{16,32},{32,16},{48,0},{1,49},{17,33},{33,17},{49,1},{2,50}... | collective-permute-start | bytes 663560 | tf_op jit(solution)/shard_map/ppermute | solution.py:400
  84.3 2.4 %collective-permute-start.14 = (bf16[4,216,128]{2,1,0:T(8,128)(2,1)S(1)}, bf16[4,216,128]{2,1,0:T(8,128)(2,1)S(1)}, u32[]{:S(2)}, u32[]{:S(2)}) collective-permute-start(bf16[4,216,128]{2,1,0:T(8,128)(2,1)S(1)} %get-tuple-element.96), channel_id=1, source_target_pairs={{0,12},{4,8},{8,4},{12,0},{1,13},{5,9},{9,5},{13,1},{2,14},{6,10},... | collective-permute-start | bytes 663560 | tf_op jit(solution)/shard_map/ppermute | solution.py:400
  86.6 3.0 %insert_own.1 = (f32[4,216,128]{2,1,0:T(8,128)S(1)}, f32[4,216,128]{2,1,0:T(8,128)S(1)}, f32[8,128]{1,0:T(8,128)}) custom-call(s32[4]{0:T(128)S(1)} %pad_add_fusion.place, f32[8,128]{1,0:T(8,128)S(1)} %get-tuple-element.88.after, bf16[2,200,1024]{2,1,0:T(8,128)(2,1)S(1)} %get-tuple-element.84.mine, bf16[2,200,1024]{2,1,0:T(8,128)(2,1)S(1)} %collective-permute-done.8.theirs, ...), custom_call_target="tpu_custom_call" | custom-call | flops 2147483648 | tf_op jit(solution)/shard_map/insert_own/pallas_call | solution.py:48
  89.7 1.8 %collective-permute-done.14.three_b = bf16[4,216,128]{2,1,0:T(8,128)(2,1)S(1)} collective-permute-done((bf16[4,216,128]{2,1,0:T(8,128)(2,1)S(1)}, bf16[4,216,128]{2,1,0:T(8,128)(2,1)S(1)}, u32[]{:S(2)}, u32[]{:S(2)}) %collective-permute-start.14) | collective-permute-done | bytes 221216 | tf_op jit(solution)/shard_map/ppermute | solution.py:400
  92.4 4.6 %collective-permute-done.15.got_a = bf16[2,216,128]{2,1,0:T(8,128)(2,1)S(1)} collective-permute-done((bf16[2,216,128]{2,1,0:T(8,128)(2,1)S(1)}, bf16[2,216,128]{2,1,0:T(8,128)(2,1)S(1)}, u32[]{:S(2)}, u32[]{:S(2)}) %collective-permute-start.15) | collective-permute-done | bytes 110624 | tf_op jit(solution)/shard_map/ppermute | solution.py:400
  97.8 1.4 %collective-permute-start.17 = (bf16[216,128]{1,0:T(8,128)(2,1)S(1)}, bf16[216,128]{1,0:T(8,128)(2,1)S(1)}, u32[]{:S(2)}, u32[]{:S(2)}) collective-permute-start(bf16[216,128]{1,0:T(8,128)(2,1)S(1)} %get-tuple-element.102), channel_id=1, source_target_pairs={{0,12},{2,50},{4,8},{6,54},{8,4},{10,58},{12,0},{14,62},{16,28},{1... | collective-permute-start | bytes 165896 | tf_op jit(solution)/shard_map/ppermute | solution.py:478
  99.2 2.5 %collective-permute-start.18 = (bf16[216,128]{1,0:T(8,128)(2,1)S(1)}, bf16[216,128]{1,0:T(8,128)(2,1)S(1)}, u32[]{:S(2)}, u32[]{:S(2)}) collective-permute-start(bf16[216,128]{1,0:T(8,128)(2,1)S(1)} %get-tuple-element.103), channel_id=1, source_target_pairs={{0,2},{2,0},{4,6},{6,4},{8,10},{10,8},{12,14},{14,12},{16,18},{18,... | collective-permute-start | bytes 165896 | tf_op jit(solution)/shard_map/ppermute | solution.py:479
  103.8 4.1 %collective-permute-done.19.across = bf16[216,128]{1,0:T(8,128)(2,1)S(1)} collective-permute-done((bf16[216,128]{1,0:T(8,128)(2,1)S(1)}, bf16[216,128]{1,0:T(8,128)(2,1)S(1)}, u32[]{:S(2)}, u32[]{:S(2)}) %collective-permute-start.19) | collective-permute-done | bytes 55328 | tf_op jit(solution)/shard_map/ppermute | solution.py:480
  108.0 1.2 %finish.1 = (f32[2,200,128]{2,1,0:T(8,128)}, f32[2,8,200]{2,1,0:T(8,128)}) custom-call(s32[4]{0:T(128)S(1)} %pad_add_fusion.place, f32[216,128]{1,0:T(8,128)S(1)} %get-tuple-element.101.stay, bf16[216,128]{1,0:T(8,128)(2,1)S(1)} %collective-permute-done.17.same, bf16[216,128]{1,0:T(8,128)(2,1)S(1)} %collective-permute-done.18.other, ...), custom_call_target="tpu_custom_call" | custom-call | tf_op jit(solution)/shard_map/finish/pallas_call | solution.py:48
  (32 shorter events, 8.1 us)
Async XLA Ops:
  2.3 13.6 %all-to-all-start = ((bf16[8,200,128]{2,1,0:T(8,128)(2,1)}), bf16[8,200,128]{2,1,0:T(8,128)(2,1)S(1)}, u32[]{:S(2)}, u32[]{:S(2)}) async-start(bf16[8,200,128]{2,1,0:T(8,128)(2,1)} %spread.1), calls=%async_computation | async-start | bytes 819200 | tf_op jit(solution)/shard_map/all_to_all | solution.py:409
  9.0 0.7 copy-start
  11.7 10.1 %collective-permute-start = (bf16[40,4224]{1,0:T(8,128)(2,1)S(1)}, bf16[40,4224]{1,0:T(8,128)(2,1)S(1)}, u32[]{:S(2)}, u32[]{:S(2)}) collective-permute-start(bf16[40,4224]{1,0:T(8,128)(2,1)S(1)} %get-tuple-element.63), channel_id=1, source_target_pairs={{0,1},{1,0},{2,3},{3,2},{4,5},{5,4},{6,7},{7,6},{8,9},{9,8},{10,11... | collective-permute-start | bytes 1013768 | tf_op jit(solution)/shard_map/ppermute | solution.py:413
  16.0 20.6 %collective-permute-start.1 = (bf16[8,200,128]{2,1,0:T(8,128)(2,1)S(1)}, bf16[8,200,128]{2,1,0:T(8,128)(2,1)S(1)}, u32[]{:S(2)}, u32[]{:S(2)}) collective-permute-start(bf16[8,200,128]{2,1,0:T(8,128)(2,1)S(1)} %all-to-all-done.after.refs_0_), channel_id=1, source_target_pairs={{0,16},{16,0},{32,48},{48,32},{1,17},{17,1},{33,49},{49,33},{2,18}... | collective-permute-start | bytes 1228808 | tf_op jit(solution)/shard_map/ppermute | solution.py:400
  17.5 19.3 %collective-permute-start.2 = (bf16[8,200,128]{2,1,0:T(8,128)(2,1)S(1)}, bf16[8,200,128]{2,1,0:T(8,128)(2,1)S(1)}, u32[]{:S(2)}, u32[]{:S(2)}) collective-permute-start(bf16[8,200,128]{2,1,0:T(8,128)(2,1)S(1)} %all-to-all-done.after.refs_0_), channel_id=1, source_target_pairs={{0,32},{16,48},{32,0},{48,16},{1,33},{17,49},{33,1},{49,17},{2,34}... | collective-permute-start | bytes 1228808 | tf_op jit(solution)/shard_map/ppermute | solution.py:400
  20.2 19.1 %collective-permute-start.3 = (bf16[8,200,128]{2,1,0:T(8,128)(2,1)S(1)}, bf16[8,200,128]{2,1,0:T(8,128)(2,1)S(1)}, u32[]{:S(2)}, u32[]{:S(2)}) collective-permute-start(bf16[8,200,128]{2,1,0:T(8,128)(2,1)S(1)} %all-to-all-done.after.refs_0_), channel_id=1, source_target_pairs={{0,48},{16,32},{32,16},{48,0},{1,49},{17,33},{33,17},{49,1},{2,50}... | collective-permute-start | bytes 1228808 | tf_op jit(solution)/shard_map/ppermute | solution.py:400
  20.7 8.9 %collective-permute-start.4 = (bf16[40,4224]{1,0:T(8,128)(2,1)S(1)}, bf16[40,4224]{1,0:T(8,128)(2,1)S(1)}, u32[]{:S(2)}, u32[]{:S(2)}) collective-permute-start(bf16[40,4224]{1,0:T(8,128)(2,1)S(1)} %get-tuple-element.62.images_a.meta_a), channel_id=1, source_target_pairs={{0,2},{2,0},{1,3},{3,1},{4,6},{6,4},{5,7},{7,5},{8,10},{10,8},{9,1... | collective-permute-start | bytes 1013768 | tf_op jit(solution)/shard_map/ppermute | solution.py:416
  21.8 8.0 %collective-permute-start.5 = (bf16[40,4224]{1,0:T(8,128)(2,1)S(1)}, bf16[40,4224]{1,0:T(8,128)(2,1)S(1)}, u32[]{:S(2)}, u32[]{:S(2)}) collective-permute-start(bf16[40,4224]{1,0:T(8,128)(2,1)S(1)} %get-tuple-element.63), channel_id=1, source_target_pairs={{0,194},{2,64},{64,2},{66,128},{128,66},{130,192},{192,130},{194,0... | collective-permute-start | bytes 1013768 | tf_op jit(solution)/shard_map/ppermute | solution.py:417
  29.8 1.7 %collective-permute-start.6 = (bf16[40,4224]{1,0:T(8,128)(2,1)S(1)}, bf16[40,4224]{1,0:T(8,128)(2,1)S(1)}, u32[]{:S(2)}, u32[]{:S(2)}) collective-permute-start(bf16[40,4224]{1,0:T(8,128)(2,1)S(1)} %collective-permute-done.5), channel_id=1, source_target_pairs={{0,1},{1,0},{2,3},{3,2},{4,5},{5,4},{6,7},{7,6},{8,9},{9,8},{10,11... | collective-permute-start | bytes 1013768 | tf_op jit(solution)/shard_map/ppermute | solution.py:422
  46.0 5.3 %collective-permute-start.7 = (f32[2,1024,256]{2,1,0:T(8,128)S(1)}, f32[2,1024,256]{2,1,0:T(8,128)S(1)}, u32[]{:S(2)}, u32[]{:S(2)}) collective-permute-start(f32[2,1024,256]{2,1,0:T(8,128)S(1)} %score_given.1), channel_id=1, source_target_pairs={{0,1},{1,0},{2,3},{3,2},{4,5},{5,4},{6,7},{7,6},{8,9},{9,8},{10,11... | collective-permute-start | bytes 6291464 | tf_op jit(solution)/shard_map/ppermute | solution.py:431
  69.7 2.6 %collective-permute-start.8 = (bf16[2,200,1024]{2,1,0:T(8,128)(2,1)S(1)}, bf16[2,200,1024]{2,1,0:T(8,128)(2,1)S(1)}, u32[]{:S(2)}, u32[]{:S(2)}) collective-permute-start(bf16[2,200,1024]{2,1,0:T(8,128)(2,1)S(1)} %get-tuple-element.84.mine), channel_id=1, source_target_pairs={{0,1},{1,0},{2,3},{3,2},{4,5},{5,4},{6,7},{7,6},{8,9},{9,8},{10,11... | collective-permute-start | bytes 2457608 | tf_op jit(solution)/shard_map/ppermute | solution.py:436
  73.9 10.3 %collective-permute-start.10 = (bf16[4,216,128]{2,1,0:T(8,128)(2,1)S(1)}, bf16[4,216,128]{2,1,0:T(8,128)(2,1)S(1)}, u32[]{:S(2)}, u32[]{:S(2)}) collective-permute-start(bf16[4,216,128]{2,1,0:T(8,128)(2,1)S(1)} %get-tuple-element.90), channel_id=1, source_target_pairs={{0,8},{4,12},{8,0},{12,4},{1,9},{5,13},{9,1},{13,5},{2,10},{6,14},... | collective-permute-start | bytes 663560 | tf_op jit(solution)/shard_map/ppermute | solution.py:400
  74.9 11.7 %collective-permute-start.9 = (bf16[4,216,128]{2,1,0:T(8,128)(2,1)S(1)}, bf16[4,216,128]{2,1,0:T(8,128)(2,1)S(1)}, u32[]{:S(2)}, u32[]{:S(2)}) collective-permute-start(bf16[4,216,128]{2,1,0:T(8,128)(2,1)S(1)} %get-tuple-element.89), channel_id=1, source_target_pairs={{0,32},{16,48},{32,0},{48,16},{1,33},{17,49},{33,1},{49,17},{2,34}... | collective-permute-start | bytes 663560 | tf_op jit(solution)/shard_map/ppermute | solution.py:400
  79.2 10.5 %collective-permute-start.11 = (bf16[4,216,128]{2,1,0:T(8,128)(2,1)S(1)}, bf16[4,216,128]{2,1,0:T(8,128)(2,1)S(1)}, u32[]{:S(2)}, u32[]{:S(2)}) collective-permute-start(bf16[4,216,128]{2,1,0:T(8,128)(2,1)S(1)} %get-tuple-element.93), channel_id=1, source_target_pairs={{0,16},{16,0},{32,48},{48,32},{1,17},{17,1},{33,49},{49,33},{2,18}... | collective-permute-start | bytes 663560 | tf_op jit(solution)/shard_map/ppermute | solution.py:400
  80.7 9.0 %collective-permute-start.12 = (bf16[4,216,128]{2,1,0:T(8,128)(2,1)S(1)}, bf16[4,216,128]{2,1,0:T(8,128)(2,1)S(1)}, u32[]{:S(2)}, u32[]{:S(2)}) collective-permute-start(bf16[4,216,128]{2,1,0:T(8,128)(2,1)S(1)} %get-tuple-element.94), channel_id=1, source_target_pairs={{0,4},{4,0},{8,12},{12,8},{1,5},{5,1},{9,13},{13,9},{2,6},{6,2},{1... | collective-permute-start | bytes 663560 | tf_op jit(solution)/shard_map/ppermute | solution.py:400
  81.5 8.2 %collective-permute-start.13 = (bf16[4,216,128]{2,1,0:T(8,128)(2,1)S(1)}, bf16[4,216,128]{2,1,0:T(8,128)(2,1)S(1)}, u32[]{:S(2)}, u32[]{:S(2)}) collective-permute-start(bf16[4,216,128]{2,1,0:T(8,128)(2,1)S(1)} %get-tuple-element.95), channel_id=1, source_target_pairs={{0,48},{16,32},{32,16},{48,0},{1,49},{17,33},{33,17},{49,1},{2,50}... | collective-permute-start | bytes 663560 | tf_op jit(solution)/shard_map/ppermute | solution.py:400
  84.3 7.3 %collective-permute-start.14 = (bf16[4,216,128]{2,1,0:T(8,128)(2,1)S(1)}, bf16[4,216,128]{2,1,0:T(8,128)(2,1)S(1)}, u32[]{:S(2)}, u32[]{:S(2)}) collective-permute-start(bf16[4,216,128]{2,1,0:T(8,128)(2,1)S(1)} %get-tuple-element.96), channel_id=1, source_target_pairs={{0,12},{4,8},{8,4},{12,0},{1,13},{5,9},{9,5},{13,1},{2,14},{6,10},... | collective-permute-start | bytes 663560 | tf_op jit(solution)/shard_map/ppermute | solution.py:400
  92.2 4.8 %collective-permute-start.15 = (bf16[2,216,128]{2,1,0:T(8,128)(2,1)S(1)}, bf16[2,216,128]{2,1,0:T(8,128)(2,1)S(1)}, u32[]{:S(2)}, u32[]{:S(2)}) collective-permute-start(bf16[2,216,128]{2,1,0:T(8,128)(2,1)S(1)} %get-tuple-element.99), channel_id=1, source_target_pairs={{0,4},{4,0},{8,12},{12,8},{1,5},{5,1},{9,13},{13,9},{2,6},{6,2},{1... | collective-permute-start | bytes 331784 | tf_op jit(solution)/shard_map/ppermute | solution.py:400
  92.3 4.8 %collective-permute-start.16 = (bf16[2,216,128]{2,1,0:T(8,128)(2,1)S(1)}, bf16[2,216,128]{2,1,0:T(8,128)(2,1)S(1)}, u32[]{:S(2)}, u32[]{:S(2)}) collective-permute-start(bf16[2,216,128]{2,1,0:T(8,128)(2,1)S(1)} %get-tuple-element.100), channel_id=1, source_target_pairs={{0,16},{16,0},{32,48},{48,32},{1,17},{17,1},{33,49},{49,33},{2,18}... | collective-permute-start | bytes 331784 | tf_op jit(solution)/shard_map/ppermute | solution.py:400
  97.8 5.9 %collective-permute-start.17 = (bf16[216,128]{1,0:T(8,128)(2,1)S(1)}, bf16[216,128]{1,0:T(8,128)(2,1)S(1)}, u32[]{:S(2)}, u32[]{:S(2)}) collective-permute-start(bf16[216,128]{1,0:T(8,128)(2,1)S(1)} %get-tuple-element.102), channel_id=1, source_target_pairs={{0,12},{2,50},{4,8},{6,54},{8,4},{10,58},{12,0},{14,62},{16,28},{1... | collective-permute-start | bytes 165896 | tf_op jit(solution)/shard_map/ppermute | solution.py:478
  99.2 4.6 %collective-permute-start.18 = (bf16[216,128]{1,0:T(8,128)(2,1)S(1)}, bf16[216,128]{1,0:T(8,128)(2,1)S(1)}, u32[]{:S(2)}, u32[]{:S(2)}) collective-permute-start(bf16[216,128]{1,0:T(8,128)(2,1)S(1)} %get-tuple-element.103), channel_id=1, source_target_pairs={{0,2},{2,0},{4,6},{6,4},{8,10},{10,8},{12,14},{14,12},{16,18},{18,... | collective-permute-start | bytes 165896 | tf_op jit(solution)/shard_map/ppermute | solution.py:479
  101.7 6.3 %collective-permute-start.19 = (bf16[216,128]{1,0:T(8,128)(2,1)S(1)}, bf16[216,128]{1,0:T(8,128)(2,1)S(1)}, u32[]{:S(2)}, u32[]{:S(2)}) collective-permute-start(bf16[216,128]{1,0:T(8,128)(2,1)S(1)} %get-tuple-element.104), channel_id=1, source_target_pairs={{0,50},{2,12},{4,54},{6,8},{8,58},{10,4},{12,62},{14,0},{16,34},{1... | collective-permute-start | bytes 165896 | tf_op jit(solution)/shard_map/ppermute | solution.py:480

commit v4 on v3

--- a/solution.py
+++ b/solution.py
@@ -415,7 +415,8 @@
     column, to_pair, to_next = lax.optimization_barrier((column, kept, other))
     next_kept = lax.ppermute(to_pair, "zl", SWAP)
     next_other = lax.ppermute(to_next, ring, [(i, (i + 1) % 8 if i % 2 else (i + 7) % 8) for i in range(8)])
-    pieces = [column] + [swap(column, "grp", d) for d in (1, 2, 3)]
+    first, third, second = (swap(column, "grp", d) for d in (1, 3, 2))
+    pieces = [column, first, second, third]
 
     built = [build_call(place, column, halves[0], halves[1], parts, turns, "build_here", 6 * 10**9)]
     next_kept, next_other, _ = lax.optimization_barrier((next_kept, next_other, built[0][8]))
@@ -424,7 +425,7 @@
     shifted = [b[:8] for b in built]
     tokens = [b[8] for b in built]
     power = call(weigh_kernel((0,)), "weigh_own", shape(GROUPS, WIDTH), (place, ctf, tokens[0], column), LIMIT, 10**8)
-    power = call(weigh_kernel((1, 2, 3)), "weigh", shape(GROUPS, WIDTH), (place, ctf, power, *pieces[1:], *tokens[1:]), LIMIT)
+    power = call(weigh_kernel((1, 3, 2)), "weigh", shape(GROUPS, WIDTH), (place, ctf, power, pieces[1], pieces[3], pieces[2], *tokens[1:]), LIMIT)
     score = shape(2, ROWS, WIDE)
     flops = 4 * ROWS * WIDE * DEPTH
     given = call(score_kernel(1), "score_given", score, (place, power, halves[1], halves[3], *pieces, *shifted[0], *shifted[1]), LIMIT, flops)

time: 109 us -> 107 us (0.982)
  waiting for transfers between devices: 20.2 us -> 16.4 us
  starting transfers between devices: 28.2 us -> 29.5 us
    ppermute x11, waiting for transfers between devices: 9.31 us -> 6.67 us  [swap(): return lax.ppermute(value, axis, [(i, i ^ d) for i in range(n)])]
    ppermute x1, starting transfers between devices: 0.67 us -> 2.09 us  [body(): lax.ppermute(sent[2], plane, [(number(i, j, k), number(*turn(i, j, 1 - k)...]
  transfers between devices with their start and end apart: 21 -> 21, of which waited for: 12 -> 10; matrix products, arithmetic and copies ran while one was open for 1% -> 1% of each run, Pallas kernels for 25% -> 25%
where the time goes in v4:
time: 107 us
  Pallas kernels  42.7 us (40%)
  starting transfers between devices  29.5 us (28%)
  waiting for transfers between devices  16.4 us (15%)
  blocking collectives  15.4 us (14%)
  between operations  1.45 us (1%)
  local copies, waits for them, and re-layouts  1.17 us (1%)
    pallas_call x12, Pallas kernels, call(): pl.pallas_call(kernel, name=name, in_specs=[SMEM] + [VMEM] * (len(args) -...  27.1 us
    all_to_all x1, blocking collectives, body(): stats = lax.all_to_all(stats, ring, 0, 0, tiled=True)  15.4 us
    ppermute x11, starting transfers between devices, swap(): return lax.ppermute(value, axis, [(i, i ^ d) for i in range(n)])  13.8 us
    pallas_call x2, Pallas kernels, build_call(): pl.pallas_call(build_kernel, name=name, in_specs=[SMEM] + [VMEM] * 5, out...  10.1 us
    ppermute x11, waiting for transfers between devices, swap(): return lax.ppermute(value, axis, [(i, i ^ d) for i in range(n)])  6.67 us
    all_to_all x1, starting transfers between devices, body(): column = lax.all_to_all(spread_call(stacks), ('y', 'zl'), 0, 0, tiled=True)  5.94 us
    all_to_all x1, waiting for transfers between devices, body(): column = lax.all_to_all(spread_call(stacks), ('y', 'zl'), 0, 0, tiled=True)  4.15 us
    ppermute x1, waiting for transfers between devices, body(): lax.ppermute(sent[2], plane, [(number(i, j, k), number(*turn(i, j, 1 - k)...  3.66 us
  transfers between devices with their start and end apart: 21, of which 10 were waited for; matrix products, arithmetic and copies ran while one was open for 1% of the time, Pallas kernels for 25%

profile of v4, /device:TPU:32, one launch (start us, length us, event | category | flops | bytes accessed | tf_op | source)
XLA Modules:
  0.0 106.8 jit_solution(1860283768569181533)
XLA Ops:
  0.6 1.7 %spread.1 = bf16[8,200,128]{2,1,0:T(8,128)(2,1)} custom-call(bf16[2,200,128]{2,1,0:T(8,128)(2,1)} %bitcast.7), custom_call_target="tpu_custom_call" | custom-call | tf_op jit(solution)/shard_map/spread/pallas_call | solution.py:83
  2.3 5.9 %all-to-all-start = ((bf16[8,200,128]{2,1,0:T(8,128)(2,1)}), bf16[8,200,128]{2,1,0:T(8,128)(2,1)S(1)}, u32[]{:S(2)}, u32[]{:S(2)}) async-start(bf16[8,200,128]{2,1,0:T(8,128)(2,1)} %spread.1), calls=%async_computation | async-start | bytes 819200 | tf_op jit(solution)/shard_map/all_to_all | solution.py:409
  9.7 2.0 %split.1 = (bf16[40,4224]{1,0:T(8,128)(2,1)S(1)}, bf16[40,4224]{1,0:T(8,128)(2,1)S(1)}, bf16[48,4096]{1,0:T(8,128)(2,1)S(1)}, f32[24,4096]{1,0:T(8,128)S(1)}, f32[8,4096]{1,0:T(8,128)S(1)}) custom-call(s32[4]{0:T(128)S(1)} %pad_add_fusion.place, s32[40]{0:T(128)S(1)} %copy-done, s32[1]{0:T(128)S(6)} %copy.9.count, bf16[40,8192]{1,0:T(8,128)(2,1)} %images.1, ...), custom_call_target="tpu_custom_call" | custom-call | tf_op jit(solution)/shard_map/split/pallas_call | solution.py:129
  11.8 4.1 %all-to-all-done.after.refs_0_ = bf16[8,200,128]{2,1,0:T(8,128)(2,1)S(1)} async-done(((bf16[8,200,128]{2,1,0:T(8,128)(2,1)}), bf16[8,200,128]{2,1,0:T(8,128)(2,1)S(1)}, u32[]{:S(2)}, u32[]{:S(2)}) %all-to-all-start) | async-done | bytes 409632 | tf_op jit(solution)/shard_map/all_to_all | solution.py:409
  16.0 1.5 %collective-permute-start.1 = (bf16[8,200,128]{2,1,0:T(8,128)(2,1)S(1)}, bf16[8,200,128]{2,1,0:T(8,128)(2,1)S(1)}, u32[]{:S(2)}, u32[]{:S(2)}) collective-permute-start(bf16[8,200,128]{2,1,0:T(8,128)(2,1)S(1)} %all-to-all-done.after.refs_0_), channel_id=1, source_target_pairs={{0,16},{16,0},{32,48},{48,32},{1,17},{17,1},{33,49},{49,33},{2,18}... | collective-permute-start | bytes 1228808 | tf_op jit(solution)/shard_map/ppermute | solution.py:400
  17.5 2.1 %collective-permute-start.2 = (bf16[8,200,128]{2,1,0:T(8,128)(2,1)S(1)}, bf16[8,200,128]{2,1,0:T(8,128)(2,1)S(1)}, u32[]{:S(2)}, u32[]{:S(2)}) collective-permute-start(bf16[8,200,128]{2,1,0:T(8,128)(2,1)S(1)} %all-to-all-done.after.refs_0_), channel_id=1, source_target_pairs={{0,48},{16,32},{32,16},{48,0},{1,49},{17,33},{33,17},{49,1},{2,50}... | collective-permute-start | bytes 1228808 | tf_op jit(solution)/shard_map/ppermute | solution.py:400
  20.2 1.2 %collective-permute-start.4 = (bf16[40,4224]{1,0:T(8,128)(2,1)S(1)}, bf16[40,4224]{1,0:T(8,128)(2,1)S(1)}, u32[]{:S(2)}, u32[]{:S(2)}) collective-permute-start(bf16[40,4224]{1,0:T(8,128)(2,1)S(1)} %get-tuple-element.62.images_a.meta_a), channel_id=1, source_target_pairs={{0,2},{2,0},{1,3},{3,1},{4,6},{6,4},{5,7},{7,5},{8,10},{10,8},{9,1... | collective-permute-start | bytes 1013768 | tf_op jit(solution)/shard_map/ppermute | solution.py:416
  21.4 2.7 %collective-permute-start.5 = (bf16[40,4224]{1,0:T(8,128)(2,1)S(1)}, bf16[40,4224]{1,0:T(8,128)(2,1)S(1)}, u32[]{:S(2)}, u32[]{:S(2)}) collective-permute-start(bf16[40,4224]{1,0:T(8,128)(2,1)S(1)} %get-tuple-element.63), channel_id=1, source_target_pairs={{0,194},{2,64},{64,2},{66,128},{128,66},{130,192},{192,130},{194,0... | collective-permute-start | bytes 1013768 | tf_op jit(solution)/shard_map/ppermute | solution.py:417
  24.0 5.1 %build_here.1 = (bf16[2,1024,512]{2,1,0:T(8,128)(2,1)S(1)}, bf16[2,1024,512]{2,1,0:T(8,128)(2,1)S(1)}, bf16[2,1024,512]{2,1,0:T(8,128)(2,1)S(1)}, bf16[2,1024,51...) custom-call(s32[4]{0:T(128)S(1)} %pad_add_fusion.place, ...), custom_call_target="tpu_custom_call" | custom-call | flops 6000000000 | bytes 100000 | tf_op jit(solution)/shard_map/build_here/pallas_call | solution.py:190
  29.6 0.9 weigh_own.1.after
  31.3 5.1 %build_next.1 = (bf16[2,1024,512]{2,1,0:T(8,128)(2,1)S(1)}, bf16[2,1024,512]{2,1,0:T(8,128)(2,1)S(1)}, bf16[2,1024,512]{2,1,0:T(8,128)(2,1)S(1)}, bf16[2,1024,51...) custom-call(s32[4]{0:T(128)S(1)} %pad_add_fusion.place, ...), custom_call_target="tpu_custom_call" | custom-call | flops 100000000 | bytes 100000 | tf_op jit(solution)/shard_map/build_next/pallas_call | solution.py:190
  36.9 1.5 %weigh.1.power = f32[8,200]{1,0:T(8,128)S(1)} custom-call(s32[4]{0:T(128)S(1)} %pad_add_fusion.place, f32[8,4096]{1,0:T(8,128)S(1)} %get-tuple-element.55.ctf, f32[8,200]{1,0:T(8,128)S(1)} %weigh_own.1.after, bf16[8,200,128]{2,1,0:T(8,128)(2,1)S(1)} %collective-permute-done.1.refs_0_.refs_1_, ...), custom_call_target="tpu_custom_call" | custom-call | tf_op jit(solution)/shard_map/weigh/pallas_call | solution.py:48
  38.4 5.2 %score_given.1 = f32[2,1024,256]{2,1,0:T(8,128)S(1)} custom-call(s32[4]{0:T(128)S(1)} %pad_add_fusion.place, f32[8,200]{1,0:T(8,128)S(1)} %weigh.1.power, bf16[40,4224]{1,0:T(8,128)(2,1)S(1)} %collective-permute-done.images_b.meta_a, bf16[40,4224]{1,0:T(8,128)(2,1)S(1)} %collective-permute-done.6.images_b.meta_b, ...), custom_call_target="tpu_custom_call" | custom-call | flops 4294967296 | tf_op jit(solution)/shard_map/score_given/pallas_call | solution.py:48
  43.7 5.2 %score_own.1.mine = f32[2,1024,256]{2,1,0:T(8,128)S(1)} custom-call(s32[4]{0:T(128)S(1)} %pad_add_fusion.place, f32[8,200]{1,0:T(8,128)S(1)} %weigh.1.power, bf16[40,4224]{1,0:T(8,128)(2,1)S(1)} %get-tuple-element.62.images_a.meta_a, bf16[40,4224]{1,0:T(8,128)(2,1)S(1)} %collective-permute-done.4.images_a.meta_b, ...), custom_call_target="tpu_custom_call" | custom-call | flops 4294967296 | tf_op jit(solution)/shard_map/score_own/pallas_call | solution.py:48
  48.9 1.3 %settle.1 = f32[8,8,128]{2,1,0:T(8,128)S(1)} custom-call(s32[4]{0:T(128)S(1)} %pad_add_fusion.place, f32[2,1024,256]{2,1,0:T(8,128)S(1)} %score_own.1.mine, f32[2,1024,256]{2,1,0:T(8,128)S(1)} %collective-permute-done.7.theirs), custom_call_target="tpu_custom_call" | custom-call | tf_op jit(solution)/shard_map/settle/pallas_call | solution.py:48
  50.1 15.4 %all_to_all.10.stats = f32[8,8,128]{2,1,0:T(8,128)S(1)} all-to-all(f32[8,8,128]{2,1,0:T(8,128)S(1)} %settle.1), channel_id=1, replica_groups=mesh['cls'=4,'grp'=4,'y'=4,'zl'=2,'core'=2] {'cls','zl'}, dimensions={0} | all-to-all | bytes 65536 | tf_op jit(solution)/shard_map/all_to_all | solution.py:435
  65.5 1.7 %posterior.1 = (bf16[2,200,1024]{2,1,0:T(8,128)(2,1)S(1)}, f32[8,40]{1,0:T(8,128)S(1)}) custom-call(s32[4]{0:T(128)S(1)} %pad_add_fusion.place, f32[2,1024,256]{2,1,0:T(8,128)S(1)} %score_own.1.mine, f32[2,1024,256]{2,1,0:T(8,128)S(1)} %collective-permute-done.7.theirs, f32[8,8,128]{2,1,0:T(8,128)S(1)} %all_to_all.10.stats, ...), custom_call_target="tpu_custom_call" | custom-call | tf_op jit(solution)/shard_map/posterior/pallas_call | solution.py:315
  67.5 1.6 %insert_begin.1 = (f32[4,200,128]{2,1,0:T(8,128)S(1)}, f32[4,200,128]{2,1,0:T(8,128)S(1)}) custom-call(s32[4]{0:T(128)S(1)} %pad_add_fusion.place, bf16[2,200,1024]{2,1,0:T(8,128)(2,1)S(1)} %get-tuple-element.84.mine, bf16[2,1024,512]{2,1,0:T(8,128)(2,1)S(1)} %get-tuple-element.69.refs_6_.a0.refs_2_, ...), custom_call_target="tpu_custom_call" | custom-call | flops 1073741824 | tf_op jit(solution)/shard_map/insert_begin/pallas_call | solution.py:48
  69.9 1.6 %insert_far.1 = (bf16[4,216,128]{2,1,0:T(8,128)(2,1)S(1)}, bf16[4,216,128]{2,1,0:T(8,128)(2,1)S(1)}, f32[8,128]{1,0:T(8,128)S(1)}) custom-call(s32[4]{0:T(128)S(1)} %pad_add_fusion.place, f32[8,40]{1,0:T(8,128)S(1)} %get-tuple-element.83.after, bf16[2,200,1024]{2,1,0:T(8,128)(2,1)S(1)} %get-tuple-element.84.mine, ...), custom_call_target="tpu_custom_call" | custom-call | flops 1073741824 | tf_op jit(solution)/shard_map/insert_far/pallas_call | solution.py:48
  71.5 1.0 collective-permute-start.10
  72.5 2.6 %collective-permute-start.9 = (bf16[4,216,128]{2,1,0:T(8,128)(2,1)S(1)}, bf16[4,216,128]{2,1,0:T(8,128)(2,1)S(1)}, u32[]{:S(2)}, u32[]{:S(2)}) collective-permute-start(bf16[4,216,128]{2,1,0:T(8,128)(2,1)S(1)} %get-tuple-element.89), channel_id=1, source_target_pairs={{0,32},{16,48},{32,0},{48,16},{1,33},{17,49},{33,1},{49,17},{2,34}... | collective-permute-start | bytes 663560 | tf_op jit(solution)/shard_map/ppermute | solution.py:400
  75.1 4.3 %insert_near.1 = (bf16[4,216,128]{2,1,0:T(8,128)(2,1)S(1)}, bf16[4,216,128]{2,1,0:T(8,128)(2,1)S(1)}, bf16[4,216,128]{2,1,0:T(8,128)(2,1)S(1)}, bf16[4,216,128]{2,1,0:T(8,128)(2,1)S(1)}, f32[8,128]{1,0:T(8,128)S(1)}) custom-call(s32[4]{0:T(128)S(1)} %pad_add_fusion.place, f32[8,128]{1,0:T(8,128)S(1)} %get-tuple-element.87.after, ...), custom_call_target="tpu_custom_call" | custom-call | flops 4294967296 | tf_op jit(solution)/shard_map/insert_near/pallas_call | solution.py:48
  80.7 1.1 %collective-permute-start.13 = (bf16[4,216,128]{2,1,0:T(8,128)(2,1)S(1)}, bf16[4,216,128]{2,1,0:T(8,128)(2,1)S(1)}, u32[]{:S(2)}, u32[]{:S(2)}) collective-permute-start(bf16[4,216,128]{2,1,0:T(8,128)(2,1)S(1)} %get-tuple-element.95), channel_id=1, source_target_pairs={{0,48},{16,32},{32,16},{48,0},{1,49},{17,33},{33,17},{49,1},{2,50}... | collective-permute-start | bytes 663560 | tf_op jit(solution)/shard_map/ppermute | solution.py:400
  81.8 2.4 %collective-permute-start.14 = (bf16[4,216,128]{2,1,0:T(8,128)(2,1)S(1)}, bf16[4,216,128]{2,1,0:T(8,128)(2,1)S(1)}, u32[]{:S(2)}, u32[]{:S(2)}) collective-permute-start(bf16[4,216,128]{2,1,0:T(8,128)(2,1)S(1)} %get-tuple-element.96), channel_id=1, source_target_pairs={{0,12},{4,8},{8,4},{12,0},{1,13},{5,9},{9,5},{13,1},{2,14},{6,10},... | collective-permute-start | bytes 663560 | tf_op jit(solution)/shard_map/ppermute | solution.py:400
  84.2 3.0 %insert_own.1 = (f32[4,216,128]{2,1,0:T(8,128)S(1)}, f32[4,216,128]{2,1,0:T(8,128)S(1)}, f32[8,128]{1,0:T(8,128)}) custom-call(s32[4]{0:T(128)S(1)} %pad_add_fusion.place, f32[8,128]{1,0:T(8,128)S(1)} %get-tuple-element.88.after, bf16[2,200,1024]{2,1,0:T(8,128)(2,1)S(1)} %get-tuple-element.84.mine, bf16[2,200,1024]{2,1,0:T(8,128)(2,1)S(1)} %collective-permute-done.8.theirs, ...), custom_call_target="tpu_custom_call" | custom-call | flops 2147483648 | tf_op jit(solution)/shard_map/insert_own/pallas_call | solution.py:48
  87.2 1.1 collective-permute-done.13.three_a
  91.0 3.7 %collective-permute-done.15.got_a = bf16[2,216,128]{2,1,0:T(8,128)(2,1)S(1)} collective-permute-done((bf16[2,216,128]{2,1,0:T(8,128)(2,1)S(1)}, bf16[2,216,128]{2,1,0:T(8,128)(2,1)S(1)}, u32[]{:S(2)}, u32[]{:S(2)}) %collective-permute-start.15) | collective-permute-done | bytes 110624 | tf_op jit(solution)/shard_map/ppermute | solution.py:400
  95.9 1.8 %collective-permute-start.17 = (bf16[216,128]{1,0:T(8,128)(2,1)S(1)}, bf16[216,128]{1,0:T(8,128)(2,1)S(1)}, u32[]{:S(2)}, u32[]{:S(2)}) collective-permute-start(bf16[216,128]{1,0:T(8,128)(2,1)S(1)} %get-tuple-element.102), channel_id=1, source_target_pairs={{0,12},{2,50},{4,8},{6,54},{8,4},{10,58},{12,0},{14,62},{16,28},{1... | collective-permute-start | bytes 165896 | tf_op jit(solution)/shard_map/ppermute | solution.py:479
  97.7 1.6 %collective-permute-start.18 = (bf16[216,128]{1,0:T(8,128)(2,1)S(1)}, bf16[216,128]{1,0:T(8,128)(2,1)S(1)}, u32[]{:S(2)}, u32[]{:S(2)}) collective-permute-start(bf16[216,128]{1,0:T(8,128)(2,1)S(1)} %get-tuple-element.103), channel_id=1, source_target_pairs={{0,2},{2,0},{4,6},{6,4},{8,10},{10,8},{12,14},{14,12},{16,18},{18,... | collective-permute-start | bytes 165896 | tf_op jit(solution)/shard_map/ppermute | solution.py:480
  99.3 2.1 %collective-permute-start.19 = (bf16[216,128]{1,0:T(8,128)(2,1)S(1)}, bf16[216,128]{1,0:T(8,128)(2,1)S(1)}, u32[]{:S(2)}, u32[]{:S(2)}) collective-permute-start(bf16[216,128]{1,0:T(8,128)(2,1)S(1)} %get-tuple-element.104), channel_id=1, source_target_pairs={{0,50},{2,12},{4,54},{6,8},{8,58},{10,4},{12,62},{14,0},{16,34},{1... | collective-permute-start | bytes 165896 | tf_op jit(solution)/shard_map/ppermute | solution.py:481
  101.9 3.7 %collective-permute-done.19.across = bf16[216,128]{1,0:T(8,128)(2,1)S(1)} collective-permute-done((bf16[216,128]{1,0:T(8,128)(2,1)S(1)}, bf16[216,128]{1,0:T(8,128)(2,1)S(1)}, u32[]{:S(2)}, u32[]{:S(2)}) %collective-permute-start.19) | collective-permute-done | bytes 55328 | tf_op jit(solution)/shard_map/ppermute | solution.py:481
  105.5 1.2 %finish.1 = (f32[2,200,128]{2,1,0:T(8,128)}, f32[2,8,200]{2,1,0:T(8,128)}) custom-call(s32[4]{0:T(128)S(1)} %pad_add_fusion.place, f32[216,128]{1,0:T(8,128)S(1)} %get-tuple-element.101.stay, bf16[216,128]{1,0:T(8,128)(2,1)S(1)} %collective-permute-done.17.same, bf16[216,128]{1,0:T(8,128)(2,1)S(1)} %collective-permute-done.18.other, ...), custom_call_target="tpu_custom_call" | custom-call | tf_op jit(solution)/shard_map/finish/pallas_call | solution.py:48
  (32 shorter events, 10.1 us)
Async XLA Ops:
  2.3 13.6 %all-to-all-start = ((bf16[8,200,128]{2,1,0:T(8,128)(2,1)}), bf16[8,200,128]{2,1,0:T(8,128)(2,1)S(1)}, u32[]{:S(2)}, u32[]{:S(2)}) async-start(bf16[8,200,128]{2,1,0:T(8,128)(2,1)} %spread.1), calls=%async_computation | async-start | bytes 819200 | tf_op jit(solution)/shard_map/all_to_all | solution.py:409
  9.0 0.7 copy-start
  11.7 9.6 %collective-permute-start = (bf16[40,4224]{1,0:T(8,128)(2,1)S(1)}, bf16[40,4224]{1,0:T(8,128)(2,1)S(1)}, u32[]{:S(2)}, u32[]{:S(2)}) collective-permute-start(bf16[40,4224]{1,0:T(8,128)(2,1)S(1)} %get-tuple-element.63), channel_id=1, source_target_pairs={{0,1},{1,0},{2,3},{3,2},{4,5},{5,4},{6,7},{7,6},{8,9},{9,8},{10,11... | collective-permute-start | bytes 1013768 | tf_op jit(solution)/shard_map/ppermute | solution.py:413
  16.0 20.4 %collective-permute-start.1 = (bf16[8,200,128]{2,1,0:T(8,128)(2,1)S(1)}, bf16[8,200,128]{2,1,0:T(8,128)(2,1)S(1)}, u32[]{:S(2)}, u32[]{:S(2)}) collective-permute-start(bf16[8,200,128]{2,1,0:T(8,128)(2,1)S(1)} %all-to-all-done.after.refs_0_), channel_id=1, source_target_pairs={{0,16},{16,0},{32,48},{48,32},{1,17},{17,1},{33,49},{49,33},{2,18}... | collective-permute-start | bytes 1228808 | tf_op jit(solution)/shard_map/ppermute | solution.py:400
  17.5 19.4 %collective-permute-start.2 = (bf16[8,200,128]{2,1,0:T(8,128)(2,1)S(1)}, bf16[8,200,128]{2,1,0:T(8,128)(2,1)S(1)}, u32[]{:S(2)}, u32[]{:S(2)}) collective-permute-start(bf16[8,200,128]{2,1,0:T(8,128)(2,1)S(1)} %all-to-all-done.after.refs_0_), channel_id=1, source_target_pairs={{0,48},{16,32},{32,16},{48,0},{1,49},{17,33},{33,17},{49,1},{2,50}... | collective-permute-start | bytes 1228808 | tf_op jit(solution)/shard_map/ppermute | solution.py:400
  19.6 17.3 %collective-permute-start.3 = (bf16[8,200,128]{2,1,0:T(8,128)(2,1)S(1)}, bf16[8,200,128]{2,1,0:T(8,128)(2,1)S(1)}, u32[]{:S(2)}, u32[]{:S(2)}) collective-permute-start(bf16[8,200,128]{2,1,0:T(8,128)(2,1)S(1)} %all-to-all-done.after.refs_0_), channel_id=1, source_target_pairs={{0,32},{16,48},{32,0},{48,16},{1,33},{17,49},{33,1},{49,17},{2,34}... | collective-permute-start | bytes 1228808 | tf_op jit(solution)/shard_map/ppermute | solution.py:400
  20.2 8.9 %collective-permute-start.4 = (bf16[40,4224]{1,0:T(8,128)(2,1)S(1)}, bf16[40,4224]{1,0:T(8,128)(2,1)S(1)}, u32[]{:S(2)}, u32[]{:S(2)}) collective-permute-start(bf16[40,4224]{1,0:T(8,128)(2,1)S(1)} %get-tuple-element.62.images_a.meta_a), channel_id=1, source_target_pairs={{0,2},{2,0},{1,3},{3,1},{4,6},{6,4},{5,7},{7,5},{8,10},{10,8},{9,1... | collective-permute-start | bytes 1013768 | tf_op jit(solution)/shard_map/ppermute | solution.py:416
  21.4 8.3 %collective-permute-start.5 = (bf16[40,4224]{1,0:T(8,128)(2,1)S(1)}, bf16[40,4224]{1,0:T(8,128)(2,1)S(1)}, u32[]{:S(2)}, u32[]{:S(2)}) collective-permute-start(bf16[40,4224]{1,0:T(8,128)(2,1)S(1)} %get-tuple-element.63), channel_id=1, source_target_pairs={{0,194},{2,64},{64,2},{66,128},{128,66},{130,192},{192,130},{194,0... | collective-permute-start | bytes 1013768 | tf_op jit(solution)/shard_map/ppermute | solution.py:417
  29.6 1.6 %collective-permute-start.6 = (bf16[40,4224]{1,0:T(8,128)(2,1)S(1)}, bf16[40,4224]{1,0:T(8,128)(2,1)S(1)}, u32[]{:S(2)}, u32[]{:S(2)}) collective-permute-start(bf16[40,4224]{1,0:T(8,128)(2,1)S(1)} %collective-permute-done.5), channel_id=1, source_target_pairs={{0,1},{1,0},{2,3},{3,2},{4,5},{5,4},{6,7},{7,6},{8,9},{9,8},{10,11... | collective-permute-start | bytes 1013768 | tf_op jit(solution)/shard_map/ppermute | solution.py:423
  43.6 5.3 %collective-permute-start.7 = (f32[2,1024,256]{2,1,0:T(8,128)S(1)}, f32[2,1024,256]{2,1,0:T(8,128)S(1)}, u32[]{:S(2)}, u32[]{:S(2)}) collective-permute-start(f32[2,1024,256]{2,1,0:T(8,128)S(1)} %score_given.1), channel_id=1, source_target_pairs={{0,1},{1,0},{2,3},{3,2},{4,5},{5,4},{6,7},{7,6},{8,9},{9,8},{10,11... | collective-permute-start | bytes 6291464 | tf_op jit(solution)/shard_map/ppermute | solution.py:432
  67.2 2.6 %collective-permute-start.8 = (bf16[2,200,1024]{2,1,0:T(8,128)(2,1)S(1)}, bf16[2,200,1024]{2,1,0:T(8,128)(2,1)S(1)}, u32[]{:S(2)}, u32[]{:S(2)}) collective-permute-start(bf16[2,200,1024]{2,1,0:T(8,128)(2,1)S(1)} %get-tuple-element.84.mine), channel_id=1, source_target_pairs={{0,1},{1,0},{2,3},{3,2},{4,5},{5,4},{6,7},{7,6},{8,9},{9,8},{10,11... | collective-permute-start | bytes 2457608 | tf_op jit(solution)/shard_map/ppermute | solution.py:437
  71.5 10.3 %collective-permute-start.10 = (bf16[4,216,128]{2,1,0:T(8,128)(2,1)S(1)}, bf16[4,216,128]{2,1,0:T(8,128)(2,1)S(1)}, u32[]{:S(2)}, u32[]{:S(2)}) collective-permute-start(bf16[4,216,128]{2,1,0:T(8,128)(2,1)S(1)} %get-tuple-element.90), channel_id=1, source_target_pairs={{0,8},{4,12},{8,0},{12,4},{1,9},{5,13},{9,1},{13,5},{2,10},{6,14},... | collective-permute-start | bytes 663560 | tf_op jit(solution)/shard_map/ppermute | solution.py:400
  72.5 11.7 %collective-permute-start.9 = (bf16[4,216,128]{2,1,0:T(8,128)(2,1)S(1)}, bf16[4,216,128]{2,1,0:T(8,128)(2,1)S(1)}, u32[]{:S(2)}, u32[]{:S(2)}) collective-permute-start(bf16[4,216,128]{2,1,0:T(8,128)(2,1)S(1)} %get-tuple-element.89), channel_id=1, source_target_pairs={{0,32},{16,48},{32,0},{48,16},{1,33},{17,49},{33,1},{49,17},{2,34}... | collective-permute-start | bytes 663560 | tf_op jit(solution)/shard_map/ppermute | solution.py:400
  79.4 7.8 %collective-permute-start.11 = (bf16[4,216,128]{2,1,0:T(8,128)(2,1)S(1)}, bf16[4,216,128]{2,1,0:T(8,128)(2,1)S(1)}, u32[]{:S(2)}, u32[]{:S(2)}) collective-permute-start(bf16[4,216,128]{2,1,0:T(8,128)(2,1)S(1)} %get-tuple-element.93), channel_id=1, source_target_pairs={{0,16},{16,0},{32,48},{48,32},{1,17},{17,1},{33,49},{49,33},{2,18}... | collective-permute-start | bytes 663560 | tf_op jit(solution)/shard_map/ppermute | solution.py:400
  80.1 7.1 %collective-permute-start.12 = (bf16[4,216,128]{2,1,0:T(8,128)(2,1)S(1)}, bf16[4,216,128]{2,1,0:T(8,128)(2,1)S(1)}, u32[]{:S(2)}, u32[]{:S(2)}) collective-permute-start(bf16[4,216,128]{2,1,0:T(8,128)(2,1)S(1)} %get-tuple-element.94), channel_id=1, source_target_pairs={{0,4},{4,0},{8,12},{12,8},{1,5},{5,1},{9,13},{13,9},{2,6},{6,2},{1... | collective-permute-start | bytes 663560 | tf_op jit(solution)/shard_map/ppermute | solution.py:400
  80.7 7.6 %collective-permute-start.13 = (bf16[4,216,128]{2,1,0:T(8,128)(2,1)S(1)}, bf16[4,216,128]{2,1,0:T(8,128)(2,1)S(1)}, u32[]{:S(2)}, u32[]{:S(2)}) collective-permute-start(bf16[4,216,128]{2,1,0:T(8,128)(2,1)S(1)} %get-tuple-element.95), channel_id=1, source_target_pairs={{0,48},{16,32},{32,16},{48,0},{1,49},{17,33},{33,17},{49,1},{2,50}... | collective-permute-start | bytes 663560 | tf_op jit(solution)/shard_map/ppermute | solution.py:400
  81.8 7.3 %collective-permute-start.14 = (bf16[4,216,128]{2,1,0:T(8,128)(2,1)S(1)}, bf16[4,216,128]{2,1,0:T(8,128)(2,1)S(1)}, u32[]{:S(2)}, u32[]{:S(2)}) collective-permute-start(bf16[4,216,128]{2,1,0:T(8,128)(2,1)S(1)} %get-tuple-element.96), channel_id=1, source_target_pairs={{0,12},{4,8},{8,4},{12,0},{1,13},{5,9},{9,5},{13,1},{2,14},{6,10},... | collective-permute-start | bytes 663560 | tf_op jit(solution)/shard_map/ppermute | solution.py:400
  89.8 4.8 %collective-permute-start.15 = (bf16[2,216,128]{2,1,0:T(8,128)(2,1)S(1)}, bf16[2,216,128]{2,1,0:T(8,128)(2,1)S(1)}, u32[]{:S(2)}, u32[]{:S(2)}) collective-permute-start(bf16[2,216,128]{2,1,0:T(8,128)(2,1)S(1)} %get-tuple-element.99), channel_id=1, source_target_pairs={{0,4},{4,0},{8,12},{12,8},{1,5},{5,1},{9,13},{13,9},{2,6},{6,2},{1... | collective-permute-start | bytes 331784 | tf_op jit(solution)/shard_map/ppermute | solution.py:400
  90.5 4.7 %collective-permute-start.16 = (bf16[2,216,128]{2,1,0:T(8,128)(2,1)S(1)}, bf16[2,216,128]{2,1,0:T(8,128)(2,1)S(1)}, u32[]{:S(2)}, u32[]{:S(2)}) collective-permute-start(bf16[2,216,128]{2,1,0:T(8,128)(2,1)S(1)} %get-tuple-element.100), channel_id=1, source_target_pairs={{0,16},{16,0},{32,48},{48,32},{1,17},{17,1},{33,49},{49,33},{2,18}... | collective-permute-start | bytes 331784 | tf_op jit(solution)/shard_map/ppermute | solution.py:400
  95.9 6.0 %collective-permute-start.17 = (bf16[216,128]{1,0:T(8,128)(2,1)S(1)}, bf16[216,128]{1,0:T(8,128)(2,1)S(1)}, u32[]{:S(2)}, u32[]{:S(2)}) collective-permute-start(bf16[216,128]{1,0:T(8,128)(2,1)S(1)} %get-tuple-element.102), channel_id=1, source_target_pairs={{0,12},{2,50},{4,8},{6,54},{8,4},{10,58},{12,0},{14,62},{16,28},{1... | collective-permute-start | bytes 165896 | tf_op jit(solution)/shard_map/ppermute | solution.py:479
  97.7 4.2 %collective-permute-start.18 = (bf16[216,128]{1,0:T(8,128)(2,1)S(1)}, bf16[216,128]{1,0:T(8,128)(2,1)S(1)}, u32[]{:S(2)}, u32[]{:S(2)}) collective-permute-start(bf16[216,128]{1,0:T(8,128)(2,1)S(1)} %get-tuple-element.103), channel_id=1, source_target_pairs={{0,2},{2,0},{4,6},{6,4},{8,10},{10,8},{12,14},{14,12},{16,18},{18,... | collective-permute-start | bytes 165896 | tf_op jit(solution)/shard_map/ppermute | solution.py:480
  99.3 6.3 %collective-permute-start.19 = (bf16[216,128]{1,0:T(8,128)(2,1)S(1)}, bf16[216,128]{1,0:T(8,128)(2,1)S(1)}, u32[]{:S(2)}, u32[]{:S(2)}) collective-permute-start(bf16[216,128]{1,0:T(8,128)(2,1)S(1)} %get-tuple-element.104), channel_id=1, source_target_pairs={{0,50},{2,12},{4,54},{6,8},{8,58},{10,4},{12,62},{14,0},{16,34},{1... | collective-permute-start | bytes 165896 | tf_op jit(solution)/shard_map/ppermute | solution.py:481

commit v5 on v4

--- a/solution.py
+++ b/solution.py
@@ -388,7 +388,7 @@
         out[...] = (jnp.where(side, odd, even) if turned else jnp.where(side, even, odd)).astype(out.dtype)
 
 
-def finish_kernel(place, stay, same, other, across, insertions, weights):
+def finish_kernel(place, stay, same, across, other, insertions, weights):
     mine = stay[...] + same[...].astype(F32)
     theirs = other[...].astype(F32) + across[...].astype(F32)
     for k, sums in ((place[2], mine), (1 - place[2], theirs)):
@@ -477,9 +477,9 @@
         return (i, j ^ 3) if side == 0 else (i ^ 3, j)
 
     same = lax.ppermute(sent[0], plane, [(number(i, j, k), number(*turn(i, j, k), k)) for i, j, k in spots])
+    across = lax.ppermute(sent[2], plane, [(number(i, j, k), number(*turn(i, j, 1 - k), 1 - k)) for i, j, k in spots])
     other = lax.ppermute(sent[1], plane, [(number(i, j, k), number(i, j, 1 - k)) for i, j, k in spots])
-    across = lax.ppermute(sent[2], plane, [(number(i, j, k), number(*turn(i, j, 1 - k), 1 - k)) for i, j, k in spots])
-    insertions, tally = call(finish_kernel, "finish", [shape(2, WIDTH, LANE), shape(2, GROUPS, WIDTH)], (place, stay, same, other, across), LIMIT)
+    insertions, tally = call(finish_kernel, "finish", [shape(2, WIDTH, LANE), shape(2, GROUPS, WIDTH)], (place, stay, same, across, other), LIMIT)
     return insertions, tally, evidence[0]
 
 

time: 107 us -> 106 us (level)
  transfers between devices with their start and end apart: 21 -> 21, of which waited for: 10 -> 12; matrix products, arithmetic and copies ran while one was open for 1% -> 1% of each run, Pallas kernels for 25% -> 26%
where the time goes in v5:
time: 106 us; the launch traced here: 105 us
  Pallas kernels  42.7 us (40%)
  starting transfers between devices  28.8 us (27%)
  waiting for transfers between devices  15.8 us (15%)
  blocking collectives  15.4 us (15%)
  between operations  1.45 us (1%)
  local copies, waits for them, and re-layouts  1.17 us (1%)
    pallas_call x12, Pallas kernels, call(): pl.pallas_call(kernel, name=name, in_specs=[SMEM] + [VMEM] * (len(args) -...  27.1 us
    all_to_all x1, blocking collectives, body(): stats = lax.all_to_all(stats, ring, 0, 0, tiled=True)  15.4 us
    ppermute x11, starting transfers between devices, swap(): return lax.ppermute(value, axis, [(i, i ^ d) for i in range(n)])  13.8 us
    pallas_call x2, Pallas kernels, build_call(): pl.pallas_call(build_kernel, name=name, in_specs=[SMEM] + [VMEM] * 5, out...  10.1 us
    ppermute x11, waiting for transfers between devices, swap(): return lax.ppermute(value, axis, [(i, i ^ d) for i in range(n)])  6.67 us
    all_to_all x1, starting transfers between devices, body(): column = lax.all_to_all(spread_call(stacks), ('y', 'zl'), 0, 0, tiled=True)  5.94 us
    all_to_all x1, waiting for transfers between devices, body(): column = lax.all_to_all(spread_call(stacks), ('y', 'zl'), 0, 0, tiled=True)  4.15 us
    ppermute x1, starting transfers between devices, body(): lax.ppermute(to_next, ring, [(i, (i + 1) % 8 if i % 2 else (i + 7) % 8) f...  2.67 us
  transfers between devices with their start and end apart: 21, of which 12 were waited for; matrix products, arithmetic and copies ran while one was open for 1% of the time, Pallas kernels for 26%

profile of v5, /device:TPU:32, one launch (start us, length us, event | category | flops | bytes accessed | tf_op | source)
XLA Modules:
  0.0 105.5 jit_solution(2534044234014258525)
XLA Ops:
  0.6 1.7 %spread.1 = bf16[8,200,128]{2,1,0:T(8,128)(2,1)} custom-call(bf16[2,200,128]{2,1,0:T(8,128)(2,1)} %bitcast.7), custom_call_target="tpu_custom_call" | custom-call | tf_op jit(solution)/shard_map/spread/pallas_call | solution.py:83
  2.3 5.9 %all-to-all-start = ((bf16[8,200,128]{2,1,0:T(8,128)(2,1)}), bf16[8,200,128]{2,1,0:T(8,128)(2,1)S(1)}, u32[]{:S(2)}, u32[]{:S(2)}) async-start(bf16[8,200,128]{2,1,0:T(8,128)(2,1)} %spread.1), calls=%async_computation | async-start | bytes 819200 | tf_op jit(solution)/shard_map/all_to_all | solution.py:409
  9.7 2.0 %split.1 = (bf16[40,4224]{1,0:T(8,128)(2,1)S(1)}, bf16[40,4224]{1,0:T(8,128)(2,1)S(1)}, bf16[48,4096]{1,0:T(8,128)(2,1)S(1)}, f32[24,4096]{1,0:T(8,128)S(1)}, f32[8,4096]{1,0:T(8,128)S(1)}) custom-call(s32[4]{0:T(128)S(1)} %pad_add_fusion.place, s32[40]{0:T(128)S(1)} %copy-done, s32[1]{0:T(128)S(6)} %copy.9.count, bf16[40,8192]{1,0:T(8,128)(2,1)} %images.1, ...), custom_call_target="tpu_custom_call" | custom-call | tf_op jit(solution)/shard_map/split/pallas_call | solution.py:129
  11.8 4.1 %all-to-all-done.after.refs_0_ = bf16[8,200,128]{2,1,0:T(8,128)(2,1)S(1)} async-done(((bf16[8,200,128]{2,1,0:T(8,128)(2,1)}), bf16[8,200,128]{2,1,0:T(8,128)(2,1)S(1)}, u32[]{:S(2)}, u32[]{:S(2)}) %all-to-all-start) | async-done | bytes 409632 | tf_op jit(solution)/shard_map/all_to_all | solution.py:409
  16.0 1.5 %collective-permute-start.1 = (bf16[8,200,128]{2,1,0:T(8,128)(2,1)S(1)}, bf16[8,200,128]{2,1,0:T(8,128)(2,1)S(1)}, u32[]{:S(2)}, u32[]{:S(2)}) collective-permute-start(bf16[8,200,128]{2,1,0:T(8,128)(2,1)S(1)} %all-to-all-done.after.refs_0_), channel_id=1, source_target_pairs={{0,16},{16,0},{32,48},{48,32},{1,17},{17,1},{33,49},{49,33},{2,18}... | collective-permute-start | bytes 1228808 | tf_op jit(solution)/shard_map/ppermute | solution.py:400
  17.5 2.1 %collective-permute-start.2 = (bf16[8,200,128]{2,1,0:T(8,128)(2,1)S(1)}, bf16[8,200,128]{2,1,0:T(8,128)(2,1)S(1)}, u32[]{:S(2)}, u32[]{:S(2)}) collective-permute-start(bf16[8,200,128]{2,1,0:T(8,128)(2,1)S(1)} %all-to-all-done.after.refs_0_), channel_id=1, source_target_pairs={{0,48},{16,32},{32,16},{48,0},{1,49},{17,33},{33,17},{49,1},{2,50}... | collective-permute-start | bytes 1228808 | tf_op jit(solution)/shard_map/ppermute | solution.py:400
  20.2 1.2 %collective-permute-start.4 = (bf16[40,4224]{1,0:T(8,128)(2,1)S(1)}, bf16[40,4224]{1,0:T(8,128)(2,1)S(1)}, u32[]{:S(2)}, u32[]{:S(2)}) collective-permute-start(bf16[40,4224]{1,0:T(8,128)(2,1)S(1)} %get-tuple-element.62.images_a.meta_a), channel_id=1, source_target_pairs={{0,2},{2,0},{1,3},{3,1},{4,6},{6,4},{5,7},{7,5},{8,10},{10,8},{9,1... | collective-permute-start | bytes 1013768 | tf_op jit(solution)/shard_map/ppermute | solution.py:416
  21.4 2.7 %collective-permute-start.5 = (bf16[40,4224]{1,0:T(8,128)(2,1)S(1)}, bf16[40,4224]{1,0:T(8,128)(2,1)S(1)}, u32[]{:S(2)}, u32[]{:S(2)}) collective-permute-start(bf16[40,4224]{1,0:T(8,128)(2,1)S(1)} %get-tuple-element.63), channel_id=1, source_target_pairs={{0,194},{2,64},{64,2},{66,128},{128,66},{130,192},{192,130},{194,0... | collective-permute-start | bytes 1013768 | tf_op jit(solution)/shard_map/ppermute | solution.py:417
  24.0 5.1 %build_here.1 = (bf16[2,1024,512]{2,1,0:T(8,128)(2,1)S(1)}, bf16[2,1024,512]{2,1,0:T(8,128)(2,1)S(1)}, bf16[2,1024,512]{2,1,0:T(8,128)(2,1)S(1)}, bf16[2,1024,51...) custom-call(s32[4]{0:T(128)S(1)} %pad_add_fusion.place, ...), custom_call_target="tpu_custom_call" | custom-call | flops 6000000000 | bytes 100000 | tf_op jit(solution)/shard_map/build_here/pallas_call | solution.py:190
  29.6 0.9 weigh_own.1.after
  31.3 5.1 %build_next.1 = (bf16[2,1024,512]{2,1,0:T(8,128)(2,1)S(1)}, bf16[2,1024,512]{2,1,0:T(8,128)(2,1)S(1)}, bf16[2,1024,512]{2,1,0:T(8,128)(2,1)S(1)}, bf16[2,1024,51...) custom-call(s32[4]{0:T(128)S(1)} %pad_add_fusion.place, ...), custom_call_target="tpu_custom_call" | custom-call | flops 100000000 | bytes 100000 | tf_op jit(solution)/shard_map/build_next/pallas_call | solution.py:190
  36.9 1.5 %weigh.1.power = f32[8,200]{1,0:T(8,128)S(1)} custom-call(s32[4]{0:T(128)S(1)} %pad_add_fusion.place, f32[8,4096]{1,0:T(8,128)S(1)} %get-tuple-element.55.ctf, f32[8,200]{1,0:T(8,128)S(1)} %weigh_own.1.after, bf16[8,200,128]{2,1,0:T(8,128)(2,1)S(1)} %collective-permute-done.1.refs_0_.refs_1_, ...), custom_call_target="tpu_custom_call" | custom-call | tf_op jit(solution)/shard_map/weigh/pallas_call | solution.py:48
  38.4 5.2 %score_given.1 = f32[2,1024,256]{2,1,0:T(8,128)S(1)} custom-call(s32[4]{0:T(128)S(1)} %pad_add_fusion.place, f32[8,200]{1,0:T(8,128)S(1)} %weigh.1.power, bf16[40,4224]{1,0:T(8,128)(2,1)S(1)} %collective-permute-done.images_b.meta_a, bf16[40,4224]{1,0:T(8,128)(2,1)S(1)} %collective-permute-done.6.images_b.meta_b, ...), custom_call_target="tpu_custom_call" | custom-call | flops 4294967296 | tf_op jit(solution)/shard_map/score_given/pallas_call | solution.py:48
  43.7 5.2 %score_own.1.mine = f32[2,1024,256]{2,1,0:T(8,128)S(1)} custom-call(s32[4]{0:T(128)S(1)} %pad_add_fusion.place, f32[8,200]{1,0:T(8,128)S(1)} %weigh.1.power, bf16[40,4224]{1,0:T(8,128)(2,1)S(1)} %get-tuple-element.62.images_a.meta_a, bf16[40,4224]{1,0:T(8,128)(2,1)S(1)} %collective-permute-done.4.images_a.meta_b, ...), custom_call_target="tpu_custom_call" | custom-call | flops 4294967296 | tf_op jit(solution)/shard_map/score_own/pallas_call | solution.py:48
  48.9 1.3 %settle.1 = f32[8,8,128]{2,1,0:T(8,128)S(1)} custom-call(s32[4]{0:T(128)S(1)} %pad_add_fusion.place, f32[2,1024,256]{2,1,0:T(8,128)S(1)} %score_own.1.mine, f32[2,1024,256]{2,1,0:T(8,128)S(1)} %collective-permute-done.7.theirs), custom_call_target="tpu_custom_call" | custom-call | tf_op jit(solution)/shard_map/settle/pallas_call | solution.py:48
  50.1 15.4 %all_to_all.10.stats = f32[8,8,128]{2,1,0:T(8,128)S(1)} all-to-all(f32[8,8,128]{2,1,0:T(8,128)S(1)} %settle.1), channel_id=1, replica_groups=mesh['cls'=4,'grp'=4,'y'=4,'zl'=2,'core'=2] {'cls','zl'}, dimensions={0} | all-to-all | bytes 65536 | tf_op jit(solution)/shard_map/all_to_all | solution.py:435
  65.5 1.7 %posterior.1 = (bf16[2,200,1024]{2,1,0:T(8,128)(2,1)S(1)}, f32[8,40]{1,0:T(8,128)S(1)}) custom-call(s32[4]{0:T(128)S(1)} %pad_add_fusion.place, f32[2,1024,256]{2,1,0:T(8,128)S(1)} %score_own.1.mine, f32[2,1024,256]{2,1,0:T(8,128)S(1)} %collective-permute-done.7.theirs, f32[8,8,128]{2,1,0:T(8,128)S(1)} %all_to_all.10.stats, ...), custom_call_target="tpu_custom_call" | custom-call | tf_op jit(solution)/shard_map/posterior/pallas_call | solution.py:315
  67.5 1.6 %insert_begin.1 = (f32[4,200,128]{2,1,0:T(8,128)S(1)}, f32[4,200,128]{2,1,0:T(8,128)S(1)}) custom-call(s32[4]{0:T(128)S(1)} %pad_add_fusion.place, bf16[2,200,1024]{2,1,0:T(8,128)(2,1)S(1)} %get-tuple-element.84.mine, bf16[2,1024,512]{2,1,0:T(8,128)(2,1)S(1)} %get-tuple-element.69.refs_6_.a0.refs_2_, ...), custom_call_target="tpu_custom_call" | custom-call | flops 1073741824 | tf_op jit(solution)/shard_map/insert_begin/pallas_call | solution.py:48
  69.9 1.6 %insert_far.1 = (bf16[4,216,128]{2,1,0:T(8,128)(2,1)S(1)}, bf16[4,216,128]{2,1,0:T(8,128)(2,1)S(1)}, f32[8,128]{1,0:T(8,128)S(1)}) custom-call(s32[4]{0:T(128)S(1)} %pad_add_fusion.place, f32[8,40]{1,0:T(8,128)S(1)} %get-tuple-element.83.after, bf16[2,200,1024]{2,1,0:T(8,128)(2,1)S(1)} %get-tuple-element.84.mine, ...), custom_call_target="tpu_custom_call" | custom-call | flops 1073741824 | tf_op jit(solution)/shard_map/insert_far/pallas_call | solution.py:48
  71.5 1.0 collective-permute-start.10
  72.5 2.6 %collective-permute-start.9 = (bf16[4,216,128]{2,1,0:T(8,128)(2,1)S(1)}, bf16[4,216,128]{2,1,0:T(8,128)(2,1)S(1)}, u32[]{:S(2)}, u32[]{:S(2)}) collective-permute-start(bf16[4,216,128]{2,1,0:T(8,128)(2,1)S(1)} %get-tuple-element.89), channel_id=1, source_target_pairs={{0,32},{16,48},{32,0},{48,16},{1,33},{17,49},{33,1},{49,17},{2,34}... | collective-permute-start | bytes 663560 | tf_op jit(solution)/shard_map/ppermute | solution.py:400
  75.1 4.3 %insert_near.1 = (bf16[4,216,128]{2,1,0:T(8,128)(2,1)S(1)}, bf16[4,216,128]{2,1,0:T(8,128)(2,1)S(1)}, bf16[4,216,128]{2,1,0:T(8,128)(2,1)S(1)}, bf16[4,216,128]{2,1,0:T(8,128)(2,1)S(1)}, f32[8,128]{1,0:T(8,128)S(1)}) custom-call(s32[4]{0:T(128)S(1)} %pad_add_fusion.place, f32[8,128]{1,0:T(8,128)S(1)} %get-tuple-element.87.after, ...), custom_call_target="tpu_custom_call" | custom-call | flops 4294967296 | tf_op jit(solution)/shard_map/insert_near/pallas_call | solution.py:48
  80.7 1.1 %collective-permute-start.13 = (bf16[4,216,128]{2,1,0:T(8,128)(2,1)S(1)}, bf16[4,216,128]{2,1,0:T(8,128)(2,1)S(1)}, u32[]{:S(2)}, u32[]{:S(2)}) collective-permute-start(bf16[4,216,128]{2,1,0:T(8,128)(2,1)S(1)} %get-tuple-element.95), channel_id=1, source_target_pairs={{0,48},{16,32},{32,16},{48,0},{1,49},{17,33},{33,17},{49,1},{2,50}... | collective-permute-start | bytes 663560 | tf_op jit(solution)/shard_map/ppermute | solution.py:400
  81.8 2.4 %collective-permute-start.14 = (bf16[4,216,128]{2,1,0:T(8,128)(2,1)S(1)}, bf16[4,216,128]{2,1,0:T(8,128)(2,1)S(1)}, u32[]{:S(2)}, u32[]{:S(2)}) collective-permute-start(bf16[4,216,128]{2,1,0:T(8,128)(2,1)S(1)} %get-tuple-element.96), channel_id=1, source_target_pairs={{0,12},{4,8},{8,4},{12,0},{1,13},{5,9},{9,5},{13,1},{2,14},{6,10},... | collective-permute-start | bytes 663560 | tf_op jit(solution)/shard_map/ppermute | solution.py:400
  84.2 3.0 %insert_own.1 = (f32[4,216,128]{2,1,0:T(8,128)S(1)}, f32[4,216,128]{2,1,0:T(8,128)S(1)}, f32[8,128]{1,0:T(8,128)}) custom-call(s32[4]{0:T(128)S(1)} %pad_add_fusion.place, f32[8,128]{1,0:T(8,128)S(1)} %get-tuple-element.88.after, bf16[2,200,1024]{2,1,0:T(8,128)(2,1)S(1)} %get-tuple-element.84.mine, bf16[2,200,1024]{2,1,0:T(8,128)(2,1)S(1)} %collective-permute-done.8.theirs, ...), custom_call_target="tpu_custom_call" | custom-call | flops 2147483648 | tf_op jit(solution)/shard_map/insert_own/pallas_call | solution.py:48
  87.2 1.1 %collective-permute-done.13.three_a = bf16[4,216,128]{2,1,0:T(8,128)(2,1)S(1)} collective-permute-done((bf16[4,216,128]{2,1,0:T(8,128)(2,1)S(1)}, bf16[4,216,128]{2,1,0:T(8,128)(2,1)S(1)}, u32[]{:S(2)}, u32[]{:S(2)}) %collective-permute-start.13) | collective-permute-done | bytes 221216 | tf_op jit(solution)/shard_map/ppermute | solution.py:400
  88.3 0.8 collective-permute-done.14.three_b
  91.0 3.7 %collective-permute-done.15.got_a = bf16[2,216,128]{2,1,0:T(8,128)(2,1)S(1)} collective-permute-done((bf16[2,216,128]{2,1,0:T(8,128)(2,1)S(1)}, bf16[2,216,128]{2,1,0:T(8,128)(2,1)S(1)}, u32[]{:S(2)}, u32[]{:S(2)}) %collective-permute-start.15) | collective-permute-done | bytes 110624 | tf_op jit(solution)/shard_map/ppermute | solution.py:400
  95.9 1.8 %collective-permute-start.17 = (bf16[216,128]{1,0:T(8,128)(2,1)S(1)}, bf16[216,128]{1,0:T(8,128)(2,1)S(1)}, u32[]{:S(2)}, u32[]{:S(2)}) collective-permute-start(bf16[216,128]{1,0:T(8,128)(2,1)S(1)} %get-tuple-element.102), channel_id=1, source_target_pairs={{0,12},{2,50},{4,8},{6,54},{8,4},{10,58},{12,0},{14,62},{16,28},{1... | collective-permute-start | bytes 165896 | tf_op jit(solution)/shard_map/ppermute | solution.py:479
  97.7 2.4 %collective-permute-start.18 = (bf16[216,128]{1,0:T(8,128)(2,1)S(1)}, bf16[216,128]{1,0:T(8,128)(2,1)S(1)}, u32[]{:S(2)}, u32[]{:S(2)}) collective-permute-start(bf16[216,128]{1,0:T(8,128)(2,1)S(1)} %get-tuple-element.103), channel_id=1, source_target_pairs={{0,50},{2,12},{4,54},{6,8},{8,58},{10,4},{12,62},{14,0},{16,34},{1... | collective-permute-start | bytes 165896 | tf_op jit(solution)/shard_map/ppermute | solution.py:480
  101.3 2.6 %collective-permute-done.18.across = bf16[216,128]{1,0:T(8,128)(2,1)S(1)} collective-permute-done((bf16[216,128]{1,0:T(8,128)(2,1)S(1)}, bf16[216,128]{1,0:T(8,128)(2,1)S(1)}, u32[]{:S(2)}, u32[]{:S(2)}) %collective-permute-start.18) | collective-permute-done | bytes 55328 | tf_op jit(solution)/shard_map/ppermute | solution.py:480
  104.2 1.2 %finish.1 = (f32[2,200,128]{2,1,0:T(8,128)}, f32[2,8,200]{2,1,0:T(8,128)}) custom-call(s32[4]{0:T(128)S(1)} %pad_add_fusion.place, f32[216,128]{1,0:T(8,128)S(1)} %get-tuple-element.101.stay, bf16[216,128]{1,0:T(8,128)(2,1)S(1)} %collective-permute-done.17.same, bf16[216,128]{1,0:T(8,128)(2,1)S(1)} %collective-permute-done.18.across, ...), custom_call_target="tpu_custom_call" | custom-call | tf_op jit(solution)/shard_map/finish/pallas_call | solution.py:48
  (32 shorter events, 10.3 us)
Async XLA Ops:
  2.3 13.6 %all-to-all-start = ((bf16[8,200,128]{2,1,0:T(8,128)(2,1)}), bf16[8,200,128]{2,1,0:T(8,128)(2,1)S(1)}, u32[]{:S(2)}, u32[]{:S(2)}) async-start(bf16[8,200,128]{2,1,0:T(8,128)(2,1)} %spread.1), calls=%async_computation | async-start | bytes 819200 | tf_op jit(solution)/shard_map/all_to_all | solution.py:409
  9.0 0.7 copy-start
  11.7 9.6 %collective-permute-start = (bf16[40,4224]{1,0:T(8,128)(2,1)S(1)}, bf16[40,4224]{1,0:T(8,128)(2,1)S(1)}, u32[]{:S(2)}, u32[]{:S(2)}) collective-permute-start(bf16[40,4224]{1,0:T(8,128)(2,1)S(1)} %get-tuple-element.63), channel_id=1, source_target_pairs={{0,1},{1,0},{2,3},{3,2},{4,5},{5,4},{6,7},{7,6},{8,9},{9,8},{10,11... | collective-permute-start | bytes 1013768 | tf_op jit(solution)/shard_map/ppermute | solution.py:413
  16.0 20.4 %collective-permute-start.1 = (bf16[8,200,128]{2,1,0:T(8,128)(2,1)S(1)}, bf16[8,200,128]{2,1,0:T(8,128)(2,1)S(1)}, u32[]{:S(2)}, u32[]{:S(2)}) collective-permute-start(bf16[8,200,128]{2,1,0:T(8,128)(2,1)S(1)} %all-to-all-done.after.refs_0_), channel_id=1, source_target_pairs={{0,16},{16,0},{32,48},{48,32},{1,17},{17,1},{33,49},{49,33},{2,18}... | collective-permute-start | bytes 1228808 | tf_op jit(solution)/shard_map/ppermute | solution.py:400
  17.5 19.4 %collective-permute-start.2 = (bf16[8,200,128]{2,1,0:T(8,128)(2,1)S(1)}, bf16[8,200,128]{2,1,0:T(8,128)(2,1)S(1)}, u32[]{:S(2)}, u32[]{:S(2)}) collective-permute-start(bf16[8,200,128]{2,1,0:T(8,128)(2,1)S(1)} %all-to-all-done.after.refs_0_), channel_id=1, source_target_pairs={{0,48},{16,32},{32,16},{48,0},{1,49},{17,33},{33,17},{49,1},{2,50}... | collective-permute-start | bytes 1228808 | tf_op jit(solution)/shard_map/ppermute | solution.py:400
  19.6 17.3 %collective-permute-start.3 = (bf16[8,200,128]{2,1,0:T(8,128)(2,1)S(1)}, bf16[8,200,128]{2,1,0:T(8,128)(2,1)S(1)}, u32[]{:S(2)}, u32[]{:S(2)}) collective-permute-start(bf16[8,200,128]{2,1,0:T(8,128)(2,1)S(1)} %all-to-all-done.after.refs_0_), channel_id=1, source_target_pairs={{0,32},{16,48},{32,0},{48,16},{1,33},{17,49},{33,1},{49,17},{2,34}... | collective-permute-start | bytes 1228808 | tf_op jit(solution)/shard_map/ppermute | solution.py:400
  20.2 8.9 %collective-permute-start.4 = (bf16[40,4224]{1,0:T(8,128)(2,1)S(1)}, bf16[40,4224]{1,0:T(8,128)(2,1)S(1)}, u32[]{:S(2)}, u32[]{:S(2)}) collective-permute-start(bf16[40,4224]{1,0:T(8,128)(2,1)S(1)} %get-tuple-element.62.images_a.meta_a), channel_id=1, source_target_pairs={{0,2},{2,0},{1,3},{3,1},{4,6},{6,4},{5,7},{7,5},{8,10},{10,8},{9,1... | collective-permute-start | bytes 1013768 | tf_op jit(solution)/shard_map/ppermute | solution.py:416
  21.4 8.3 %collective-permute-start.5 = (bf16[40,4224]{1,0:T(8,128)(2,1)S(1)}, bf16[40,4224]{1,0:T(8,128)(2,1)S(1)}, u32[]{:S(2)}, u32[]{:S(2)}) collective-permute-start(bf16[40,4224]{1,0:T(8,128)(2,1)S(1)} %get-tuple-element.63), channel_id=1, source_target_pairs={{0,194},{2,64},{64,2},{66,128},{128,66},{130,192},{192,130},{194,0... | collective-permute-start | bytes 1013768 | tf_op jit(solution)/shard_map/ppermute | solution.py:417
  29.6 1.6 %collective-permute-start.6 = (bf16[40,4224]{1,0:T(8,128)(2,1)S(1)}, bf16[40,4224]{1,0:T(8,128)(2,1)S(1)}, u32[]{:S(2)}, u32[]{:S(2)}) collective-permute-start(bf16[40,4224]{1,0:T(8,128)(2,1)S(1)} %collective-permute-done.5), channel_id=1, source_target_pairs={{0,1},{1,0},{2,3},{3,2},{4,5},{5,4},{6,7},{7,6},{8,9},{9,8},{10,11... | collective-permute-start | bytes 1013768 | tf_op jit(solution)/shard_map/ppermute | solution.py:423
  43.6 5.3 %collective-permute-start.7 = (f32[2,1024,256]{2,1,0:T(8,128)S(1)}, f32[2,1024,256]{2,1,0:T(8,128)S(1)}, u32[]{:S(2)}, u32[]{:S(2)}) collective-permute-start(f32[2,1024,256]{2,1,0:T(8,128)S(1)} %score_given.1), channel_id=1, source_target_pairs={{0,1},{1,0},{2,3},{3,2},{4,5},{5,4},{6,7},{7,6},{8,9},{9,8},{10,11... | collective-permute-start | bytes 6291464 | tf_op jit(solution)/shard_map/ppermute | solution.py:432
  67.2 2.6 %collective-permute-start.8 = (bf16[2,200,1024]{2,1,0:T(8,128)(2,1)S(1)}, bf16[2,200,1024]{2,1,0:T(8,128)(2,1)S(1)}, u32[]{:S(2)}, u32[]{:S(2)}) collective-permute-start(bf16[2,200,1024]{2,1,0:T(8,128)(2,1)S(1)} %get-tuple-element.84.mine), channel_id=1, source_target_pairs={{0,1},{1,0},{2,3},{3,2},{4,5},{5,4},{6,7},{7,6},{8,9},{9,8},{10,11... | collective-permute-start | bytes 2457608 | tf_op jit(solution)/shard_map/ppermute | solution.py:437
  71.5 10.3 %collective-permute-start.10 = (bf16[4,216,128]{2,1,0:T(8,128)(2,1)S(1)}, bf16[4,216,128]{2,1,0:T(8,128)(2,1)S(1)}, u32[]{:S(2)}, u32[]{:S(2)}) collective-permute-start(bf16[4,216,128]{2,1,0:T(8,128)(2,1)S(1)} %get-tuple-element.90), channel_id=1, source_target_pairs={{0,8},{4,12},{8,0},{12,4},{1,9},{5,13},{9,1},{13,5},{2,10},{6,14},... | collective-permute-start | bytes 663560 | tf_op jit(solution)/shard_map/ppermute | solution.py:400
  72.5 11.7 %collective-permute-start.9 = (bf16[4,216,128]{2,1,0:T(8,128)(2,1)S(1)}, bf16[4,216,128]{2,1,0:T(8,128)(2,1)S(1)}, u32[]{:S(2)}, u32[]{:S(2)}) collective-permute-start(bf16[4,216,128]{2,1,0:T(8,128)(2,1)S(1)} %get-tuple-element.89), channel_id=1, source_target_pairs={{0,32},{16,48},{32,0},{48,16},{1,33},{17,49},{33,1},{49,17},{2,34}... | collective-permute-start | bytes 663560 | tf_op jit(solution)/shard_map/ppermute | solution.py:400
  79.4 7.8 %collective-permute-start.11 = (bf16[4,216,128]{2,1,0:T(8,128)(2,1)S(1)}, bf16[4,216,128]{2,1,0:T(8,128)(2,1)S(1)}, u32[]{:S(2)}, u32[]{:S(2)}) collective-permute-start(bf16[4,216,128]{2,1,0:T(8,128)(2,1)S(1)} %get-tuple-element.93), channel_id=1, source_target_pairs={{0,16},{16,0},{32,48},{48,32},{1,17},{17,1},{33,49},{49,33},{2,18}... | collective-permute-start | bytes 663560 | tf_op jit(solution)/shard_map/ppermute | solution.py:400
  80.1 7.1 %collective-permute-start.12 = (bf16[4,216,128]{2,1,0:T(8,128)(2,1)S(1)}, bf16[4,216,128]{2,1,0:T(8,128)(2,1)S(1)}, u32[]{:S(2)}, u32[]{:S(2)}) collective-permute-start(bf16[4,216,128]{2,1,0:T(8,128)(2,1)S(1)} %get-tuple-element.94), channel_id=1, source_target_pairs={{0,4},{4,0},{8,12},{12,8},{1,5},{5,1},{9,13},{13,9},{2,6},{6,2},{1... | collective-permute-start | bytes 663560 | tf_op jit(solution)/shard_map/ppermute | solution.py:400
  80.7 7.6 %collective-permute-start.13 = (bf16[4,216,128]{2,1,0:T(8,128)(2,1)S(1)}, bf16[4,216,128]{2,1,0:T(8,128)(2,1)S(1)}, u32[]{:S(2)}, u32[]{:S(2)}) collective-permute-start(bf16[4,216,128]{2,1,0:T(8,128)(2,1)S(1)} %get-tuple-element.95), channel_id=1, source_target_pairs={{0,48},{16,32},{32,16},{48,0},{1,49},{17,33},{33,17},{49,1},{2,50}... | collective-permute-start | bytes 663560 | tf_op jit(solution)/shard_map/ppermute | solution.py:400
  81.8 7.3 %collective-permute-start.14 = (bf16[4,216,128]{2,1,0:T(8,128)(2,1)S(1)}, bf16[4,216,128]{2,1,0:T(8,128)(2,1)S(1)}, u32[]{:S(2)}, u32[]{:S(2)}) collective-permute-start(bf16[4,216,128]{2,1,0:T(8,128)(2,1)S(1)} %get-tuple-element.96), channel_id=1, source_target_pairs={{0,12},{4,8},{8,4},{12,0},{1,13},{5,9},{9,5},{13,1},{2,14},{6,10},... | collective-permute-start | bytes 663560 | tf_op jit(solution)/shard_map/ppermute | solution.py:400
  89.8 4.8 %collective-permute-start.15 = (bf16[2,216,128]{2,1,0:T(8,128)(2,1)S(1)}, bf16[2,216,128]{2,1,0:T(8,128)(2,1)S(1)}, u32[]{:S(2)}, u32[]{:S(2)}) collective-permute-start(bf16[2,216,128]{2,1,0:T(8,128)(2,1)S(1)} %get-tuple-element.99), channel_id=1, source_target_pairs={{0,4},{4,0},{8,12},{12,8},{1,5},{5,1},{9,13},{13,9},{2,6},{6,2},{1... | collective-permute-start | bytes 331784 | tf_op jit(solution)/shard_map/ppermute | solution.py:400
  90.5 4.7 %collective-permute-start.16 = (bf16[2,216,128]{2,1,0:T(8,128)(2,1)S(1)}, bf16[2,216,128]{2,1,0:T(8,128)(2,1)S(1)}, u32[]{:S(2)}, u32[]{:S(2)}) collective-permute-start(bf16[2,216,128]{2,1,0:T(8,128)(2,1)S(1)} %get-tuple-element.100), channel_id=1, source_target_pairs={{0,16},{16,0},{32,48},{48,32},{1,17},{17,1},{33,49},{49,33},{2,18}... | collective-permute-start | bytes 331784 | tf_op jit(solution)/shard_map/ppermute | solution.py:400
  95.9 5.5 %collective-permute-start.17 = (bf16[216,128]{1,0:T(8,128)(2,1)S(1)}, bf16[216,128]{1,0:T(8,128)(2,1)S(1)}, u32[]{:S(2)}, u32[]{:S(2)}) collective-permute-start(bf16[216,128]{1,0:T(8,128)(2,1)S(1)} %get-tuple-element.102), channel_id=1, source_target_pairs={{0,12},{2,50},{4,8},{6,54},{8,4},{10,58},{12,0},{14,62},{16,28},{1... | collective-permute-start | bytes 165896 | tf_op jit(solution)/shard_map/ppermute | solution.py:479
  97.7 6.3 %collective-permute-start.18 = (bf16[216,128]{1,0:T(8,128)(2,1)S(1)}, bf16[216,128]{1,0:T(8,128)(2,1)S(1)}, u32[]{:S(2)}, u32[]{:S(2)}) collective-permute-start(bf16[216,128]{1,0:T(8,128)(2,1)S(1)} %get-tuple-element.103), channel_id=1, source_target_pairs={{0,50},{2,12},{4,54},{6,8},{8,58},{10,4},{12,62},{14,0},{16,34},{1... | collective-permute-start | bytes 165896 | tf_op jit(solution)/shard_map/ppermute | solution.py:480
  100.1 4.2 %collective-permute-start.19 = (bf16[216,128]{1,0:T(8,128)(2,1)S(1)}, bf16[216,128]{1,0:T(8,128)(2,1)S(1)}, u32[]{:S(2)}, u32[]{:S(2)}) collective-permute-start(bf16[216,128]{1,0:T(8,128)(2,1)S(1)} %get-tuple-element.104), channel_id=1, source_target_pairs={{0,2},{2,0},{4,6},{6,4},{8,10},{10,8},{12,14},{14,12},{16,18},{18,... | collective-permute-start | bytes 165896 | tf_op jit(solution)/shard_map/ppermute | solution.py:481

commit v6 on v5

--- a/solution.py
+++ b/solution.py
@@ -370,14 +370,14 @@
     return kernel
 
 
-def gather_kernel(place, own_a, own_b, one_a, one_b, three_a, three_b, kept_a, kept_b, sent_a, sent_b):
-    y = place[1]
-    for out, planes in ((kept_a, (y, y ^ 3)), (sent_a, (y ^ 1, y ^ 2))):
-        for i, n in enumerate(planes):
-            out[i] = (own_a[n] + one_a[n].astype(F32) + three_a[n].astype(F32)).astype(out.dtype)
-    for out, planes in ((kept_b, (0, 3)), (sent_b, (1, 2))):
-        for i, n in enumerate(planes):
-            out[i] = (own_b[n] + one_b[n].astype(F32) + three_b[n].astype(F32)).astype(out.dtype)
+def gather_kernel(along):
+    def kernel(place, own, one, three, kept, sent):
+        y = place[1] if along else 0
+        for out, planes in ((kept, (y, y ^ 3)), (sent, (y ^ 1, y ^ 2))):
+            for i, n in enumerate(planes):
+                out[i] = (own[n] + one[n].astype(F32) + three[n].astype(F32)).astype(out.dtype)
+
+    return kernel
 
 
 def middle_kernel(place, kept_a, kept_b, got_a, got_b, stay, same, other, across):
@@ -463,10 +463,13 @@
         insert_kernel(1, joined=True), "insert_own", [*block(F32), token], (place, after, low, other_low, *far, *columns(0)), LIMIT, flops
     )
     pair = (2, TALL, LANE)
-    out = [shape(*pair)] * 2 + [shape(*pair, dtype=BF16)] * 2
-    *kept, send_a, send_b = call(gather_kernel, "gather", out, (place, *own, *near), LIMIT)
+    out = [shape(*pair), shape(*pair, dtype=BF16)]
+    kept_a, send_a = call(gather_kernel(True), "gather_a", out, (place, own[0], near[0], near[2]), LIMIT)
+    got_a = swap(send_a, "y", 1)
+    kept_b, send_b = call(gather_kernel(False), "gather_b", out, (place, own[1], near[1], near[3]), LIMIT)
+    got_b = swap(send_b, "grp", 1)
     out = [shape(*pair[1:])] + [shape(*pair[1:], dtype=BF16)] * 3
-    stay, *sent = call(middle_kernel, "middle", out, (place, *kept, swap(send_a, "y", 1), swap(send_b, "grp", 1)), LIMIT)
+    stay, *sent = call(middle_kernel, "middle", out, (place, kept_a, kept_b, got_a, got_b), LIMIT)
     plane = ("grp", "y", "zl")
     spots = [(i, j, k) for i in range(4) for j in range(4) for k in range(2)]
 

time: 106 us -> 107 us (level)
    pallas_call x12 -> x13, Pallas kernels: 27.1 us -> 27.7 us  [call(): pl.pallas_call(kernel, name=name, in_specs=[SMEM] + [VMEM] * (len(args) -...]
  transfers between devices with their start and end apart: 21 -> 21, of which waited for: 12 -> 12; matrix products, arithmetic and copies ran while one was open for 1% -> 1% of each run, Pallas kernels for 26% -> 27%
where the time goes in v6:
time: 107 us; the launch traced here: 106 us
  Pallas kernels  43.3 us (40%)
  starting transfers between devices  28.7 us (27%)
  waiting for transfers between devices  15.9 us (15%)
  blocking collectives  15.4 us (14%)
  between operations  1.45 us (1%)
  local copies, waits for them, and re-layouts  1.17 us (1%)
    pallas_call x13, Pallas kernels, call(): pl.pallas_call(kernel, name=name, in_specs=[SMEM] + [VMEM] * (len(args) -...  27.7 us
    all_to_all x1, blocking collectives, body(): stats = lax.all_to_all(stats, ring, 0, 0, tiled=True)  15.4 us
    ppermute x11, starting transfers between devices, swap(): return lax.ppermute(value, axis, [(i, i ^ d) for i in range(n)])  13.7 us
    pallas_call x2, Pallas kernels, build_call(): pl.pallas_call(build_kernel, name=name, in_specs=[SMEM] + [VMEM] * 5, out...  10.1 us
    ppermute x11, waiting for transfers between devices, swap(): return lax.ppermute(value, axis, [(i, i ^ d) for i in range(n)])  6.76 us
    all_to_all x1, starting transfers between devices, body(): column = lax.all_to_all(spread_call(stacks), ('y', 'zl'), 0, 0, tiled=True)  5.94 us
    all_to_all x1, waiting for transfers between devices, body(): column = lax.all_to_all(spread_call(stacks), ('y', 'zl'), 0, 0, tiled=True)  4.15 us
    ppermute x1, starting transfers between devices, body(): lax.ppermute(sent[2], plane, [(number(i, j, k), number(*turn(i, j, 1 - k)...  3 us
  transfers between devices with their start and end apart: 21, of which 12 were waited for; matrix products, arithmetic and copies ran while one was open for 1% of the time, Pallas kernels for 27%

profile of v6, /device:TPU:32, one launch (start us, length us, event | category | flops | bytes accessed | tf_op | source)
XLA Modules:
  0.0 106.0 jit_solution(6154507574170116404)
XLA Ops:
  0.6 1.7 %spread.1 = bf16[8,200,128]{2,1,0:T(8,128)(2,1)} custom-call(bf16[2,200,128]{2,1,0:T(8,128)(2,1)} %bitcast.7), custom_call_target="tpu_custom_call" | custom-call | tf_op jit(solution)/shard_map/spread/pallas_call | solution.py:83
  2.4 5.9 %all-to-all-start = ((bf16[8,200,128]{2,1,0:T(8,128)(2,1)}), bf16[8,200,128]{2,1,0:T(8,128)(2,1)S(1)}, u32[]{:S(2)}, u32[]{:S(2)}) async-start(bf16[8,200,128]{2,1,0:T(8,128)(2,1)} %spread.1), calls=%async_computation | async-start | bytes 819200 | tf_op jit(solution)/shard_map/all_to_all | solution.py:409
  9.7 2.0 %split.1 = (bf16[40,4224]{1,0:T(8,128)(2,1)S(1)}, bf16[40,4224]{1,0:T(8,128)(2,1)S(1)}, bf16[48,4096]{1,0:T(8,128)(2,1)S(1)}, f32[24,4096]{1,0:T(8,128)S(1)}, f32[8,4096]{1,0:T(8,128)S(1)}) custom-call(s32[4]{0:T(128)S(1)} %pad_add_fusion.place, s32[40]{0:T(128)S(1)} %copy-done, s32[1]{0:T(128)S(6)} %copy.9.count, bf16[40,8192]{1,0:T(8,128)(2,1)} %images.1, ...), custom_call_target="tpu_custom_call" | custom-call | tf_op jit(solution)/shard_map/split/pallas_call | solution.py:129
  11.8 4.1 %all-to-all-done.after.refs_0_ = bf16[8,200,128]{2,1,0:T(8,128)(2,1)S(1)} async-done(((bf16[8,200,128]{2,1,0:T(8,128)(2,1)}), bf16[8,200,128]{2,1,0:T(8,128)(2,1)S(1)}, u32[]{:S(2)}, u32[]{:S(2)}) %all-to-all-start) | async-done | bytes 409632 | tf_op jit(solution)/shard_map/all_to_all | solution.py:409
  16.0 1.5 %collective-permute-start.1 = (bf16[8,200,128]{2,1,0:T(8,128)(2,1)S(1)}, bf16[8,200,128]{2,1,0:T(8,128)(2,1)S(1)}, u32[]{:S(2)}, u32[]{:S(2)}) collective-permute-start(bf16[8,200,128]{2,1,0:T(8,128)(2,1)S(1)} %all-to-all-done.after.refs_0_), channel_id=1, source_target_pairs={{0,16},{16,0},{32,48},{48,32},{1,17},{17,1},{33,49},{49,33},{2,18}... | collective-permute-start | bytes 1228808 | tf_op jit(solution)/shard_map/ppermute | solution.py:400
  17.5 2.1 %collective-permute-start.2 = (bf16[8,200,128]{2,1,0:T(8,128)(2,1)S(1)}, bf16[8,200,128]{2,1,0:T(8,128)(2,1)S(1)}, u32[]{:S(2)}, u32[]{:S(2)}) collective-permute-start(bf16[8,200,128]{2,1,0:T(8,128)(2,1)S(1)} %all-to-all-done.after.refs_0_), channel_id=1, source_target_pairs={{0,48},{16,32},{32,16},{48,0},{1,49},{17,33},{33,17},{49,1},{2,50}... | collective-permute-start | bytes 1228808 | tf_op jit(solution)/shard_map/ppermute | solution.py:400
  20.2 1.2 %collective-permute-start.4 = (bf16[40,4224]{1,0:T(8,128)(2,1)S(1)}, bf16[40,4224]{1,0:T(8,128)(2,1)S(1)}, u32[]{:S(2)}, u32[]{:S(2)}) collective-permute-start(bf16[40,4224]{1,0:T(8,128)(2,1)S(1)} %get-tuple-element.62.images_a.meta_a), channel_id=1, source_target_pairs={{0,2},{2,0},{1,3},{3,1},{4,6},{6,4},{5,7},{7,5},{8,10},{10,8},{9,1... | collective-permute-start | bytes 1013768 | tf_op jit(solution)/shard_map/ppermute | solution.py:416
  21.4 2.7 %collective-permute-start.5 = (bf16[40,4224]{1,0:T(8,128)(2,1)S(1)}, bf16[40,4224]{1,0:T(8,128)(2,1)S(1)}, u32[]{:S(2)}, u32[]{:S(2)}) collective-permute-start(bf16[40,4224]{1,0:T(8,128)(2,1)S(1)} %get-tuple-element.63), channel_id=1, source_target_pairs={{0,194},{2,64},{64,2},{66,128},{128,66},{130,192},{192,130},{194,0... | collective-permute-start | bytes 1013768 | tf_op jit(solution)/shard_map/ppermute | solution.py:417
  24.0 5.1 %build_here.1 = (bf16[2,1024,512]{2,1,0:T(8,128)(2,1)S(1)}, bf16[2,1024,512]{2,1,0:T(8,128)(2,1)S(1)}, bf16[2,1024,512]{2,1,0:T(8,128)(2,1)S(1)}, bf16[2,1024,51...) custom-call(s32[4]{0:T(128)S(1)} %pad_add_fusion.place, ...), custom_call_target="tpu_custom_call" | custom-call | flops 6000000000 | bytes 100000 | tf_op jit(solution)/shard_map/build_here/pallas_call | solution.py:190
  29.6 0.9 weigh_own.1.after
  31.3 5.1 %build_next.1 = (bf16[2,1024,512]{2,1,0:T(8,128)(2,1)S(1)}, bf16[2,1024,512]{2,1,0:T(8,128)(2,1)S(1)}, bf16[2,1024,512]{2,1,0:T(8,128)(2,1)S(1)}, bf16[2,1024,51...) custom-call(s32[4]{0:T(128)S(1)} %pad_add_fusion.place, ...), custom_call_target="tpu_custom_call" | custom-call | flops 100000000 | bytes 100000 | tf_op jit(solution)/shard_map/build_next/pallas_call | solution.py:190
  36.9 1.5 %weigh.1.power = f32[8,200]{1,0:T(8,128)S(1)} custom-call(s32[4]{0:T(128)S(1)} %pad_add_fusion.place, f32[8,4096]{1,0:T(8,128)S(1)} %get-tuple-element.55.ctf, f32[8,200]{1,0:T(8,128)S(1)} %weigh_own.1.after, bf16[8,200,128]{2,1,0:T(8,128)(2,1)S(1)} %collective-permute-done.1.refs_0_.refs_1_, ...), custom_call_target="tpu_custom_call" | custom-call | tf_op jit(solution)/shard_map/weigh/pallas_call | solution.py:48
  38.4 5.2 %score_given.1 = f32[2,1024,256]{2,1,0:T(8,128)S(1)} custom-call(s32[4]{0:T(128)S(1)} %pad_add_fusion.place, f32[8,200]{1,0:T(8,128)S(1)} %weigh.1.power, bf16[40,4224]{1,0:T(8,128)(2,1)S(1)} %collective-permute-done.images_b.meta_a, bf16[40,4224]{1,0:T(8,128)(2,1)S(1)} %collective-permute-done.6.images_b.meta_b, ...), custom_call_target="tpu_custom_call" | custom-call | flops 4294967296 | tf_op jit(solution)/shard_map/score_given/pallas_call | solution.py:48
  43.7 5.2 %score_own.1.mine = f32[2,1024,256]{2,1,0:T(8,128)S(1)} custom-call(s32[4]{0:T(128)S(1)} %pad_add_fusion.place, f32[8,200]{1,0:T(8,128)S(1)} %weigh.1.power, bf16[40,4224]{1,0:T(8,128)(2,1)S(1)} %get-tuple-element.62.images_a.meta_a, bf16[40,4224]{1,0:T(8,128)(2,1)S(1)} %collective-permute-done.4.images_a.meta_b, ...), custom_call_target="tpu_custom_call" | custom-call | flops 4294967296 | tf_op jit(solution)/shard_map/score_own/pallas_call | solution.py:48
  48.9 1.3 %settle.1 = f32[8,8,128]{2,1,0:T(8,128)S(1)} custom-call(s32[4]{0:T(128)S(1)} %pad_add_fusion.place, f32[2,1024,256]{2,1,0:T(8,128)S(1)} %score_own.1.mine, f32[2,1024,256]{2,1,0:T(8,128)S(1)} %collective-permute-done.7.theirs), custom_call_target="tpu_custom_call" | custom-call | tf_op jit(solution)/shard_map/settle/pallas_call | solution.py:48
  50.1 15.4 %all_to_all.10.stats = f32[8,8,128]{2,1,0:T(8,128)S(1)} all-to-all(f32[8,8,128]{2,1,0:T(8,128)S(1)} %settle.1), channel_id=1, replica_groups=mesh['cls'=4,'grp'=4,'y'=4,'zl'=2,'core'=2] {'cls','zl'}, dimensions={0} | all-to-all | bytes 65536 | tf_op jit(solution)/shard_map/all_to_all | solution.py:435
  65.5 1.7 %posterior.1 = (bf16[2,200,1024]{2,1,0:T(8,128)(2,1)S(1)}, f32[8,40]{1,0:T(8,128)S(1)}) custom-call(s32[4]{0:T(128)S(1)} %pad_add_fusion.place, f32[2,1024,256]{2,1,0:T(8,128)S(1)} %score_own.1.mine, f32[2,1024,256]{2,1,0:T(8,128)S(1)} %collective-permute-done.7.theirs, f32[8,8,128]{2,1,0:T(8,128)S(1)} %all_to_all.10.stats, ...), custom_call_target="tpu_custom_call" | custom-call | tf_op jit(solution)/shard_map/posterior/pallas_call | solution.py:315
  67.6 1.6 %insert_begin.1 = (f32[4,200,128]{2,1,0:T(8,128)S(1)}, f32[4,200,128]{2,1,0:T(8,128)S(1)}) custom-call(s32[4]{0:T(128)S(1)} %pad_add_fusion.place, bf16[2,200,1024]{2,1,0:T(8,128)(2,1)S(1)} %get-tuple-element.84.mine, bf16[2,1024,512]{2,1,0:T(8,128)(2,1)S(1)} %get-tuple-element.69.refs_6_.a0.refs_2_, ...), custom_call_target="tpu_custom_call" | custom-call | flops 1073741824 | tf_op jit(solution)/shard_map/insert_begin/pallas_call | solution.py:48
  69.9 1.6 %insert_far.1 = (bf16[4,216,128]{2,1,0:T(8,128)(2,1)S(1)}, bf16[4,216,128]{2,1,0:T(8,128)(2,1)S(1)}, f32[8,128]{1,0:T(8,128)S(1)}) custom-call(s32[4]{0:T(128)S(1)} %pad_add_fusion.place, f32[8,40]{1,0:T(8,128)S(1)} %get-tuple-element.83.after, bf16[2,200,1024]{2,1,0:T(8,128)(2,1)S(1)} %get-tuple-element.84.mine, ...), custom_call_target="tpu_custom_call" | custom-call | flops 1073741824 | tf_op jit(solution)/shard_map/insert_far/pallas_call | solution.py:48
  71.5 1.0 collective-permute-start.10
  72.5 2.6 %collective-permute-start.9 = (bf16[4,216,128]{2,1,0:T(8,128)(2,1)S(1)}, bf16[4,216,128]{2,1,0:T(8,128)(2,1)S(1)}, u32[]{:S(2)}, u32[]{:S(2)}) collective-permute-start(bf16[4,216,128]{2,1,0:T(8,128)(2,1)S(1)} %get-tuple-element.89), channel_id=1, source_target_pairs={{0,32},{16,48},{32,0},{48,16},{1,33},{17,49},{33,1},{49,17},{2,34}... | collective-permute-start | bytes 663560 | tf_op jit(solution)/shard_map/ppermute | solution.py:400
  75.1 4.3 %insert_near.1 = (bf16[4,216,128]{2,1,0:T(8,128)(2,1)S(1)}, bf16[4,216,128]{2,1,0:T(8,128)(2,1)S(1)}, bf16[4,216,128]{2,1,0:T(8,128)(2,1)S(1)}, bf16[4,216,128]{2,1,0:T(8,128)(2,1)S(1)}, f32[8,128]{1,0:T(8,128)S(1)}) custom-call(s32[4]{0:T(128)S(1)} %pad_add_fusion.place, f32[8,128]{1,0:T(8,128)S(1)} %get-tuple-element.87.after, ...), custom_call_target="tpu_custom_call" | custom-call | flops 4294967296 | tf_op jit(solution)/shard_map/insert_near/pallas_call | solution.py:48
  80.2 1.9 %collective-permute-start.14 = (bf16[4,216,128]{2,1,0:T(8,128)(2,1)S(1)}, bf16[4,216,128]{2,1,0:T(8,128)(2,1)S(1)}, u32[]{:S(2)}, u32[]{:S(2)}) collective-permute-start(bf16[4,216,128]{2,1,0:T(8,128)(2,1)S(1)} %get-tuple-element.97), channel_id=1, source_target_pairs={{0,12},{4,8},{8,4},{12,0},{1,13},{5,9},{9,5},{13,1},{2,14},{6,10},... | collective-permute-start | bytes 663560 | tf_op jit(solution)/shard_map/ppermute | solution.py:400
  83.1 1.1 %collective-permute-start.12 = (bf16[4,216,128]{2,1,0:T(8,128)(2,1)S(1)}, bf16[4,216,128]{2,1,0:T(8,128)(2,1)S(1)}, u32[]{:S(2)}, u32[]{:S(2)}) collective-permute-start(bf16[4,216,128]{2,1,0:T(8,128)(2,1)S(1)} %get-tuple-element.93), channel_id=1, source_target_pairs={{0,48},{16,32},{32,16},{48,0},{1,49},{17,33},{33,17},{49,1},{2,50}... | collective-permute-start | bytes 663560 | tf_op jit(solution)/shard_map/ppermute | solution.py:400
  84.2 3.0 %insert_own.1 = (f32[4,216,128]{2,1,0:T(8,128)S(1)}, f32[4,216,128]{2,1,0:T(8,128)S(1)}, f32[8,128]{1,0:T(8,128)}) custom-call(s32[4]{0:T(128)S(1)} %pad_add_fusion.place, f32[8,128]{1,0:T(8,128)S(1)} %get-tuple-element.88.after, bf16[2,200,1024]{2,1,0:T(8,128)(2,1)S(1)} %get-tuple-element.84.mine, bf16[2,200,1024]{2,1,0:T(8,128)(2,1)S(1)} %collective-permute-done.8.theirs, ...), custom_call_target="tpu_custom_call" | custom-call | flops 2147483648 | tf_op jit(solution)/shard_map/insert_own/pallas_call | solution.py:48
  89.3 1.0 collective-permute-done.12.three
  91.4 2.1 %collective-permute-done.16.got_b = bf16[2,216,128]{2,1,0:T(8,128)(2,1)S(1)} collective-permute-done((bf16[2,216,128]{2,1,0:T(8,128)(2,1)S(1)}, bf16[2,216,128]{2,1,0:T(8,128)(2,1)S(1)}, u32[]{:S(2)}, u32[]{:S(2)}) %collective-permute-start.16) | collective-permute-done | bytes 110624 | tf_op jit(solution)/shard_map/ppermute | solution.py:400
  93.5 2.3 %collective-permute-done.15.got_a = bf16[2,216,128]{2,1,0:T(8,128)(2,1)S(1)} collective-permute-done((bf16[2,216,128]{2,1,0:T(8,128)(2,1)S(1)}, bf16[2,216,128]{2,1,0:T(8,128)(2,1)S(1)}, u32[]{:S(2)}, u32[]{:S(2)}) %collective-permute-start.15) | collective-permute-done | bytes 110624 | tf_op jit(solution)/shard_map/ppermute | solution.py:400
  96.4 1.2 %collective-permute-start.17 = (bf16[216,128]{1,0:T(8,128)(2,1)S(1)}, bf16[216,128]{1,0:T(8,128)(2,1)S(1)}, u32[]{:S(2)}, u32[]{:S(2)}) collective-permute-start(bf16[216,128]{1,0:T(8,128)(2,1)S(1)} %get-tuple-element.102), channel_id=1, source_target_pairs={{0,12},{2,50},{4,8},{6,54},{8,4},{10,58},{12,0},{14,62},{16,28},{1... | collective-permute-start | bytes 165896 | tf_op jit(solution)/shard_map/ppermute | solution.py:482
  97.6 3.0 %collective-permute-start.18 = (bf16[216,128]{1,0:T(8,128)(2,1)S(1)}, bf16[216,128]{1,0:T(8,128)(2,1)S(1)}, u32[]{:S(2)}, u32[]{:S(2)}) collective-permute-start(bf16[216,128]{1,0:T(8,128)(2,1)S(1)} %get-tuple-element.103), channel_id=1, source_target_pairs={{0,50},{2,12},{4,54},{6,8},{8,58},{10,4},{12,62},{14,0},{16,34},{1... | collective-permute-start | bytes 165896 | tf_op jit(solution)/shard_map/ppermute | solution.py:483
  101.9 2.0 %collective-permute-done.18.across = bf16[216,128]{1,0:T(8,128)(2,1)S(1)} collective-permute-done((bf16[216,128]{1,0:T(8,128)(2,1)S(1)}, bf16[216,128]{1,0:T(8,128)(2,1)S(1)}, u32[]{:S(2)}, u32[]{:S(2)}) %collective-permute-start.18) | collective-permute-done | bytes 55328 | tf_op jit(solution)/shard_map/ppermute | solution.py:483
  104.8 1.2 %finish.1 = (f32[2,200,128]{2,1,0:T(8,128)}, f32[2,8,200]{2,1,0:T(8,128)}) custom-call(s32[4]{0:T(128)S(1)} %pad_add_fusion.place, f32[216,128]{1,0:T(8,128)S(1)} %get-tuple-element.101.stay, bf16[216,128]{1,0:T(8,128)(2,1)S(1)} %collective-permute-done.17.same, bf16[216,128]{1,0:T(8,128)(2,1)S(1)} %collective-permute-done.18.across, ...), custom_call_target="tpu_custom_call" | custom-call | tf_op jit(solution)/shard_map/finish/pallas_call | solution.py:48
  (33 shorter events, 11.9 us)
Async XLA Ops:
  2.4 13.6 %all-to-all-start = ((bf16[8,200,128]{2,1,0:T(8,128)(2,1)}), bf16[8,200,128]{2,1,0:T(8,128)(2,1)S(1)}, u32[]{:S(2)}, u32[]{:S(2)}) async-start(bf16[8,200,128]{2,1,0:T(8,128)(2,1)} %spread.1), calls=%async_computation | async-start | bytes 819200 | tf_op jit(solution)/shard_map/all_to_all | solution.py:409
  9.0 0.7 copy-start
  11.7 9.6 %collective-permute-start = (bf16[40,4224]{1,0:T(8,128)(2,1)S(1)}, bf16[40,4224]{1,0:T(8,128)(2,1)S(1)}, u32[]{:S(2)}, u32[]{:S(2)}) collective-permute-start(bf16[40,4224]{1,0:T(8,128)(2,1)S(1)} %get-tuple-element.63), channel_id=1, source_target_pairs={{0,1},{1,0},{2,3},{3,2},{4,5},{5,4},{6,7},{7,6},{8,9},{9,8},{10,11... | collective-permute-start | bytes 1013768 | tf_op jit(solution)/shard_map/ppermute | solution.py:413
  16.0 20.4 %collective-permute-start.1 = (bf16[8,200,128]{2,1,0:T(8,128)(2,1)S(1)}, bf16[8,200,128]{2,1,0:T(8,128)(2,1)S(1)}, u32[]{:S(2)}, u32[]{:S(2)}) collective-permute-start(bf16[8,200,128]{2,1,0:T(8,128)(2,1)S(1)} %all-to-all-done.after.refs_0_), channel_id=1, source_target_pairs={{0,16},{16,0},{32,48},{48,32},{1,17},{17,1},{33,49},{49,33},{2,18}... | collective-permute-start | bytes 1228808 | tf_op jit(solution)/shard_map/ppermute | solution.py:400
  17.5 19.4 %collective-permute-start.2 = (bf16[8,200,128]{2,1,0:T(8,128)(2,1)S(1)}, bf16[8,200,128]{2,1,0:T(8,128)(2,1)S(1)}, u32[]{:S(2)}, u32[]{:S(2)}) collective-permute-start(bf16[8,200,128]{2,1,0:T(8,128)(2,1)S(1)} %all-to-all-done.after.refs_0_), channel_id=1, source_target_pairs={{0,48},{16,32},{32,16},{48,0},{1,49},{17,33},{33,17},{49,1},{2,50}... | collective-permute-start | bytes 1228808 | tf_op jit(solution)/shard_map/ppermute | solution.py:400
  19.6 17.3 %collective-permute-start.3 = (bf16[8,200,128]{2,1,0:T(8,128)(2,1)S(1)}, bf16[8,200,128]{2,1,0:T(8,128)(2,1)S(1)}, u32[]{:S(2)}, u32[]{:S(2)}) collective-permute-start(bf16[8,200,128]{2,1,0:T(8,128)(2,1)S(1)} %all-to-all-done.after.refs_0_), channel_id=1, source_target_pairs={{0,32},{16,48},{32,0},{48,16},{1,33},{17,49},{33,1},{49,17},{2,34}... | collective-permute-start | bytes 1228808 | tf_op jit(solution)/shard_map/ppermute | solution.py:400
  20.2 8.9 %collective-permute-start.4 = (bf16[40,4224]{1,0:T(8,128)(2,1)S(1)}, bf16[40,4224]{1,0:T(8,128)(2,1)S(1)}, u32[]{:S(2)}, u32[]{:S(2)}) collective-permute-start(bf16[40,4224]{1,0:T(8,128)(2,1)S(1)} %get-tuple-element.62.images_a.meta_a), channel_id=1, source_target_pairs={{0,2},{2,0},{1,3},{3,1},{4,6},{6,4},{5,7},{7,5},{8,10},{10,8},{9,1... | collective-permute-start | bytes 1013768 | tf_op jit(solution)/shard_map/ppermute | solution.py:416
  21.4 8.3 %collective-permute-start.5 = (bf16[40,4224]{1,0:T(8,128)(2,1)S(1)}, bf16[40,4224]{1,0:T(8,128)(2,1)S(1)}, u32[]{:S(2)}, u32[]{:S(2)}) collective-permute-start(bf16[40,4224]{1,0:T(8,128)(2,1)S(1)} %get-tuple-element.63), channel_id=1, source_target_pairs={{0,194},{2,64},{64,2},{66,128},{128,66},{130,192},{192,130},{194,0... | collective-permute-start | bytes 1013768 | tf_op jit(solution)/shard_map/ppermute | solution.py:417
  29.6 1.6 %collective-permute-start.6 = (bf16[40,4224]{1,0:T(8,128)(2,1)S(1)}, bf16[40,4224]{1,0:T(8,128)(2,1)S(1)}, u32[]{:S(2)}, u32[]{:S(2)}) collective-permute-start(bf16[40,4224]{1,0:T(8,128)(2,1)S(1)} %collective-permute-done.5), channel_id=1, source_target_pairs={{0,1},{1,0},{2,3},{3,2},{4,5},{5,4},{6,7},{7,6},{8,9},{9,8},{10,11... | collective-permute-start | bytes 1013768 | tf_op jit(solution)/shard_map/ppermute | solution.py:423
  43.6 5.3 %collective-permute-start.7 = (f32[2,1024,256]{2,1,0:T(8,128)S(1)}, f32[2,1024,256]{2,1,0:T(8,128)S(1)}, u32[]{:S(2)}, u32[]{:S(2)}) collective-permute-start(f32[2,1024,256]{2,1,0:T(8,128)S(1)} %score_given.1), channel_id=1, source_target_pairs={{0,1},{1,0},{2,3},{3,2},{4,5},{5,4},{6,7},{7,6},{8,9},{9,8},{10,11... | collective-permute-start | bytes 6291464 | tf_op jit(solution)/shard_map/ppermute | solution.py:432
  67.2 2.6 %collective-permute-start.8 = (bf16[2,200,1024]{2,1,0:T(8,128)(2,1)S(1)}, bf16[2,200,1024]{2,1,0:T(8,128)(2,1)S(1)}, u32[]{:S(2)}, u32[]{:S(2)}) collective-permute-start(bf16[2,200,1024]{2,1,0:T(8,128)(2,1)S(1)} %get-tuple-element.84.mine), channel_id=1, source_target_pairs={{0,1},{1,0},{2,3},{3,2},{4,5},{5,4},{6,7},{7,6},{8,9},{9,8},{10,11... | collective-permute-start | bytes 2457608 | tf_op jit(solution)/shard_map/ppermute | solution.py:437
  71.5 11.5 %collective-permute-start.10 = (bf16[4,216,128]{2,1,0:T(8,128)(2,1)S(1)}, bf16[4,216,128]{2,1,0:T(8,128)(2,1)S(1)}, u32[]{:S(2)}, u32[]{:S(2)}) collective-permute-start(bf16[4,216,128]{2,1,0:T(8,128)(2,1)S(1)} %get-tuple-element.90), channel_id=1, source_target_pairs={{0,8},{4,12},{8,0},{12,4},{1,9},{5,13},{9,1},{13,5},{2,10},{6,14},... | collective-permute-start | bytes 663560 | tf_op jit(solution)/shard_map/ppermute | solution.py:400
  72.5 11.7 %collective-permute-start.9 = (bf16[4,216,128]{2,1,0:T(8,128)(2,1)S(1)}, bf16[4,216,128]{2,1,0:T(8,128)(2,1)S(1)}, u32[]{:S(2)}, u32[]{:S(2)}) collective-permute-start(bf16[4,216,128]{2,1,0:T(8,128)(2,1)S(1)} %get-tuple-element.89), channel_id=1, source_target_pairs={{0,32},{16,48},{32,0},{48,16},{1,33},{17,49},{33,1},{49,17},{2,34}... | collective-permute-start | bytes 663560 | tf_op jit(solution)/shard_map/ppermute | solution.py:400
  79.4 7.8 %collective-permute-start.13 = (bf16[4,216,128]{2,1,0:T(8,128)(2,1)S(1)}, bf16[4,216,128]{2,1,0:T(8,128)(2,1)S(1)}, u32[]{:S(2)}, u32[]{:S(2)}) collective-permute-start(bf16[4,216,128]{2,1,0:T(8,128)(2,1)S(1)} %get-tuple-element.96), channel_id=1, source_target_pairs={{0,4},{4,0},{8,12},{12,8},{1,5},{5,1},{9,13},{13,9},{2,6},{6,2},{1... | collective-permute-start | bytes 663560 | tf_op jit(solution)/shard_map/ppermute | solution.py:400
  80.2 7.8 %collective-permute-start.14 = (bf16[4,216,128]{2,1,0:T(8,128)(2,1)S(1)}, bf16[4,216,128]{2,1,0:T(8,128)(2,1)S(1)}, u32[]{:S(2)}, u32[]{:S(2)}) collective-permute-start(bf16[4,216,128]{2,1,0:T(8,128)(2,1)S(1)} %get-tuple-element.97), channel_id=1, source_target_pairs={{0,12},{4,8},{8,4},{12,0},{1,13},{5,9},{9,5},{13,1},{2,14},{6,10},... | collective-permute-start | bytes 663560 | tf_op jit(solution)/shard_map/ppermute | solution.py:400
  82.1 7.1 %collective-permute-start.11 = (bf16[4,216,128]{2,1,0:T(8,128)(2,1)S(1)}, bf16[4,216,128]{2,1,0:T(8,128)(2,1)S(1)}, u32[]{:S(2)}, u32[]{:S(2)}) collective-permute-start(bf16[4,216,128]{2,1,0:T(8,128)(2,1)S(1)} %get-tuple-element.92), channel_id=1, source_target_pairs={{0,16},{16,0},{32,48},{48,32},{1,17},{17,1},{33,49},{49,33},{2,18}... | collective-permute-start | bytes 663560 | tf_op jit(solution)/shard_map/ppermute | solution.py:400
  83.1 7.3 %collective-permute-start.12 = (bf16[4,216,128]{2,1,0:T(8,128)(2,1)S(1)}, bf16[4,216,128]{2,1,0:T(8,128)(2,1)S(1)}, u32[]{:S(2)}, u32[]{:S(2)}) collective-permute-start(bf16[4,216,128]{2,1,0:T(8,128)(2,1)S(1)} %get-tuple-element.93), channel_id=1, source_target_pairs={{0,48},{16,32},{32,16},{48,0},{1,49},{17,33},{33,17},{49,1},{2,50}... | collective-permute-start | bytes 663560 | tf_op jit(solution)/shard_map/ppermute | solution.py:400
  88.6 4.8 %collective-permute-start.16 = (bf16[2,216,128]{2,1,0:T(8,128)(2,1)S(1)}, bf16[2,216,128]{2,1,0:T(8,128)(2,1)S(1)}, u32[]{:S(2)}, u32[]{:S(2)}) collective-permute-start(bf16[2,216,128]{2,1,0:T(8,128)(2,1)S(1)} %get-tuple-element.100), channel_id=1, source_target_pairs={{0,16},{16,0},{32,48},{48,32},{1,17},{17,1},{33,49},{49,33},{2,18}... | collective-permute-start | bytes 331784 | tf_op jit(solution)/shard_map/ppermute | solution.py:400
  91.0 4.8 %collective-permute-start.15 = (bf16[2,216,128]{2,1,0:T(8,128)(2,1)S(1)}, bf16[2,216,128]{2,1,0:T(8,128)(2,1)S(1)}, u32[]{:S(2)}, u32[]{:S(2)}) collective-permute-start(bf16[2,216,128]{2,1,0:T(8,128)(2,1)S(1)} %get-tuple-element.99), channel_id=1, source_target_pairs={{0,4},{4,0},{8,12},{12,8},{1,5},{5,1},{9,13},{13,9},{2,6},{6,2},{1... | collective-permute-start | bytes 331784 | tf_op jit(solution)/shard_map/ppermute | solution.py:400
  96.4 5.5 %collective-permute-start.17 = (bf16[216,128]{1,0:T(8,128)(2,1)S(1)}, bf16[216,128]{1,0:T(8,128)(2,1)S(1)}, u32[]{:S(2)}, u32[]{:S(2)}) collective-permute-start(bf16[216,128]{1,0:T(8,128)(2,1)S(1)} %get-tuple-element.102), channel_id=1, source_target_pairs={{0,12},{2,50},{4,8},{6,54},{8,4},{10,58},{12,0},{14,62},{16,28},{1... | collective-permute-start | bytes 165896 | tf_op jit(solution)/shard_map/ppermute | solution.py:482
  97.6 6.3 %collective-permute-start.18 = (bf16[216,128]{1,0:T(8,128)(2,1)S(1)}, bf16[216,128]{1,0:T(8,128)(2,1)S(1)}, u32[]{:S(2)}, u32[]{:S(2)}) collective-permute-start(bf16[216,128]{1,0:T(8,128)(2,1)S(1)} %get-tuple-element.103), channel_id=1, source_target_pairs={{0,50},{2,12},{4,54},{6,8},{8,58},{10,4},{12,62},{14,0},{16,34},{1... | collective-permute-start | bytes 165896 | tf_op jit(solution)/shard_map/ppermute | solution.py:483
  100.6 4.2 %collective-permute-start.19 = (bf16[216,128]{1,0:T(8,128)(2,1)S(1)}, bf16[216,128]{1,0:T(8,128)(2,1)S(1)}, u32[]{:S(2)}, u32[]{:S(2)}) collective-permute-start(bf16[216,128]{1,0:T(8,128)(2,1)S(1)} %get-tuple-element.104), channel_id=1, source_target_pairs={{0,2},{2,0},{4,6},{6,4},{8,10},{10,8},{12,14},{14,12},{16,18},{18,... | collective-permute-start | bytes 165896 | tf_op jit(solution)/shard_map/ppermute | solution.py:484
